TPU v7x, 32 devices: a whole 2x2x4 slice. The times are simulated.
32 devices in a mesh: lon: 8 (over y, x, core), lat: 4 (over z).
Axes of the slice: x: 2, y: 2, z: 4, core: 2. Of those that a mesh axis runs over, the one named last changes fastest.
Arguments:
- grad_field: float32 [16, 32, 137, 128], P('lat', 'lon'), may hold values from -6 to 6
- lat_weights: float32 [8, 3], replicated, may hold values from 0.2 to 1
- block_offsets: int32 [8, 5], replicated, may hold values from -3 to 3, as said below
- filters: bfloat16 [8, 5, 128, 128], replicated, may hold values from -0.25 to 0.25
- vertical: bfloat16 [8, 137, 137], replicated, may hold values from -0.5 to 0.5
- slot_of_band: int32 [8], replicated, may hold values from 0 to 7, each once
Outputs:
- band_control: bfloat16 [8, 16, 32, 137, 128], P('lat', 'lon')
Inputs may be any that keep to these rules, and one draw needn't show every extreme that they name: `block_offsets`: each band names 5 different offsets; offset -3 is named by some band and offset 3 by some band.
All inputs are finite; a program needn't handle non-finite values.
Results may differ from a plain program's by a relative error of at most 0.0058.
Values may be sent and summed in bfloat16 or wider, within the bound.
No kernel may reach another device: no remote copies, remote signals or barrier semaphores. Data moves between devices by JAX's collectives and lax.ppermute only.
A program may use at most 128 MiB of HBM per device.

v0:
```python
import jax
import jax.numpy as jnp
from jax import lax
from jax.sharding import PartitionSpec as P


def extended(value, sides, width):
    for axis, dim in sides:
        count, length = (lax.axis_size(axis), value.shape[dim])
        up = [(i, (i + 1) % count) for i in range(count - 1)]
        down = [(j, i) for i, j in up]
        last = lax.slice_in_dim(value, length - width, length, axis=dim)
        first = lax.slice_in_dim(value, 0, width, axis=dim)
        before = lax.ppermute(last, axis, up)
        after = lax.ppermute(first, axis, down)
        value = jnp.concatenate([before, value, after], axis=dim)
    return value


def slot_tables(lat_weights, block_offsets, filters, vertical, slot_of_band):
    band_count = slot_of_band.shape[0]
    ordinal = jnp.arange(band_count, dtype=jnp.int32)
    matches = (slot_of_band[None, :] == ordinal[:, None]).astype(jnp.int32)
    band_at_slot = jnp.sum(matches * ordinal[None, :], axis=1)
    return tuple(
        (
            jnp.take(source_table, band_at_slot, axis=0)
            for source_table in (lat_weights, block_offsets, filters, vertical)
        )
    )


def blend_rows(framed, weights):
    row_count = framed.shape[0] - 2
    blended = (
        weights[0] * framed[0:row_count]
        + weights[1] * framed[1 : row_count + 1]
        + weights[2] * framed[2 : row_count + 2]
    )
    return blended.astype(jnp.bfloat16)


def band_output(blended, offsets, filter_set, vertical_b, count_q):
    running = None
    for position in range(filter_set.shape[0]):
        picks = (jnp.arange(count_q, dtype=jnp.int32) + offsets[position]) % count_q
        window = jnp.take(blended, picks, axis=1)
        term = jnp.einsum(
            "rqlc,cd->rqld", window, filter_set[position], preferred_element_type=jnp.float32
        )
        running = term if running is None else running + term
    smoothed = running.astype(jnp.bfloat16)
    result = jnp.einsum("ml,rqlc->rqmc", vertical_b, smoothed, preferred_element_type=jnp.float32)
    return result.astype(jnp.bfloat16)


def owned_slots(tables, band_count):
    group = band_count // lax.axis_size("lat")
    first_slot = lax.axis_index("lat") * group
    return (
        group,
        tuple((lax.dynamic_slice_in_dim(table, first_slot, group, 0) for table in tables)),
    )


def on_device(grad_field, lat_weights, block_offsets, filters, vertical, slot_of_band):
    weights_s, offsets_s, filters_s, vertical_s = slot_tables(
        lat_weights, block_offsets, filters, vertical, slot_of_band
    )
    band_count = slot_of_band.shape[0]
    columns = lax.all_gather(grad_field, "lat", axis=0, tiled=True)
    circles = lax.all_to_all(columns, "lon", split_axis=0, concat_axis=1, tiled=True)
    framed = extended(circles, (("lon", 0),), 1)
    group, owned = owned_slots((weights_s, offsets_s, filters_s, vertical_s), band_count)
    weights_g, offsets_g, filters_g, vertical_g = owned
    count_q = circles.shape[1]
    results = []
    for member in range(group):
        blended = blend_rows(framed, weights_g[member])
        results.append(
            band_output(blended, offsets_g[member], filters_g[member], vertical_g[member], count_q)
        )
    return jnp.stack(results)


def solution(mesh):
    placed = (P("lat", "lon", None, None), P(), P(), P(), P(), P())
    return jax.shard_map(
        on_device,
        mesh=mesh,
        in_specs=placed,
        out_specs=P("lat", "lon", None, None, None),
        check_vma=False,
    )
```

profile of v0, /device:TPU:1, one launch (start us, length us, event | category | flops | bytes accessed | tf_op | source)
XLA Modules:
  0.0 397.8 jit_solution(8821421418451634393)
XLA Ops:
  7.3 89.4 %all-gather.2.cloned.1.call-done = f32[16,4,137,128]{3,1,2,0:T(4,128)} async-done(((f32[4,4,137,128]{3,1,2,0:T(4,128)}), f32[16,4,137,128]{3,1,2,0:T(4,128)}) %all-gather.2.cloned.1.call-update) | async-done | bytes 4489232 | tf_op jit(solution)/shard_map/all_gather | solution.py:71
  96.7 5.1 %all-to-all-start = ((f32[16,4,137,128]{3,1,2,0:T(4,128)}), f32[16,4,137,128]{3,1,2,0:T(4,128)}, u32[]{:S(2)}, u32[]{:S(2)}) async-start(f32[16,4,137,128]{3,1,2,0:T(4,128)} %all-gather.2.cloned.1.call-done), calls=%async_computation | async-start | bytes 8978432 | tf_op jit(solution)/shard_map/all_to_all | solution.py:72
  118.7 31.9 %all-to-all-done = f32[16,4,137,128]{3,1,2,0:T(4,128)} async-done(((f32[16,4,137,128]{3,1,2,0:T(4,128)}), f32[16,4,137,128]{3,1,2,0:T(4,128)}, u32[]{:S(2)}, u32[]{:S(2)}) %all-to-all-start) | async-done | bytes 4489248 | tf_op jit(solution)/shard_map/all_to_all | solution.py:72
  150.6 3.6 copy.121
  157.5 5.7 %collective-permute-start = (f32[1,32,137,128]{3,0,2,1:T(1,128)S(1)}, f32[1,32,137,128]{3,0,2,1:T(1,128)S(1)}, u32[]{:S(2)}, u32[]{:S(2)}) collective-permute-start(f32[1,32,137,128]{3,0,2,1:T(1,128)S(1)} %copy.55), channel_id=1, source_target_pairs={{0,4},{4,8},{8,12},{12,16},{16,20},{20,24},{24,28},{1,5},{5,9},{9,... | collective-permute-start | bytes 6733832 | tf_op jit(solution)/shard_map/ppermute | solution.py:14
  170.1 3.5 copy.56
  173.6 14.1 %collective-permute-done = f32[1,32,137,128]{3,0,2,1:T(1,128)S(1)} collective-permute-done((f32[1,32,137,128]{3,0,2,1:T(1,128)S(1)}, f32[1,32,137,128]{3,0,2,1:T(1,128)S(1)}, u32[]{:S(2)}, u32[]{:S(2)}) %collective-permute-start) | collective-permute-done | bytes 2244640 | tf_op jit(solution)/shard_map/ppermute | solution.py:14
  187.7 25.7 %collective-permute-done.1 = f32[1,32,137,128]{3,0,2,1:T(1,128)S(1)} collective-permute-done((f32[1,32,137,128]{3,0,2,1:T(1,128)S(1)}, f32[1,32,137,128]{3,0,2,1:T(1,128)S(1)}, u32[]{:S(2)}, u32[]{:S(2)}) %collective-permute-start.1) | collective-permute-done | bytes 2244640 | tf_op jit(solution)/shard_map/ppermute | solution.py:15
  213.5 18.6 %add_convert_fusion.3 = (bf16[2,32,137,128]{3,0,2,1:T(2,128)(2,1)}, bf16[2,32,137,128]{3,0,2,1:T(2,128)(2,1)S(1)}) fusion(f32[2,32,137,128]{3,0,2,1:T(2,128)S(1)} %copy.56, f32[]{:T(128)} %bitcast.10, f32[]{:T(128)} %bitcast.8, f32[]{:T(128)} %bitcast.3, f32[1,32,137,128]{3,0,2,1:T(1,128)S(1)} %collective-permute-done, ...), kind=kLoop, calls=%fused_computation.20 | loop fusion | flops 15712256 | bytes 13467672 | tf_op jit(solution)/shard_map/convert_element_type | solution.py:40
  232.1 8.1 %gather_fusion.8 = bf16[32,2,137,128]{3,1,2,0:T(2,128)(2,1)} fusion(bf16[2,32,137,128]{3,0,2,1:T(2,128)(2,1)} %get-tuple-element.6, s32[1024]{0:T(1024)S(1)} %pad_clamp_fusion.5), kind=kCustom, calls=%fused_computation.4.clone | custom fusion | bytes 4489344 | tf_op jit(solution)/shard_map/jit(_take)/gather | solution.py:47
  240.2 8.3 %gather_fusion.7 = bf16[32,2,137,128]{3,1,2,0:T(2,128)(2,1)} fusion(bf16[2,32,137,128]{3,0,2,1:T(2,128)(2,1)} %get-tuple-element.6, s32[1024]{0:T(1024)S(1)} %pad_clamp_fusion.6), kind=kCustom, calls=%fused_computation.3.clone | custom fusion | bytes 4489344 | tf_op jit(solution)/shard_map/jit(_take)/gather | solution.py:47
  248.5 3.7 fusion.34
  260.1 8.1 %gather_fusion.6 = bf16[32,2,137,128]{3,1,2,0:T(2,128)(2,1)} fusion(bf16[2,32,137,128]{3,0,2,1:T(2,128)(2,1)} %get-tuple-element.6, s32[1024]{0:T(1024)S(1)} %pad_clamp_fusion.7), kind=kCustom, calls=%fused_computation.2.clone | custom fusion | bytes 4489344 | tf_op jit(solution)/shard_map/jit(_take)/gather | solution.py:47
  268.2 3.7 fusion.32
  271.9 3.0 fusion.16
  274.9 8.5 %gather_fusion.5 = bf16[32,2,137,128]{3,1,2,0:T(2,128)(2,1)} fusion(bf16[2,32,137,128]{3,0,2,1:T(2,128)(2,1)} %get-tuple-element.6, s32[1024]{0:T(1024)S(1)} %pad_clamp_fusion.8), kind=kCustom, calls=%fused_computation.1.clone | custom fusion | bytes 4489344 | tf_op jit(solution)/shard_map/jit(_take)/gather | solution.py:47
  283.4 3.7 fusion.31
  287.1 3.0 fusion.18
  290.1 8.1 %gather_fusion.4 = bf16[32,2,137,128]{3,1,2,0:T(2,128)(2,1)} fusion(bf16[2,32,137,128]{3,0,2,1:T(2,128)(2,1)} %get-tuple-element.6, s32[1024]{0:T(1024)S(1)} %pad_clamp_fusion.9), kind=kCustom, calls=%fused_computation.clone | custom fusion | bytes 4489344 | tf_op jit(solution)/shard_map/jit(_take)/gather | solution.py:47
  298.2 6.6 %gather_fusion.12 = bf16[32,2,137,128]{3,1,2,0:T(2,128)(2,1)} fusion(bf16[2,32,137,128]{3,0,2,1:T(2,128)(2,1)S(1)} %get-tuple-element.7, s32[1024]{0:T(1024)S(1)} %pad_clamp_fusion.1), kind=kCustom, calls=%fused_computation.8.clone | custom fusion | bytes 4489344 | tf_op jit(solution)/shard_map/jit(_take)/gather | solution.py:47
  304.9 3.7 fusion.38
  311.5 6.5 %gather_fusion.11 = bf16[32,2,137,128]{3,1,2,0:T(2,128)(2,1)} fusion(bf16[2,32,137,128]{3,0,2,1:T(2,128)(2,1)S(1)} %get-tuple-element.7, s32[1024]{0:T(1024)S(1)} %pad_clamp_fusion.2), kind=kCustom, calls=%fused_computation.7.clone | custom fusion | bytes 4489344 | tf_op jit(solution)/shard_map/jit(_take)/gather | solution.py:47
  318.0 3.7 fusion.37
  324.7 6.7 %gather_fusion.10 = bf16[32,2,137,128]{3,1,2,0:T(2,128)(2,1)} fusion(bf16[2,32,137,128]{3,0,2,1:T(2,128)(2,1)S(1)} %get-tuple-element.7, s32[1024]{0:T(1024)S(1)} %pad_clamp_fusion.3), kind=kCustom, calls=%fused_computation.6.clone | custom fusion | bytes 4489344 | tf_op jit(solution)/shard_map/jit(_take)/gather | solution.py:47
  331.3 3.7 fusion.36
  337.9 6.5 %gather_fusion.13 = bf16[32,2,137,128]{3,1,2,0:T(2,128)(2,1)} fusion(bf16[2,32,137,128]{3,0,2,1:T(2,128)(2,1)S(1)} %get-tuple-element.7, s32[1024]{0:T(1024)S(1)} %pad_clamp_fusion), kind=kCustom, calls=%fused_computation.9.clone | custom fusion | bytes 4489344 | tf_op jit(solution)/shard_map/jit(_take)/gather | solution.py:47
  344.4 3.7 fusion.39
  350.9 6.7 %gather_fusion.9 = bf16[32,2,137,128]{3,1,2,0:T(2,128)(2,1)} fusion(bf16[2,32,137,128]{3,0,2,1:T(2,128)(2,1)S(1)} %get-tuple-element.7, s32[1024]{0:T(1024)S(1)} %pad_clamp_fusion.4), kind=kCustom, calls=%fused_computation.5.clone | custom fusion | bytes 4489344 | tf_op jit(solution)/shard_map/jit(_take)/gather | solution.py:47
  357.7 5.2 %fusion.30 = bf16[2,32,137,128]{3,0,2,1:T(2,128)(2,1)} fusion(bf16[32,2,137,128]{3,1,2,0:T(2,128)(2,1)} %gather_fusion.4, pred[32]{0:T(512)(128)(4,1)S(1)} %get-tuple-element.47), kind=kLoop, calls=%fused_computation.55 | loop fusion | flops 1122304 | bytes 4489248 | tf_op jit(solution)/shard_map/jit(_take)/select_n | solution.py:47
  364.9 10.0 %convert_bitcast_fusion.1 = bf16[1,2,32,137,128]{4,3,2,1,0:T(8,128)(2,1)} fusion(f32[2,32,137,128]{3,2,1,0:T(8,128)} %fusion.12, f32[2,32,137,128]{3,2,1,0:T(8,128)} %fusion.14, f32[2,32,137,128]{3,2,1,0:T(8,128)} %fusion.16, f32[2,32,137,128]{3,2,1,0:T(8,128)} %fusion.18, bf16[2,32,137,128]{3,0,2,1:T(2,128)(2,1)} %fusion.30, ...), kind=kOutput, calls=%fused_computation.54 | convolution fusion | flops 601554944 | bytes 22552576 | tf_op jit(solution)/shard_map/ml,rqlc->rqmc/dot_general | solution.py:53
  374.9 9.4 %convert_bitcast_fusion = bf16[1,2,32,137,128]{4,3,2,1,0:T(8,128)(2,1)} fusion(f32[2,32,137,128]{3,2,1,0:T(8,128)} %fusion.2, f32[2,32,137,128]{3,2,1,0:T(8,128)} %fusion.4, f32[2,32,137,128]{3,2,1,0:T(8,128)} %fusion.6, f32[2,32,137,128]{3,2,1,0:T(8,128)} %fusion.8, bf16[2,32,137,128]{3,0,2,1:T(2,128)(2,1)S(1)} %fusion.35, ...), kind=kOutput, calls=%fused_computation.53 | convolution fusion | flops 601554944 | bytes 22552576 | tf_op jit(solution)/shard_map/ml,rqlc->rqmc/dot_general | solution.py:53
  387.2 3.3 copy.72
  (70 shorter events, 52.2 us)
Async XLA Ops:
  6.5 96.6 %copy-start = (bf16[8,5,128,128]{3,2,1,0:T(8,128)(2,1)S(1)}, bf16[8,5,128,128]{3,2,1,0:T(8,128)(2,1)}, u32[]{:S(2)}) copy-start(bf16[8,5,128,128]{3,2,1,0:T(8,128)(2,1)} %param.11) | copy-start | bytes 3932164
  6.5 90.2 %all-gather.2.cloned.1.call-start = ((), (), s32[]{:S(2)}) async-start(), calls=%async_computation.1 | async-start | bytes 5611520 | tf_op jit(solution)/shard_map/all_gather | solution.py:71
  7.3 94.6 %copy-start.6 = (f32[8,3]{0,1:T(4,128)S(1)}, f32[8,3]{0,1:T(4,128)}, u32[]{:S(2)}) copy-start(f32[8,3]{0,1:T(4,128)} %param.9) | copy-start | bytes 292
  7.3 94.6 %copy-start.7 = (s32[8]{0:T(128)S(1)}, s32[8]{0:T(128)}, u32[]{:S(2)}) copy-start(s32[8]{0:T(128)} %param.13) | copy-start | bytes 100
  7.3 95.3 %copy-start.5 = (s32[8,5]{1,0:T(8,128)S(1)}, s32[8,5]{1,0:T(8,128)}, u32[]{:S(2)}) copy-start(s32[8,5]{1,0:T(8,128)} %param.10) | copy-start | bytes 484
  96.7 53.9 %all-to-all-start = ((f32[16,4,137,128]{3,1,2,0:T(4,128)}), f32[16,4,137,128]{3,1,2,0:T(4,128)}, u32[]{:S(2)}, u32[]{:S(2)}) async-start(f32[16,4,137,128]{3,1,2,0:T(4,128)} %all-gather.2.cloned.1.call-done), calls=%async_computation | async-start | bytes 8978432 | tf_op jit(solution)/shard_map/all_to_all | solution.py:72
  101.8 2.2 copy-start.2
  157.5 30.2 %collective-permute-start = (f32[1,32,137,128]{3,0,2,1:T(1,128)S(1)}, f32[1,32,137,128]{3,0,2,1:T(1,128)S(1)}, u32[]{:S(2)}, u32[]{:S(2)}) collective-permute-start(f32[1,32,137,128]{3,0,2,1:T(1,128)S(1)} %copy.55), channel_id=1, source_target_pairs={{0,4},{4,8},{8,12},{12,16},{16,20},{20,24},{24,28},{1,5},{5,9},{9,... | collective-permute-start | bytes 6733832 | tf_op jit(solution)/shard_map/ppermute | solution.py:14
  165.5 47.9 %collective-permute-start.1 = (f32[1,32,137,128]{3,0,2,1:T(1,128)S(1)}, f32[1,32,137,128]{3,0,2,1:T(1,128)S(1)}, u32[]{:S(2)}, u32[]{:S(2)}) collective-permute-start(f32[1,32,137,128]{3,0,2,1:T(1,128)S(1)} %copy.58), channel_id=1, source_target_pairs={{4,0},{8,4},{12,8},{16,12},{20,16},{24,20},{28,24},{5,1},{9,5},{13... | collective-permute-start | bytes 6733832 | tf_op jit(solution)/shard_map/ppermute | solution.py:15
  252.2 2.9 copy-start.4
  357.7 5.2 %copy-start.3 = (bf16[32,2,137,128]{3,1,2,0:T(2,128)(2,1)S(1)}, bf16[32,2,137,128]{3,1,2,0:T(2,128)(2,1)}, u32[]{:S(2)}) copy-start(bf16[32,2,137,128]{3,1,2,0:T(2,128)(2,1)} %gather_fusion.9) | copy-start | bytes 6733828
  384.3 6.2 %copy-start.1 = (bf16[8,5,128,128]{3,2,1,0:T(8,128)(2,1)S(1)}, bf16[8,5,128,128]{3,2,1,0:T(8,128)(2,1)}, u32[]{:S(2)}) copy-start(bf16[8,5,128,128]{3,2,1,0:T(8,128)(2,1)} %param.11) | copy-start | bytes 3932164
Sparse Core Ops, SparseCore 0:
  8.9 87.7 all-gather.1
where the time goes:
time: 406 us; the launch traced here: 398 us
  waiting for transfers between devices  162 us (40%)
  local copies, waits for them, and re-layouts  96 us (24%)
  other arithmetic  70 us (17%)
  matrix products  42.9 us (11%)
  between operations  14.2 us (3%)
  starting transfers between devices  12.8 us (3%)
    all_gather x1, waiting for transfers between devices, on_device(): columns = lax.all_gather(grad_field, 'lat', axis=0, tiled=True)  89.4 us
    gather x10, local copies, waits for them, and re-layouts, band_output(): window = jnp.take(blended, picks, axis=1)  74.2 us
    select_n x15, other arithmetic, band_output(): window = jnp.take(blended, picks, axis=1)  41.5 us
    all_to_all x1, waiting for transfers between devices, on_device(): lax.all_to_all(columns, 'lon', split_axis=0, concat_axis=1, tiled=True)  31.9 us
    ppermute x1, waiting for transfers between devices, extended(): after = lax.ppermute(first, axis, down)  25.7 us
    dot_general x8, matrix products, band_output(): jnp.einsum('rqlc,cd->rqld', window, filter_set[position], preferred_eleme...  23.5 us
    dot_general x2, matrix products, band_output(): jnp.einsum('ml,rqlc->rqmc', vertical_b, smoothed, preferred_element_type=...  19.4 us
    convert_element_type x1, other arithmetic, blend_rows(): return blended.astype(jnp.bfloat16)  18.6 us
  transfers between devices with their start and end apart: 4, of which 4 were waited for; matrix products, arithmetic and copies ran while one was open for 6% of the time, Pallas kernels for 0%

commit v1 on v0

v1 whole, which is shorter than its diff:
```python
import functools

import jax
import jax.numpy as jnp
from jax import lax
from jax.experimental import pallas as pl
from jax.experimental.pallas import tpu as pltpu
from jax.sharding import PartitionSpec as P

REACH = 3


def round_up(value, step):
    return (value + step - 1) // step * step


def owned_tables(lat_weights, block_offsets, filters, vertical, slot_of_band):
    band_count = slot_of_band.shape[0]
    group = band_count // lax.axis_size("lat")
    slots = lax.axis_index("lat") * group + jnp.arange(group, dtype=jnp.int32)
    bands = jnp.argmax(slot_of_band[None, :] == slots[:, None], axis=1)
    return tuple(jnp.take(t, bands, axis=0) for t in (lat_weights, block_offsets, filters, vertical))


def paired_filters(offsets, filters):
    group, _, c, d = filters.shape
    width = 2 * REACH + 1
    named = (offsets[:, None, :] + REACH == jnp.arange(width)[None, :, None])[..., None, None]
    dense = jnp.sum(jnp.where(named, filters[:, None], 0), axis=2, dtype=filters.dtype)
    left = jnp.pad(dense, ((0, 0), (0, 1), (0, 0), (0, 0)))
    right = jnp.pad(dense, ((0, 0), (1, 0), (0, 0), (0, 0)))
    both = jnp.concatenate([left, right], axis=3)
    return both.reshape(group, (width + 1) // 2, 2 * c, 2 * d)


def row_coefficients(weights, rows, row_total):
    place = lax.axis_index("lon")
    even = (place % 2 == 0).astype(jnp.float32)
    above = jnp.where(place > 0, 1.0, 0.0)
    below = jnp.where((place + 1) * rows < row_total, 1.0, 0.0)
    w0, w1, w2 = weights[:, 0], weights[:, 1], weights[:, 2]
    zero = jnp.zeros_like(w0)
    first = jnp.stack([w0 * even * above, w0 * (1 - even) * above, w1, w2], axis=1)
    second = jnp.stack([w2 * (1 - even) * below, w2 * even * below, w0, w1], axis=1)
    del zero
    return jnp.stack([first, second], axis=1)


def band_kernel(levels, coef_ref, main_ref, outer_ref, inner_ref, filt_ref, vert_ref, out_ref, window, spread):
    r, b = pl.program_id(0), pl.program_id(1)
    sources, _, per_source, padded, c = main_ref.shape
    blocks = sources * per_source
    half = blocks // 2
    taps = filt_ref.shape[1]
    k_outer, k_inner = coef_ref[b, r, 0], coef_ref[b, r, 1]
    k_first, k_second = coef_ref[b, r, 2], coef_ref[b, r, 3]

    def blend(e, _):
        parts = []
        for i in range(2):
            q = lax.rem(2 * e - REACH + i + blocks, blocks)
            s, n = q // per_source, lax.rem(q, per_source)
            value = (
                k_outer * outer_ref[s, 0, n].astype(jnp.float32)
                + k_inner * inner_ref[s, 0, n].astype(jnp.float32)
                + k_first * main_ref[s, 0, n].astype(jnp.float32)
                + k_second * main_ref[s, 1, n].astype(jnp.float32)
            )
            parts.append(value.astype(jnp.bfloat16))
        window[e] = jnp.concatenate(parts, axis=-1)
        return 0

    lax.fori_loop(0, half, blend, 0)
    for e in range(taps - 1):
        window[half + e] = window[e]

    step = 2
    vert = vert_ref[0]

    def apply(j, _):
        total = None
        for t in range(taps):
            lhs = window[pl.ds(j * step + t, step)].reshape(step * padded, 2 * c)
            term = jnp.dot(lhs, filt_ref[0, t], preferred_element_type=jnp.float32)
            total = term if total is None else total + term
        smoothed = total.astype(jnp.bfloat16)
        for i in range(step):
            mixed = jnp.dot(vert, smoothed[i * padded : (i + 1) * padded], preferred_element_type=jnp.float32)
            q = 2 * (j * step + i)
            for h in range(2):
                spread[pl.ds(q + h, padded, stride=blocks), :] = mixed[:, h * c : (h + 1) * c]
        return 0

    lax.fori_loop(0, half // step, apply, 0)
    out_ref[0, 0] = spread[: levels * blocks].reshape(levels, blocks, c).astype(jnp.bfloat16)


def band_outputs(coef, main, outer, inner, filt, vert, levels):
    sources, rows, per_source, padded, c = main.shape
    group, taps = filt.shape[:2]
    blocks = sources * per_source
    whole = lambda a: pl.BlockSpec(a.shape, lambda r, b: (0,) * a.ndim)
    flops = 2 * group * rows * blocks * padded * (taps * 2 * c * c * 2 // 2 + padded * c)
    return pl.pallas_call(
        functools.partial(band_kernel, levels),
        grid=(rows, group),
        in_specs=[
            pl.BlockSpec(memory_space=pltpu.SMEM),
            whole(main),
            whole(outer),
            whole(inner),
            pl.BlockSpec((1,) + filt.shape[1:], lambda r, b: (b, 0, 0, 0)),
            pl.BlockSpec((1,) + vert.shape[1:], lambda r, b: (b, 0, 0)),
        ],
        out_specs=pl.BlockSpec((1, 1, levels, blocks, c), lambda r, b: (b, r, 0, 0, 0)),
        out_shape=jax.ShapeDtypeStruct((group, rows, levels, blocks, c), jnp.bfloat16),
        scratch_shapes=[
            pltpu.VMEM((blocks // 2 + taps - 1, padded, 2 * c), jnp.bfloat16),
            pltpu.VMEM((padded * blocks, c), jnp.float32),
        ],
        compiler_params=pltpu.CompilerParams(vmem_limit_bytes=56 * 1024 * 1024),
        cost_estimate=pl.CostEstimate(flops=flops, bytes_accessed=10_000_000, transcendentals=0),
    )(coef, main, outer, inner, filt, vert)


def on_device(grad_field, lat_weights, block_offsets, filters, vertical, slot_of_band):
    levels = grad_field.shape[2]
    padded = round_up(levels, 16)
    sources = lax.axis_size("lon")
    weights, offsets, filters_g, vertical_g = owned_tables(
        lat_weights, block_offsets, filters, vertical, slot_of_band
    )
    filt = paired_filters(offsets, filters_g)
    extra = padded - levels
    vert = jnp.pad(vertical_g, ((0, 0), (0, extra), (0, extra)))

    own = jnp.pad(grad_field.astype(jnp.bfloat16), ((0, 0), (0, 0), (0, extra), (0, 0)))
    columns = lax.all_gather(own, "lat", axis=0, tiled=True)
    row_total = columns.shape[0]
    rows = row_total // sources
    coef = row_coefficients(weights, rows, row_total)
    by_place = columns.reshape((sources, rows) + columns.shape[1:])
    outer_rows = [max(p * rows - 1, 0) if p % 2 == 0 else min((p + 1) * rows, row_total - 1) for p in range(sources)]
    outer_send = jnp.stack([columns[i : i + 1] for i in outer_rows])
    main = lax.all_to_all(by_place, "lon", split_axis=0, concat_axis=0)
    outer = lax.all_to_all(outer_send, "lon", split_axis=0, concat_axis=0)
    even = lax.axis_index("lon") % 2 == 0
    give = jnp.where(even, main[:, 1:2], main[:, 0:1])
    inner = lax.ppermute(give, "lon", [(i, i ^ 1) for i in range(sources)])
    result = band_outputs(coef, main, outer, inner, filt, vert, levels)
    return result.transpose(0, 1, 3, 2, 4)


def solution(mesh):
    placed = (P("lat", "lon", None, None), P(), P(), P(), P(), P())
    return jax.shard_map(
        on_device,
        mesh=mesh,
        in_specs=placed,
        out_specs=P("lat", "lon", None, None, None),
        check_vma=False,
    )
```

time: 406 us -> 159 us (0.39)
  the two profiles are of different devices: /device:TPU:1 before, /device:TPU:0 now
where the time goes in v1:
time: 159 us; the launch traced here: 158 us
  waiting for transfers between devices  80.7 us (51%)
  Pallas kernels  29.6 us (19%)
  local copies, waits for them, and re-layouts  18.8 us (12%)
  between operations  13.6 us (9%)
  starting transfers between devices  7.94 us (5%)
  other arithmetic  7.84 us (5%)
    all_gather x1, waiting for transfers between devices, on_device(): columns = lax.all_gather(own, 'lat', axis=0, tiled=True)  48.1 us
    pallas_call x1, Pallas kernels, band_outputs(): pl.pallas_call(functools.partial(band_kernel, levels), grid=(rows, group)...  29.6 us
    all_to_all x1, waiting for transfers between devices, on_device(): main = lax.all_to_all(by_place, 'lon', split_axis=0, concat_axis=0)  17.6 us
    all_to_all x1, waiting for transfers between devices, on_device(): outer = lax.all_to_all(outer_send, 'lon', split_axis=0, concat_axis=0)  14.9 us
    unnamed x21, local copies, waits for them, and re-layouts  12.3 us
    all_to_all x1, starting transfers between devices, on_device(): main = lax.all_to_all(by_place, 'lon', split_axis=0, concat_axis=0)  4.37 us
    all_to_all x1, starting transfers between devices, on_device(): outer = lax.all_to_all(outer_send, 'lon', split_axis=0, concat_axis=0)  3.56 us
    gather x4, local copies, waits for them, and re-layouts, owned_tables(): jnp.take(t, bands, axis=0)  3.35 us
  transfers between devices with their start and end apart: 4, of which 3 were waited for; matrix products, arithmetic and copies ran while one was open for 13% of the time, Pallas kernels for 0%

profile of v1, /device:TPU:0, one launch (start us, length us, event | category | flops | bytes accessed | tf_op | source)
XLA Modules:
  0.0 158.5 jit_solution(7952253969354421290)
XLA Ops:
  6.5 1.5 convert_element_type.17
  8.1 0.1 copy.31
  8.2 0.9 pad.16.clone
  9.2 0.1 copy.26
  9.2 0.7 compare_reduce_fusion
  10.0 0.6 gather_fusion.1
  10.6 0.6 gather_fusion
  11.1 1.6 %gather_fusion.3 = bf16[2,137,137]{2,0,1:T(2,128)(2,1)S(1)} fusion(bf16[8,137,137]{2,0,1:T(8,128)(2,1)S(1)} %copy-done.1, s32[1024]{0:T(1024)S(1)} %pad_clamp_fusion), kind=kCustom, calls=%fused_computation.3 | custom fusion | bytes 150160 | tf_op jit(solution)/shard_map/jit(_take)/gather | solution.py:22
  12.8 0.1 copy_select_fusion
  12.9 0.7 pad.19.vert_ref
  13.5 0.6 gather_fusion.2
  14.3 48.1 %all-gather.2.cloned.1.call-done = bf16[16,4,144,128]{3,2,1,0:T(8,128)(2,1)} async-done(((bf16[4,4,144,128]{3,2,1,0:T(8,128)(2,1)}), bf16[16,4,144,128]{3,2,1,0:T(8,128)(2,1)}) %all-gather.2.cloned.1.call-update) | async-done | bytes 2359312 | tf_op jit(solution)/shard_map/all_gather | solution.py:138
  62.5 4.4 %all-to-all-start = ((bf16[8,2,4,144,128]{4,3,2,1,0:T(8,128)(2,1)}), bf16[8,2,4,144,128]{4,3,2,1,0:T(8,128)(2,1)}, u32[]{:S(2)}, u32[]{:S(2)}) async-start(bf16[8,2,4,144,128]{4,3,2,1,0:T(8,128)(2,1)} %bitcast.41), calls=%async_computation | async-start | bytes 4718592 | tf_op jit(solution)/shard_map/all_to_all | solution.py:145
  66.9 0.1 pad_maximum_fusion.1
  67.0 0.6 pad_maximum_fusion.coef_ref
  67.6 1.6 fusion.10
  69.2 1.6 fusion.9
  70.7 1.6 fusion.8
  72.3 1.6 fusion.7
  73.9 1.6 fusion.6
  75.5 1.6 fusion.5
  77.1 1.6 fusion.4
  78.6 17.6 %all-to-all-done.main_ref = bf16[8,2,4,144,128]{4,3,2,1,0:T(8,128)(2,1)} async-done(((bf16[8,2,4,144,128]{4,3,2,1,0:T(8,128)(2,1)}), bf16[8,2,4,144,128]{4,3,2,1,0:T(8,128)(2,1)}, u32[]{:S(2)}, u32[]{:S(2)}) %all-to-all-start) | async-done | bytes 2359328 | tf_op jit(solution)/shard_map/all_to_all | solution.py:145
  96.3 2.8 %slice_select_fusion = bf16[8,1,4,144,128]{4,3,2,1,0:T(8,128)(2,1)} fusion(bf16[8,2,4,144,128]{4,3,2,1,0:T(8,128)(2,1)} %all-to-all-done.main_ref, pred[]{:T(512)S(6)} %eq.42), kind=kLoop, calls=%fused_computation.9 | loop fusion | flops 589824 | bytes 3538945 | tf_op jit(solution)/shard_map/jit(_where)/select_n | solution.py:148
  99.1 1.6 fusion.3
  100.7 3.6 %all-to-all-start.1 = ((bf16[8,1,4,144,128]{4,3,2,1,0:T(8,128)(2,1)}), bf16[8,1,4,144,128]{4,3,2,1,0:T(8,128)(2,1)S(1)}, u32[]{:S(2)}, u32[]{:S(2)}) async-start(bf16[8,1,4,144,128]{4,3,2,1,0:T(8,128)(2,1)} %fusion.3), calls=%async_computation.1 | async-start | bytes 2359296 | tf_op jit(solution)/shard_map/all_to_all | solution.py:146
  104.3 0.1 broadcast_select_fusion
  104.4 0.6 select_reduce_fusion
  105.0 1.1 fusion.2
  106.1 14.9 %all-to-all-done.1.outer_ref = bf16[8,1,4,144,128]{4,3,2,1,0:T(8,128)(2,1)S(1)} async-done(((bf16[8,1,4,144,128]{4,3,2,1,0:T(8,128)(2,1)}), bf16[8,1,4,144,128]{4,3,2,1,0:T(8,128)(2,1)S(1)}, u32[]{:S(2)}, u32[]{:S(2)}) %all-to-all-start.1) | async-done | bytes 1179680 | tf_op jit(solution)/shard_map/all_to_all | solution.py:146
  121.0 1.0 copy-done.2
  122.0 29.6 %shard_map.64 = bf16[2,2,137,32,128]{4,3,2,1,0:T(8,128)(2,1)} custom-call(f32[2,2,4]{2,1,0:T(2,128)} %pad_maximum_fusion.coef_ref, bf16[8,2,4,144,128]{4,3,2,1,0:T(8,128)(2,1)} %all-to-all-done.main_ref, bf16[8,1,4,144,128]{4,3,2,1,0:T(8,128)(2,1)} %copy-done.2, bf16[8,1,4,144,128]{4,3,2,1,0:T(8,128)(2,1)} %collective-permute-done.inner_ref, ...), custom_call_target="tpu_custom_call" | custom-call | flops 5511315456 | bytes 10000000 | tf_op jit(solution)/shard_map/pallas_call | solution.py:104
  (24 shorter events, 0.4 us)
Async XLA Ops:
  6.5 7.0 %copy-start = (bf16[8,5,128,128]{3,2,1,0:T(8,128)(2,1)S(1)}, bf16[8,5,128,128]{3,2,1,0:T(8,128)(2,1)}, u32[]{:S(2)}) copy-start(bf16[8,5,128,128]{3,2,1,0:T(8,128)(2,1)} %param.9) | copy-start | bytes 3932164
  6.5 55.9 %all-gather.2.cloned.1.call-start = ((), (), s32[]{:S(2)}) async-start(), calls=%async_computation.2 | async-start | bytes 2949120 | tf_op jit(solution)/shard_map/all_gather | solution.py:138
  8.2 1.0 copy-start.4
  8.2 1.1 copy-start.5
  8.2 1.8 %copy-start.3 = (s32[8,5]{1,0:T(8,128)S(1)}, s32[8,5]{1,0:T(8,128)}, u32[]{:S(2)}) copy-start(s32[8,5]{1,0:T(8,128)} %param.8) | copy-start | bytes 484
  8.2 2.9 %copy-start.1 = (bf16[8,137,137]{2,0,1:T(8,128)(2,1)S(1)}, bf16[8,137,137]{2,0,1:T(8,128)(2,1)}, u32[]{:S(2)}) copy-start(bf16[8,137,137]{2,0,1:T(8,128)(2,1)} %param.10) | copy-start | bytes 900916
  62.5 33.8 %all-to-all-start = ((bf16[8,2,4,144,128]{4,3,2,1,0:T(8,128)(2,1)}), bf16[8,2,4,144,128]{4,3,2,1,0:T(8,128)(2,1)}, u32[]{:S(2)}, u32[]{:S(2)}) async-start(bf16[8,2,4,144,128]{4,3,2,1,0:T(8,128)(2,1)} %bitcast.41), calls=%async_computation | async-start | bytes 4718592 | tf_op jit(solution)/shard_map/all_to_all | solution.py:145
  99.1 21.9 %collective-permute-start = (bf16[8,1,4,144,128]{4,3,2,1,0:T(8,128)(2,1)}, bf16[8,1,4,144,128]{4,3,2,1,0:T(8,128)(2,1)}, u32[]{:S(2)}, u32[]{:S(2)}) collective-permute-start(bf16[8,1,4,144,128]{4,3,2,1,0:T(8,128)(2,1)} %slice_select_fusion), channel_id=1, source_target_pairs={{0,4},{4,0},{8,12},{12,8},{16,20},{20,16},{24,28},{28,24},{1,5},{5... | collective-permute-start | bytes 3538952 | tf_op jit(solution)/shard_map/ppermute | solution.py:149
  100.7 20.3 %all-to-all-start.1 = ((bf16[8,1,4,144,128]{4,3,2,1,0:T(8,128)(2,1)}), bf16[8,1,4,144,128]{4,3,2,1,0:T(8,128)(2,1)S(1)}, u32[]{:S(2)}, u32[]{:S(2)}) async-start(bf16[8,1,4,144,128]{4,3,2,1,0:T(8,128)(2,1)} %fusion.3), calls=%async_computation.1 | async-start | bytes 2359296 | tf_op jit(solution)/shard_map/all_to_all | solution.py:146
  121.0 1.0 copy-start.2
Sparse Core Ops, SparseCore 0:
  9.2 53.1 all-gather.1

commit v2 on v0

v2 whole, which is shorter than its diff:
```python
import functools

import jax
import jax.numpy as jnp
from jax import lax
from jax.experimental import pallas as pl
from jax.experimental.pallas import tpu as pltpu
from jax.sharding import PartitionSpec as P

REACH = 3
SUBLANES = 16
SPREAD_GAP = 8
CUTS = (48, 96)


SCALAR = pl.BlockSpec(memory_space=pltpu.SMEM)
PARAMS = pltpu.CompilerParams(vmem_limit_bytes=20 * 1024 * 1024)


def round_up(value, step):
    return (value + step - 1) // step * step


def band_of(slot_ref, slot):
    band = 0
    for i in range(slot_ref.shape[0]):
        band = jnp.where(slot_ref[i] == slot, i, band)
    return band


def table_kernel(where_ref, slot_ref, offset_ref, filter_ref, vertical_ref, filt_out, vert_out):
    group, _, c, _ = filt_out.shape
    levels = vertical_ref.shape[1]
    filt_out[...] = jnp.zeros_like(filt_out)
    vert_out[...] = jnp.zeros_like(vert_out)
    for g in range(group):
        band = band_of(slot_ref, where_ref[1] * group + g)
        for k in range(filter_ref.shape[1]):
            n = offset_ref[band, k] + REACH
            for h in range(2):
                filt_out[g, n + h, :, h * c : (h + 1) * c] = filter_ref[band, k]
        vert_out[g, :levels, :levels] = vertical_ref[band]


def owned_tables(where, slot_of_band, block_offsets, filters, vertical, group, padded):
    c = filters.shape[-1]
    vmem = pl.BlockSpec(memory_space=pltpu.VMEM)
    filt, vert = pl.pallas_call(
        table_kernel,
        in_specs=[SCALAR] * 3 + [vmem] * 2,
        out_specs=[vmem] * 2,
        out_shape=[
            jax.ShapeDtypeStruct((group, 2 * REACH + 2, c, 2 * c), filters.dtype),
            jax.ShapeDtypeStruct((group, padded, padded), vertical.dtype),
        ],
        compiler_params=PARAMS,
        cost_estimate=pl.CostEstimate(flops=0, bytes_accessed=4_000_000, transcendentals=0),
    )(where, slot_of_band, block_offsets, filters, vertical)
    return filt.reshape(group, REACH + 1, 2 * c, 2 * c), vert


def row_weights(where_ref, slot_ref, weight_ref, r, b, rows, row_total):
    group = slot_ref.shape[0] // where_ref[3]
    band = band_of(slot_ref, where_ref[1] * group + b)
    row = where_ref[0] * rows + r
    above = jnp.where(row > 0, weight_ref[band, 0], 0.0)
    below = jnp.where(row + 1 < row_total, weight_ref[band, 2], 0.0)
    return above, weight_ref[band, 1], below


def fill_window(window, place, weights, r, sides):
    chips = len(sides[0])
    shard_rows, per_source, _, c = sides[0][0].shape
    half = chips * per_source
    first = lax.rem(place, 2) * ((shard_rows - 2) // 2) + r
    for k in range(chips):
        for side in range(2):
            source = (place ^ (2 * k)) ^ side
            for n in range(per_source):
                value = None
                for i in range(3):
                    term = weights[i] * sides[side][k][first + i, n].astype(jnp.float32)
                    value = term if value is None else value + term
                e = lax.rem(source * (per_source // 2) + (n + REACH) // 2, half)
                lane = (n + REACH) % 2 * c
                window[e, :, lane : lane + c] = value.astype(jnp.bfloat16)
    for e in range(window.shape[0] - half):
        window[half + e] = window[e]


def filtered(window, filt, j, step):
    _, depth, width = window.shape
    total = None
    for t in range(filt.shape[0]):
        lhs = window[j + t : j + t + step].reshape(step * depth, width)
        term = jnp.dot(lhs, filt[t], preferred_element_type=jnp.float32)
        total = term if total is None else total + term
    return total.astype(jnp.bfloat16)


def first_kernel(chips, where_ref, slot_ref, weight_ref, *refs):
    kept, got, (filt_ref, out_ref, window) = refs[:chips], refs[chips : 2 * chips], refs[2 * chips :]
    r, b = pl.program_id(0), pl.program_id(1)
    rows = (kept[0].shape[0] - 2) // 2
    weights = row_weights(where_ref, slot_ref, weight_ref, r, b, rows, 2 * rows * chips)
    fill_window(window, where_ref[0], weights, r, (kept, got))
    half, depth, width = out_ref.shape[2:]
    step = 4
    for j in range(0, half, step):
        out_ref[0, 0, j : j + step] = filtered(window, filt_ref[0], j, step).reshape(step, depth, width)


def last_kernel(chips, where_ref, slot_ref, weight_ref, *refs):
    kept, got, refs = refs[:chips], refs[chips : 2 * chips], refs[2 * chips :]
    filt_ref, vert_ref = refs[:2]
    done, (out_ref, window, spread) = refs[2:-3], refs[-3:]
    r, b = pl.program_id(0), pl.program_id(1)
    rows = (kept[0].shape[0] - 2) // 2
    weights = row_weights(where_ref, slot_ref, weight_ref, r, b, rows, 2 * rows * chips)
    fill_window(window, where_ref[0], weights, r, (kept, got))
    levels, blocks, c = out_ref.shape[2:]
    half, depth = blocks // 2, window.shape[1]
    padded = vert_ref.shape[1]
    pitch = spread.shape[0] // padded
    step = 4
    for j in range(0, half, step):
        later = filtered(window, filt_ref[0], j, step)
        for i in range(step):
            column = [d[0, 0, j + i] for d in done] + [later[i * depth : (i + 1) * depth]]
            column = jnp.concatenate(column, axis=0)
            mixed = jnp.dot(vert_ref[0], column, preferred_element_type=jnp.float32)
            for h in range(2):
                spread[pl.ds(2 * (j + i) + h, padded, stride=pitch), :] = mixed[:, h * c : (h + 1) * c]
    for m in range(levels):
        out_ref[0, 0, m] = spread[m * pitch : m * pitch + blocks].astype(jnp.bfloat16)


def whole(a):
    return pl.BlockSpec(a.shape, lambda r, b: (0,) * a.ndim)


def banded(a):
    return pl.BlockSpec((1,) + a.shape[1:], lambda r, b: (b,) + (0,) * (a.ndim - 1))


def by_row_and_band(a):
    return pl.BlockSpec((1, 1) + a.shape[2:], lambda r, b: (b, r) + (0,) * (a.ndim - 2))


def first_part(scalars, kept, got, filt, rows):
    group, taps, width, _ = filt.shape
    _, per_source, depth, _ = kept[0].shape
    half = len(kept) * per_source
    out = jax.ShapeDtypeStruct((group, rows, half, depth, width), jnp.bfloat16)
    return pl.pallas_call(
        functools.partial(first_kernel, len(kept)),
        grid=(rows, group),
        in_specs=[SCALAR] * 3 + [whole(m) for m in kept + got] + [banded(filt)],
        out_specs=by_row_and_band(out),
        out_shape=out,
        scratch_shapes=[pltpu.VMEM((half + taps - 1, depth, width), jnp.bfloat16)],
        compiler_params=PARAMS,
        cost_estimate=pl.CostEstimate(flops=2_000_000_000, bytes_accessed=8_000_000, transcendentals=0),
    )(*scalars, *kept, *got, filt)


def last_part(scalars, kept, got, filt, vert, done, rows, levels):
    group, taps, width, _ = filt.shape
    _, per_source, depth, c = kept[0].shape
    half = len(kept) * per_source
    padded = vert.shape[1]
    out = jax.ShapeDtypeStruct((group, rows, levels, 2 * half, c), jnp.bfloat16)
    return pl.pallas_call(
        functools.partial(last_kernel, len(kept)),
        grid=(rows, group),
        in_specs=[SCALAR] * 3
        + [whole(m) for m in kept + got]
        + [banded(filt), banded(vert)]
        + [by_row_and_band(d) for d in done],
        out_specs=by_row_and_band(out),
        out_shape=out,
        scratch_shapes=[
            pltpu.VMEM((half + taps - 1, depth, width), jnp.bfloat16),
            pltpu.VMEM((padded * (2 * half + SPREAD_GAP), c), jnp.float32),
        ],
        compiler_params=PARAMS,
        cost_estimate=pl.CostEstimate(flops=4_000_000_000, bytes_accessed=12_000_000, transcendentals=0),
    )(*scalars, *kept, *got, filt, vert, *done)


def swapped(value, axis, by):
    return lax.ppermute(value, axis, [(i, i ^ by) for i in range(lax.axis_size(axis))])


def sort_kernel(where_ref, *refs):
    count = (len(refs) - 1) // 2
    pieces, outs, sems = refs[:count], refs[count:-1], refs[-1]
    shard_rows = pieces[0].shape[0]
    chip, z = where_ref[0] // 2, where_ref[1]

    def copies(k, piece):
        main = pltpu.make_async_copy(piece, outs[k].at[pl.ds(1, shard_rows)], sems.at[k, 0])
        above = pltpu.make_async_copy(piece.at[pl.ds(shard_rows - 1, 1)], outs[k].at[pl.ds(0, 1)], sems.at[k, 1])
        below = pltpu.make_async_copy(piece.at[pl.ds(0, 1)], outs[k].at[pl.ds(shard_rows + 1, 1)], sems.at[k, 2])
        return main, above, below

    for k in range(count):
        plane = chip ^ k
        for j, piece in enumerate(pieces):
            main, above, below = copies(k, piece)
            pl.when((plane ^ z) == j)(main.start)
            pl.when((jnp.maximum(plane - 1, 0) ^ z) == j)(above.start)
            pl.when((jnp.minimum(plane + 1, count - 1) ^ z) == j)(below.start)
    for k in range(count):
        for copy in copies(k, pieces[0]):
            copy.wait()


def sorted_rows(where, pieces):
    shape = pieces[0].shape
    out = jax.ShapeDtypeStruct((shape[0] + 2,) + shape[1:], pieces[0].dtype)
    anywhere = pl.BlockSpec(memory_space=pl.ANY)
    return pl.pallas_call(
        sort_kernel,
        in_specs=[SCALAR] + [anywhere] * len(pieces),
        out_specs=[anywhere] * len(pieces),
        out_shape=[out] * len(pieces),
        scratch_shapes=[pltpu.SemaphoreType.DMA((len(pieces), 3))],
        compiler_params=PARAMS,
        cost_estimate=pl.CostEstimate(flops=0, bytes_accessed=3_000_000, transcendentals=0),
    )(where, *pieces)


def along_lat(own):
    order = sorted(range(1, lax.axis_size("lat")), key=lambda j: j == 1)
    got = {j: swapped(own, "lat", j) for j in order}
    return [own] + [got[j] for j in sorted(got)]


def along_lon(sends):
    order = sorted(range(1, len(sends)), key=lambda k: -k)
    got = {k: swapped(sends[k], "lon", 2 * k) for k in order}
    kept = [sends[0]] + [got[k] for k in sorted(got)]
    return kept, [swapped(m, "lon", 1) for m in kept]


def on_device(grad_field, lat_weights, block_offsets, filters, vertical, slot_of_band):
    shard_rows, _, levels, _ = grad_field.shape
    lats, lons = lax.axis_size("lat"), lax.axis_size("lon")
    rows = shard_rows * lats // lons
    group = slot_of_band.shape[0] // lats
    padded = round_up(levels, SUBLANES)
    extra = padded - levels
    cuts = [0] + list(CUTS) + [padded]

    place = [lax.axis_index("lon"), lax.axis_index("lat"), jnp.int32(lons), jnp.int32(lats)]
    where = jnp.stack(place).astype(jnp.int32)
    scalars = (where, slot_of_band, lat_weights)
    filt, vert = owned_tables(where, slot_of_band, block_offsets, filters, vertical, group, padded)

    own = jnp.pad(grad_field.astype(jnp.bfloat16), ((0, 0), (0, 0), (0, extra), (0, 0)))
    parts = [own[:, :, lo:hi] for lo, hi in zip(cuts, cuts[1:])]
    pieces = []
    for part in parts:
        if pieces:
            part, _ = lax.optimization_barrier((part, pieces[-1][2]))
        pieces.append(along_lat(part))
    sides = [along_lon(sorted_rows(where, piece)) for piece in pieces]
    done = [first_part(scalars, kept, got, filt, rows) for kept, got in sides[:-1]]
    kept, got = sides[-1]
    result = last_part(scalars, kept, got, filt, vert, done, rows, levels)
    return result.transpose(0, 1, 3, 2, 4)


def solution(mesh):
    placed = (P("lat", "lon", None, None), P(), P(), P(), P(), P())
    return jax.shard_map(
        on_device,
        mesh=mesh,
        in_specs=placed,
        out_specs=P("lat", "lon", None, None, None),
        check_vma=False,
    )
```

time: 406 us -> 103 us (0.25)
  the two profiles are of different devices: /device:TPU:1 before, /device:TPU:0 now
where the time goes in v2:
time: 103 us; the launch traced here: 102 us
  starting transfers between devices  36.3 us (35%)
  waiting for transfers between devices  31.8 us (31%)
  Pallas kernels  26.9 us (26%)
  local copies, waits for them, and re-layouts  7.07 us (7%)
    ppermute x30, starting transfers between devices, swapped(): lax.ppermute(value, axis, [(i, i ^ by) for i in range(lax.axis_size(axis))])  36.3 us
    ppermute x30, waiting for transfers between devices, swapped(): lax.ppermute(value, axis, [(i, i ^ by) for i in range(lax.axis_size(axis))])  31.8 us
    pallas_call x1, Pallas kernels, last_part(): pl.pallas_call(functools.partial(last_kernel, len(kept)), grid=(rows, gro...  10.1 us
    pallas_call x2, Pallas kernels, first_part(): pl.pallas_call(functools.partial(first_kernel, len(kept)), grid=(rows, gr...  8.79 us
    pallas_call x3, Pallas kernels, sorted_rows(): pl.pallas_call(sort_kernel, in_specs=[SCALAR] + [anywhere] * len(pieces),...  7.21 us
    unnamed x35, local copies, waits for them, and re-layouts  7.01 us
  transfers between devices with their start and end apart: 30, of which 8 were waited for; matrix products, arithmetic and copies ran while one was open for 1% of the time, Pallas kernels for 16%

profile of v2, /device:TPU:0, one launch (start us, length us, event | category | flops | bytes accessed | tf_op | source)
XLA Modules:
  0.0 102.4 jit_solution(8014662278057333277)
XLA Ops:
  0.0 1.4 %copy.13 = bf16[4,4,137,128]{3,2,1,0:T(8,128)(2,1)S(1)} copy(f32[4,4,137,128]{3,1,2,0:T(4,128)} %param.6) | data formatting | bytes 1683456 | tf_op args[0]
  1.4 4.1 %collective-permute-start = (bf16[4,4,48,128]{3,2,1,0:T(8,128)(2,1)S(1)}, bf16[4,4,48,128]{3,2,1,0:T(8,128)(2,1)S(1)}, u32[]{:S(2)}, u32[]{:S(2)}) collective-permute-start(bf16[4,4,48,128]{3,2,1,0:T(8,128)(2,1)S(1)} %get-tuple-element.37.refs_0_), channel_id=1, source_target_pairs={{0,2},{1,3},{2,0},{3,1},{4,6},{5,7},{6,4},{7,5},{8,10},{9,11},{10,... | collective-permute-start | bytes 589832 | tf_op jit(solution)/shard_map/ppermute | solution.py:192
  5.5 1.3 %collective-permute-start.13 = (bf16[4,4,48,128]{3,2,1,0:T(8,128)(2,1)S(1)}, bf16[4,4,48,128]{3,2,1,0:T(8,128)(2,1)S(1)}, u32[]{:S(2)}, u32[]{:S(2)}) collective-permute-start(bf16[4,4,48,128]{3,2,1,0:T(8,128)(2,1)S(1)} %get-tuple-element.37.refs_0_), channel_id=1, source_target_pairs={{0,3},{1,2},{2,1},{3,0},{4,7},{5,6},{6,5},{7,4},{8,11},{9,10},{10,... | collective-permute-start | bytes 589832 | tf_op jit(solution)/shard_map/ppermute | solution.py:192
  7.1 12.6 %collective-permute-done.refs_2_ = bf16[4,4,48,128]{3,2,1,0:T(8,128)(2,1)S(1)} collective-permute-done((bf16[4,4,48,128]{3,2,1,0:T(8,128)(2,1)S(1)}, bf16[4,4,48,128]{3,2,1,0:T(8,128)(2,1)S(1)}, u32[]{:S(2)}, u32[]{:S(2)}) %collective-permute-start) | collective-permute-done | bytes 196640 | tf_op jit(solution)/shard_map/ppermute | solution.py:192
  19.7 2.8 %collective-permute-start.22 = (bf16[4,4,48,128]{3,2,1,0:T(8,128)(2,1)S(1)}, bf16[4,4,48,128]{3,2,1,0:T(8,128)(2,1)S(1)}, u32[]{:S(2)}, u32[]{:S(2)}) collective-permute-start(bf16[4,4,48,128]{3,2,1,0:T(8,128)(2,1)S(1)} %get-tuple-element.21.refs_0_), channel_id=1, source_target_pairs={{0,3},{1,2},{2,1},{3,0},{4,7},{5,6},{6,5},{7,4},{8,11},{9,10},{10,... | collective-permute-start | bytes 589832 | tf_op jit(solution)/shard_map/ppermute | solution.py:192
  22.6 2.4 %shard_map.66 = (bf16[6,4,48,128]{3,2,1,0:T(8,128)(2,1)S(1)}, bf16[6,4,48,128]{3,2,1,0:T(8,128)(2,1)S(1)}, bf16[6,4,48,128]{3,2,1,0:T(8,128)(2,1)S(1)}, bf16[6,4,48,128]{3,2,1,0:T(8,128)(2,1)S(1)}) custom-call(s32[4]{0:T(128)S(1)} %pad_add_fusion.where_ref, bf16[4,4,48,128]{3,2,1,0:T(8,128)(2,1)S(1)} %get-tuple-element.37.refs_0_, ...), custom_call_target="tpu_custom_call" | custom-call | bytes 3000000 | tf_op jit(solution)/shard_map/pallas_call | solution.py:223
  25.1 1.6 %collective-permute-start.14 = (bf16[6,4,48,128]{3,2,1,0:T(8,128)(2,1)S(1)}, bf16[6,4,48,128]{3,2,1,0:T(8,128)(2,1)S(1)}, u32[]{:S(2)}, u32[]{:S(2)}) collective-permute-start(bf16[6,4,48,128]{3,2,1,0:T(8,128)(2,1)S(1)} %get-tuple-element.30), channel_id=1, source_target_pairs={{0,8},{4,12},{8,0},{12,4},{16,24},{20,28},{24,16},{28,20},{1,9},{5... | collective-permute-start | bytes 884744 | tf_op jit(solution)/shard_map/ppermute | solution.py:192
  26.7 1.5 %collective-permute-start.15 = (bf16[6,4,48,128]{3,2,1,0:T(8,128)(2,1)S(1)}, bf16[6,4,48,128]{3,2,1,0:T(8,128)(2,1)S(1)}, u32[]{:S(2)}, u32[]{:S(2)}) collective-permute-start(bf16[6,4,48,128]{3,2,1,0:T(8,128)(2,1)S(1)} %get-tuple-element.31), channel_id=1, source_target_pairs={{0,16},{4,20},{8,24},{12,28},{16,0},{20,4},{24,8},{28,12},{1,17},{... | collective-permute-start | bytes 884744 | tf_op jit(solution)/shard_map/ppermute | solution.py:192
  28.2 10.7 %collective-permute-start.21 = (bf16[4,4,48,128]{3,2,1,0:T(8,128)(2,1)S(1)}, bf16[4,4,48,128]{3,2,1,0:T(8,128)(2,1)S(1)}, u32[]{:S(2)}, u32[]{:S(2)}) collective-permute-start(bf16[4,4,48,128]{3,2,1,0:T(8,128)(2,1)S(1)} %get-tuple-element.21.refs_0_), channel_id=1, source_target_pairs={{0,1},{1,0},{2,3},{3,2},{4,5},{5,4},{6,7},{7,6},{8,9},{9,8},{10,11... | collective-permute-start | bytes 589832 | tf_op jit(solution)/shard_map/ppermute | solution.py:192
  39.0 1.0 collective-permute-done.1.refs_2_
  40.0 2.5 %collective-permute-done.21.refs_1_ = bf16[4,4,48,128]{3,2,1,0:T(8,128)(2,1)S(1)} collective-permute-done((bf16[4,4,48,128]{3,2,1,0:T(8,128)(2,1)S(1)}, bf16[4,4,48,128]{3,2,1,0:T(8,128)(2,1)S(1)}, u32[]{:S(2)}, u32[]{:S(2)}) %collective-permute-start.21) | collective-permute-done | bytes 196640 | tf_op jit(solution)/shard_map/ppermute | solution.py:192
  42.5 3.1 %collective-permute-start.4 = (bf16[4,4,48,128]{3,2,1,0:T(8,128)(2,1)S(1)}, bf16[4,4,48,128]{3,2,1,0:T(8,128)(2,1)S(1)}, u32[]{:S(2)}, u32[]{:S(2)}) collective-permute-start(bf16[4,4,48,128]{3,2,1,0:T(8,128)(2,1)S(1)} %get-tuple-element.22.refs_0_), channel_id=1, source_target_pairs={{0,3},{1,2},{2,1},{3,0},{4,7},{5,6},{6,5},{7,4},{8,11},{9,10},{10,... | collective-permute-start | bytes 589832 | tf_op jit(solution)/shard_map/ppermute | solution.py:192
  45.6 2.4 %shard_map.68 = (bf16[6,4,48,128]{3,2,1,0:T(8,128)(2,1)S(1)}, bf16[6,4,48,128]{3,2,1,0:T(8,128)(2,1)S(1)}, bf16[6,4,48,128]{3,2,1,0:T(8,128)(2,1)S(1)}, bf16[6,4,48,128]{3,2,1,0:T(8,128)(2,1)S(1)}) custom-call(s32[4]{0:T(128)S(1)} %pad_add_fusion.where_ref, bf16[4,4,48,128]{3,2,1,0:T(8,128)(2,1)S(1)} %get-tuple-element.21.refs_0_, ...), custom_call_target="tpu_custom_call" | custom-call | bytes 3000000 | tf_op jit(solution)/shard_map/pallas_call | solution.py:223
  48.1 1.6 %collective-permute-start.23 = (bf16[6,4,48,128]{3,2,1,0:T(8,128)(2,1)S(1)}, bf16[6,4,48,128]{3,2,1,0:T(8,128)(2,1)}, u32[]{:S(2)}, u32[]{:S(2)}) collective-permute-start(bf16[6,4,48,128]{3,2,1,0:T(8,128)(2,1)S(1)} %get-tuple-element.34), channel_id=1, source_target_pairs={{0,8},{4,12},{8,0},{12,4},{16,24},{20,28},{24,16},{28,20},{1,9},{5... | collective-permute-start | bytes 884744 | tf_op jit(solution)/shard_map/ppermute | solution.py:192
  50.4 2.1 %collective-permute-start.2 = (bf16[4,4,48,128]{3,2,1,0:T(8,128)(2,1)S(1)}, bf16[4,4,48,128]{3,2,1,0:T(8,128)(2,1)S(1)}, u32[]{:S(2)}, u32[]{:S(2)}) collective-permute-start(bf16[4,4,48,128]{3,2,1,0:T(8,128)(2,1)S(1)} %get-tuple-element.22.refs_0_), channel_id=1, source_target_pairs={{0,1},{1,0},{2,3},{3,2},{4,5},{5,4},{6,7},{7,6},{8,9},{9,8},{10,11... | collective-permute-start | bytes 589832 | tf_op jit(solution)/shard_map/ppermute | solution.py:192
  52.5 1.2 %collective-permute-start.25 = (bf16[6,4,48,128]{3,2,1,0:T(8,128)(2,1)S(1)}, bf16[6,4,48,128]{3,2,1,0:T(8,128)(2,1)}, u32[]{:S(2)}, u32[]{:S(2)}) collective-permute-start(bf16[6,4,48,128]{3,2,1,0:T(8,128)(2,1)S(1)} %get-tuple-element.36), channel_id=1, source_target_pairs={{0,24},{4,28},{8,16},{12,20},{16,8},{20,12},{24,0},{28,4},{1,25},{... | collective-permute-start | bytes 884744 | tf_op jit(solution)/shard_map/ppermute | solution.py:192
  53.7 6.5 %collective-permute-done.3.refs_2_ = bf16[4,4,48,128]{3,2,1,0:T(8,128)(2,1)S(1)} collective-permute-done((bf16[4,4,48,128]{3,2,1,0:T(8,128)(2,1)S(1)}, bf16[4,4,48,128]{3,2,1,0:T(8,128)(2,1)S(1)}, u32[]{:S(2)}, u32[]{:S(2)}) %collective-permute-start.3) | collective-permute-done | bytes 196640 | tf_op jit(solution)/shard_map/ppermute | solution.py:192
  60.8 2.1 %collective-permute-done.24.refs_2_ = bf16[6,4,48,128]{3,2,1,0:T(8,128)(2,1)} collective-permute-done((bf16[6,4,48,128]{3,2,1,0:T(8,128)(2,1)S(1)}, bf16[6,4,48,128]{3,2,1,0:T(8,128)(2,1)}, u32[]{:S(2)}, u32[]{:S(2)}) %collective-permute-start.24) | collective-permute-done | bytes 294944 | tf_op jit(solution)/shard_map/ppermute | solution.py:192
  62.9 2.3 %shard_map.64 = (bf16[6,4,48,128]{3,2,1,0:T(8,128)(2,1)S(1)}, bf16[6,4,48,128]{3,2,1,0:T(8,128)(2,1)S(1)}, bf16[6,4,48,128]{3,2,1,0:T(8,128)(2,1)}, bf16[6,4,48,128]{3,2,1,0:T(8,128)(2,1)}) custom-call(s32[4]{0:T(128)S(1)} %pad_add_fusion.where_ref, bf16[4,4,48,128]{3,2,1,0:T(8,128)(2,1)S(1)} %get-tuple-element.22.refs_0_, ...), custom_call_target="tpu_custom_call" | custom-call | bytes 3000000 | tf_op jit(solution)/shard_map/pallas_call | solution.py:223
  66.7 2.0 %collective-permute-start.6 = (bf16[6,4,48,128]{3,2,1,0:T(8,128)(2,1)}, bf16[6,4,48,128]{3,2,1,0:T(8,128)(2,1)}, u32[]{:S(2)}, u32[]{:S(2)}) collective-permute-start(bf16[6,4,48,128]{3,2,1,0:T(8,128)(2,1)} %get-tuple-element.25), channel_id=1, source_target_pairs={{0,16},{4,20},{8,24},{12,28},{16,0},{20,4},{24,8},{28,12},{1,17},{... | collective-permute-start | bytes 884744 | tf_op jit(solution)/shard_map/ppermute | solution.py:192
  69.5 1.4 %collective-permute-start.7 = (bf16[6,4,48,128]{3,2,1,0:T(8,128)(2,1)}, bf16[6,4,48,128]{3,2,1,0:T(8,128)(2,1)}, u32[]{:S(2)}, u32[]{:S(2)}) collective-permute-start(bf16[6,4,48,128]{3,2,1,0:T(8,128)(2,1)} %get-tuple-element.26), channel_id=1, source_target_pairs={{0,24},{4,28},{8,16},{12,20},{16,8},{20,12},{24,0},{28,4},{1,25},{... | collective-permute-start | bytes 884744 | tf_op jit(solution)/shard_map/ppermute | solution.py:192
  70.9 0.7 copy-done.11
  71.6 0.7 copy-done.13
  72.9 2.9 %collective-permute-done.5.refs_1_ = bf16[6,4,48,128]{3,2,1,0:T(8,128)(2,1)S(1)} collective-permute-done((bf16[6,4,48,128]{3,2,1,0:T(8,128)(2,1)S(1)}, bf16[6,4,48,128]{3,2,1,0:T(8,128)(2,1)S(1)}, u32[]{:S(2)}, u32[]{:S(2)}) %collective-permute-start.5) | collective-permute-done | bytes 294944 | tf_op jit(solution)/shard_map/ppermute | solution.py:192
  75.8 0.7 copy-done.9
  76.6 1.3 %copy.8.vertical_ref = bf16[8,137,137]{2,1,0:T(8,128)(2,1)S(1)} copy(bf16[8,137,137]{2,0,1:T(8,128)(2,1)} %param.10) | data formatting | bytes 600608 | tf_op args[4]
  77.9 0.8 shard_map.65
  78.7 3.4 %collective-permute-done.6.refs_2_ = bf16[6,4,48,128]{3,2,1,0:T(8,128)(2,1)} collective-permute-done((bf16[6,4,48,128]{3,2,1,0:T(8,128)(2,1)}, bf16[6,4,48,128]{3,2,1,0:T(8,128)(2,1)}, u32[]{:S(2)}, u32[]{:S(2)}) %collective-permute-start.6) | collective-permute-done | bytes 294944 | tf_op jit(solution)/shard_map/ppermute | solution.py:192
  82.1 0.7 collective-permute-done.7.refs_3_
  83.4 4.0 %shard_map.67.refs_10_ = bf16[2,2,16,48,256]{4,3,2,1,0:T(8,128)(2,1)S(1)} custom-call(s32[4]{0:T(128)S(1)} %pad_add_fusion.where_ref, s32[8]{0:T(128)S(1)} %copy-done.2, f32[8,3]{1,0:T(8,128)S(1)} %copy.11.weight_ref, bf16[6,4,48,128]{3,2,1,0:T(8,128)(2,1)S(1)} %get-tuple-element.29.refs_0_, bf16[6,4,48,128]{3,2,1,0:T(8,128)(2,1)S(1)} %collective-permute-done.14.refs_1_, ...), custom_call_target="tpu_custom_call" | custom-call | flops 2000000000 | bytes 8000000 | tf_op jit(solution)/shard_map/pallas_call | solution.py:155
  87.4 4.8 %shard_map.69.refs_11_ = bf16[2,2,16,48,256]{4,3,2,1,0:T(8,128)(2,1)S(1)} custom-call(s32[4]{0:T(128)S(1)} %pad_add_fusion.where_ref, s32[8]{0:T(128)S(1)} %copy-done.2, f32[8,3]{1,0:T(8,128)S(1)} %copy.11.weight_ref, bf16[6,4,48,128]{3,2,1,0:T(8,128)(2,1)S(1)} %get-tuple-element.33.refs_0_, bf16[6,4,48,128]{3,2,1,0:T(8,128)(2,1)} %collective-permute-done.23.refs_1_, ...), custom_call_target="tpu_custom_call" | custom-call | flops 2000000000 | bytes 8000000 | tf_op jit(solution)/shard_map/pallas_call | solution.py:155
  92.3 10.1 %shard_map.70 = bf16[2,2,137,32,128]{4,3,2,1,0:T(8,128)(2,1)} custom-call(s32[4]{0:T(128)S(1)} %pad_add_fusion.where_ref, s32[8]{0:T(128)S(1)} %copy-done.2, f32[8,3]{1,0:T(8,128)S(1)} %copy.11.weight_ref, bf16[6,4,48,128]{3,2,1,0:T(8,128)(2,1)S(1)} %copy-done.6, bf16[6,4,48,128]{3,2,1,0:T(8,128)(2,1)S(1)} %copy-done.10, ...), custom_call_target="tpu_custom_call" | custom-call | flops 4000000000 | bytes 12000000 | tf_op jit(solution)/shard_map/pallas_call | solution.py:173
  (72 shorter events, 5.2 us)
Async XLA Ops:
  1.4 75.1 %copy-start.15 = (f32[8,3]{0,1:T(4,128)S(1)}, f32[8,3]{0,1:T(4,128)}, u32[]{:S(2)}) copy-start(f32[8,3]{0,1:T(4,128)} %param.7) | copy-start | bytes 292
  1.4 18.3 %collective-permute-start = (bf16[4,4,48,128]{3,2,1,0:T(8,128)(2,1)S(1)}, bf16[4,4,48,128]{3,2,1,0:T(8,128)(2,1)S(1)}, u32[]{:S(2)}, u32[]{:S(2)}) collective-permute-start(bf16[4,4,48,128]{3,2,1,0:T(8,128)(2,1)S(1)} %get-tuple-element.37.refs_0_), channel_id=1, source_target_pairs={{0,2},{1,3},{2,0},{3,1},{4,6},{5,7},{6,4},{7,5},{8,10},{9,11},{10,... | collective-permute-start | bytes 589832 | tf_op jit(solution)/shard_map/ppermute | solution.py:192
  5.5 17.1 %collective-permute-start.13 = (bf16[4,4,48,128]{3,2,1,0:T(8,128)(2,1)S(1)}, bf16[4,4,48,128]{3,2,1,0:T(8,128)(2,1)S(1)}, u32[]{:S(2)}, u32[]{:S(2)}) collective-permute-start(bf16[4,4,48,128]{3,2,1,0:T(8,128)(2,1)S(1)} %get-tuple-element.37.refs_0_), channel_id=1, source_target_pairs={{0,3},{1,2},{2,1},{3,0},{4,7},{5,6},{6,5},{7,4},{8,11},{9,10},{10,... | collective-permute-start | bytes 589832 | tf_op jit(solution)/shard_map/ppermute | solution.py:192
  6.9 15.7 %collective-permute-start.12 = (bf16[4,4,48,128]{3,2,1,0:T(8,128)(2,1)S(1)}, bf16[4,4,48,128]{3,2,1,0:T(8,128)(2,1)S(1)}, u32[]{:S(2)}, u32[]{:S(2)}) collective-permute-start(bf16[4,4,48,128]{3,2,1,0:T(8,128)(2,1)S(1)} %get-tuple-element.37.refs_0_), channel_id=1, source_target_pairs={{0,1},{1,0},{2,3},{3,2},{4,5},{5,4},{6,7},{7,6},{8,9},{9,8},{10,11... | collective-permute-start | bytes 589832 | tf_op jit(solution)/shard_map/ppermute | solution.py:192
  19.7 19.1 %collective-permute-start.22 = (bf16[4,4,48,128]{3,2,1,0:T(8,128)(2,1)S(1)}, bf16[4,4,48,128]{3,2,1,0:T(8,128)(2,1)S(1)}, u32[]{:S(2)}, u32[]{:S(2)}) collective-permute-start(bf16[4,4,48,128]{3,2,1,0:T(8,128)(2,1)S(1)} %get-tuple-element.21.refs_0_), channel_id=1, source_target_pairs={{0,3},{1,2},{2,1},{3,0},{4,7},{5,6},{6,5},{7,4},{8,11},{9,10},{10,... | collective-permute-start | bytes 589832 | tf_op jit(solution)/shard_map/ppermute | solution.py:192
  22.5 17.4 %collective-permute-start.1 = (bf16[4,4,48,128]{3,2,1,0:T(8,128)(2,1)S(1)}, bf16[4,4,48,128]{3,2,1,0:T(8,128)(2,1)S(1)}, u32[]{:S(2)}, u32[]{:S(2)}) collective-permute-start(bf16[4,4,48,128]{3,2,1,0:T(8,128)(2,1)S(1)} %get-tuple-element.21.refs_0_), channel_id=1, source_target_pairs={{0,2},{1,3},{2,0},{3,1},{4,6},{5,7},{6,4},{7,5},{8,10},{9,11},{10,... | collective-permute-start | bytes 589832 | tf_op jit(solution)/shard_map/ppermute | solution.py:192
  25.1 52.8 %copy-start = (bf16[8,5,128,128]{3,2,1,0:T(8,128)(2,1)S(1)}, bf16[8,5,128,128]{3,2,1,0:T(8,128)(2,1)}, u32[]{:S(2)}) copy-start(bf16[8,5,128,128]{3,2,1,0:T(8,128)(2,1)} %filter_ref.1) | copy-start | bytes 3932164
  25.1 23.0 %collective-permute-start.14 = (bf16[6,4,48,128]{3,2,1,0:T(8,128)(2,1)S(1)}, bf16[6,4,48,128]{3,2,1,0:T(8,128)(2,1)S(1)}, u32[]{:S(2)}, u32[]{:S(2)}) collective-permute-start(bf16[6,4,48,128]{3,2,1,0:T(8,128)(2,1)S(1)} %get-tuple-element.30), channel_id=1, source_target_pairs={{0,8},{4,12},{8,0},{12,4},{16,24},{20,28},{24,16},{28,20},{1,9},{5... | collective-permute-start | bytes 884744 | tf_op jit(solution)/shard_map/ppermute | solution.py:192
  26.7 23.0 %collective-permute-start.15 = (bf16[6,4,48,128]{3,2,1,0:T(8,128)(2,1)S(1)}, bf16[6,4,48,128]{3,2,1,0:T(8,128)(2,1)S(1)}, u32[]{:S(2)}, u32[]{:S(2)}) collective-permute-start(bf16[6,4,48,128]{3,2,1,0:T(8,128)(2,1)S(1)} %get-tuple-element.31), channel_id=1, source_target_pairs={{0,16},{4,20},{8,24},{12,28},{16,0},{20,4},{24,8},{28,12},{1,17},{... | collective-permute-start | bytes 884744 | tf_op jit(solution)/shard_map/ppermute | solution.py:192
  28.2 14.3 %collective-permute-start.21 = (bf16[4,4,48,128]{3,2,1,0:T(8,128)(2,1)S(1)}, bf16[4,4,48,128]{3,2,1,0:T(8,128)(2,1)S(1)}, u32[]{:S(2)}, u32[]{:S(2)}) collective-permute-start(bf16[4,4,48,128]{3,2,1,0:T(8,128)(2,1)S(1)} %get-tuple-element.21.refs_0_), channel_id=1, source_target_pairs={{0,1},{1,0},{2,3},{3,2},{4,5},{5,4},{6,7},{7,6},{8,9},{9,8},{10,11... | collective-permute-start | bytes 589832 | tf_op jit(solution)/shard_map/ppermute | solution.py:192
  38.9 11.4 %collective-permute-start.16 = (bf16[6,4,48,128]{3,2,1,0:T(8,128)(2,1)S(1)}, bf16[6,4,48,128]{3,2,1,0:T(8,128)(2,1)S(1)}, u32[]{:S(2)}, u32[]{:S(2)}) collective-permute-start(bf16[6,4,48,128]{3,2,1,0:T(8,128)(2,1)S(1)} %get-tuple-element.32), channel_id=1, source_target_pairs={{0,24},{4,28},{8,16},{12,20},{16,8},{20,12},{24,0},{28,4},{1,25},{... | collective-permute-start | bytes 884744 | tf_op jit(solution)/shard_map/ppermute | solution.py:192
  40.0 10.4 %collective-permute-start.17 = (bf16[6,4,48,128]{3,2,1,0:T(8,128)(2,1)S(1)}, bf16[6,4,48,128]{3,2,1,0:T(8,128)(2,1)S(1)}, u32[]{:S(2)}, u32[]{:S(2)}) collective-permute-start(bf16[6,4,48,128]{3,2,1,0:T(8,128)(2,1)S(1)} %get-tuple-element.29.refs_0_), channel_id=1, source_target_pairs={{0,4},{4,0},{8,12},{12,8},{16,20},{20,16},{24,28},{28,24},{1,5},{5... | collective-permute-start | bytes 884744 | tf_op jit(solution)/shard_map/ppermute | solution.py:192
  42.5 10.0 %collective-permute-start.4 = (bf16[4,4,48,128]{3,2,1,0:T(8,128)(2,1)S(1)}, bf16[4,4,48,128]{3,2,1,0:T(8,128)(2,1)S(1)}, u32[]{:S(2)}, u32[]{:S(2)}) collective-permute-start(bf16[4,4,48,128]{3,2,1,0:T(8,128)(2,1)S(1)} %get-tuple-element.22.refs_0_), channel_id=1, source_target_pairs={{0,3},{1,2},{2,1},{3,0},{4,7},{5,6},{6,5},{7,4},{8,11},{9,10},{10,... | collective-permute-start | bytes 589832 | tf_op jit(solution)/shard_map/ppermute | solution.py:192
  48.1 12.6 %collective-permute-start.23 = (bf16[6,4,48,128]{3,2,1,0:T(8,128)(2,1)S(1)}, bf16[6,4,48,128]{3,2,1,0:T(8,128)(2,1)}, u32[]{:S(2)}, u32[]{:S(2)}) collective-permute-start(bf16[6,4,48,128]{3,2,1,0:T(8,128)(2,1)S(1)} %get-tuple-element.34), channel_id=1, source_target_pairs={{0,8},{4,12},{8,0},{12,4},{16,24},{20,28},{24,16},{28,20},{1,9},{5... | collective-permute-start | bytes 884744 | tf_op jit(solution)/shard_map/ppermute | solution.py:192
  49.6 13.3 %collective-permute-start.24 = (bf16[6,4,48,128]{3,2,1,0:T(8,128)(2,1)S(1)}, bf16[6,4,48,128]{3,2,1,0:T(8,128)(2,1)}, u32[]{:S(2)}, u32[]{:S(2)}) collective-permute-start(bf16[6,4,48,128]{3,2,1,0:T(8,128)(2,1)S(1)} %get-tuple-element.35), channel_id=1, source_target_pairs={{0,16},{4,20},{8,24},{12,28},{16,0},{20,4},{24,8},{28,12},{1,17},{... | collective-permute-start | bytes 884744 | tf_op jit(solution)/shard_map/ppermute | solution.py:192
  50.3 9.9 %collective-permute-start.3 = (bf16[4,4,48,128]{3,2,1,0:T(8,128)(2,1)S(1)}, bf16[4,4,48,128]{3,2,1,0:T(8,128)(2,1)S(1)}, u32[]{:S(2)}, u32[]{:S(2)}) collective-permute-start(bf16[4,4,48,128]{3,2,1,0:T(8,128)(2,1)S(1)} %get-tuple-element.22.refs_0_), channel_id=1, source_target_pairs={{0,2},{1,3},{2,0},{3,1},{4,6},{5,7},{6,4},{7,5},{8,10},{9,11},{10,... | collective-permute-start | bytes 589832 | tf_op jit(solution)/shard_map/ppermute | solution.py:192
  50.4 9.9 %collective-permute-start.2 = (bf16[4,4,48,128]{3,2,1,0:T(8,128)(2,1)S(1)}, bf16[4,4,48,128]{3,2,1,0:T(8,128)(2,1)S(1)}, u32[]{:S(2)}, u32[]{:S(2)}) collective-permute-start(bf16[4,4,48,128]{3,2,1,0:T(8,128)(2,1)S(1)} %get-tuple-element.22.refs_0_), channel_id=1, source_target_pairs={{0,1},{1,0},{2,3},{3,2},{4,5},{5,4},{6,7},{7,6},{8,9},{9,8},{10,11... | collective-permute-start | bytes 589832 | tf_op jit(solution)/shard_map/ppermute | solution.py:192
  52.5 13.5 %collective-permute-start.25 = (bf16[6,4,48,128]{3,2,1,0:T(8,128)(2,1)S(1)}, bf16[6,4,48,128]{3,2,1,0:T(8,128)(2,1)}, u32[]{:S(2)}, u32[]{:S(2)}) collective-permute-start(bf16[6,4,48,128]{3,2,1,0:T(8,128)(2,1)S(1)} %get-tuple-element.36), channel_id=1, source_target_pairs={{0,24},{4,28},{8,16},{12,20},{16,8},{20,12},{24,0},{28,4},{1,25},{... | collective-permute-start | bytes 884744 | tf_op jit(solution)/shard_map/ppermute | solution.py:192
  60.2 5.8 %collective-permute-start.26 = (bf16[6,4,48,128]{3,2,1,0:T(8,128)(2,1)S(1)}, bf16[6,4,48,128]{3,2,1,0:T(8,128)(2,1)S(1)}, u32[]{:S(2)}, u32[]{:S(2)}) collective-permute-start(bf16[6,4,48,128]{3,2,1,0:T(8,128)(2,1)S(1)} %get-tuple-element.33.refs_0_), channel_id=1, source_target_pairs={{0,4},{4,0},{8,12},{12,8},{16,20},{20,16},{24,28},{28,24},{1,5},{5... | collective-permute-start | bytes 884744 | tf_op jit(solution)/shard_map/ppermute | solution.py:192
  60.2 8.6 %collective-permute-start.18 = (bf16[6,4,48,128]{3,2,1,0:T(8,128)(2,1)S(1)}, bf16[6,4,48,128]{3,2,1,0:T(8,128)(2,1)S(1)}, u32[]{:S(2)}, u32[]{:S(2)}) collective-permute-start(bf16[6,4,48,128]{3,2,1,0:T(8,128)(2,1)S(1)} %collective-permute-done.14.refs_1_), channel_id=1, source_target_pairs={{0,4},{4,0},{8,12},{12,8},{16,20},{20,16},{24,28},{28,24},{1,5},{5... | collective-permute-start | bytes 884744 | tf_op jit(solution)/shard_map/ppermute | solution.py:192
  60.7 10.2 %collective-permute-start.19 = (bf16[6,4,48,128]{3,2,1,0:T(8,128)(2,1)S(1)}, bf16[6,4,48,128]{3,2,1,0:T(8,128)(2,1)S(1)}, u32[]{:S(2)}, u32[]{:S(2)}) collective-permute-start(bf16[6,4,48,128]{3,2,1,0:T(8,128)(2,1)S(1)} %collective-permute-done.15.refs_2_), channel_id=1, source_target_pairs={{0,4},{4,0},{8,12},{12,8},{16,20},{20,16},{24,28},{28,24},{1,5},{5... | collective-permute-start | bytes 884744 | tf_op jit(solution)/shard_map/ppermute | solution.py:192
  62.9 8.7 %collective-permute-start.20 = (bf16[6,4,48,128]{3,2,1,0:T(8,128)(2,1)S(1)}, bf16[6,4,48,128]{3,2,1,0:T(8,128)(2,1)S(1)}, u32[]{:S(2)}, u32[]{:S(2)}) collective-permute-start(bf16[6,4,48,128]{3,2,1,0:T(8,128)(2,1)S(1)} %collective-permute-done.16.refs_3_), channel_id=1, source_target_pairs={{0,4},{4,0},{8,12},{12,8},{16,20},{20,16},{24,28},{28,24},{1,5},{5... | collective-permute-start | bytes 884744 | tf_op jit(solution)/shard_map/ppermute | solution.py:192
  66.0 9.8 %collective-permute-start.5 = (bf16[6,4,48,128]{3,2,1,0:T(8,128)(2,1)S(1)}, bf16[6,4,48,128]{3,2,1,0:T(8,128)(2,1)S(1)}, u32[]{:S(2)}, u32[]{:S(2)}) collective-permute-start(bf16[6,4,48,128]{3,2,1,0:T(8,128)(2,1)S(1)} %get-tuple-element.24), channel_id=1, source_target_pairs={{0,8},{4,12},{8,0},{12,4},{16,24},{20,28},{24,16},{28,20},{1,9},{5... | collective-permute-start | bytes 884744 | tf_op jit(solution)/shard_map/ppermute | solution.py:192
  66.7 15.3 %collective-permute-start.6 = (bf16[6,4,48,128]{3,2,1,0:T(8,128)(2,1)}, bf16[6,4,48,128]{3,2,1,0:T(8,128)(2,1)}, u32[]{:S(2)}, u32[]{:S(2)}) collective-permute-start(bf16[6,4,48,128]{3,2,1,0:T(8,128)(2,1)} %get-tuple-element.25), channel_id=1, source_target_pairs={{0,16},{4,20},{8,24},{12,28},{16,0},{20,4},{24,8},{28,12},{1,17},{... | collective-permute-start | bytes 884744 | tf_op jit(solution)/shard_map/ppermute | solution.py:192
  69.5 13.3 %collective-permute-start.7 = (bf16[6,4,48,128]{3,2,1,0:T(8,128)(2,1)}, bf16[6,4,48,128]{3,2,1,0:T(8,128)(2,1)}, u32[]{:S(2)}, u32[]{:S(2)}) collective-permute-start(bf16[6,4,48,128]{3,2,1,0:T(8,128)(2,1)} %get-tuple-element.26), channel_id=1, source_target_pairs={{0,24},{4,28},{8,16},{12,20},{16,8},{20,12},{24,0},{28,4},{1,25},{... | collective-permute-start | bytes 884744 | tf_op jit(solution)/shard_map/ppermute | solution.py:192
  71.6 11.2 %collective-permute-start.27 = (bf16[6,4,48,128]{3,2,1,0:T(8,128)(2,1)}, bf16[6,4,48,128]{3,2,1,0:T(8,128)(2,1)}, u32[]{:S(2)}, u32[]{:S(2)}) collective-permute-start(bf16[6,4,48,128]{3,2,1,0:T(8,128)(2,1)} %collective-permute-done.23.refs_1_), channel_id=1, source_target_pairs={{0,4},{4,0},{8,12},{12,8},{16,20},{20,16},{24,28},{28,24},{1,5},{5... | collective-permute-start | bytes 884744 | tf_op jit(solution)/shard_map/ppermute | solution.py:192
  72.4 11.0 %collective-permute-start.28 = (bf16[6,4,48,128]{3,2,1,0:T(8,128)(2,1)}, bf16[6,4,48,128]{3,2,1,0:T(8,128)(2,1)}, u32[]{:S(2)}, u32[]{:S(2)}) collective-permute-start(bf16[6,4,48,128]{3,2,1,0:T(8,128)(2,1)} %collective-permute-done.24.refs_2_), channel_id=1, source_target_pairs={{0,4},{4,0},{8,12},{12,8},{16,20},{20,16},{24,28},{28,24},{1,5},{5... | collective-permute-start | bytes 884744 | tf_op jit(solution)/shard_map/ppermute | solution.py:192
  76.5 10.8 %collective-permute-start.29 = (bf16[6,4,48,128]{3,2,1,0:T(8,128)(2,1)}, bf16[6,4,48,128]{3,2,1,0:T(8,128)(2,1)}, u32[]{:S(2)}, u32[]{:S(2)}) collective-permute-start(bf16[6,4,48,128]{3,2,1,0:T(8,128)(2,1)} %collective-permute-done.25.refs_3_), channel_id=1, source_target_pairs={{0,4},{4,0},{8,12},{12,8},{16,20},{20,16},{24,28},{28,24},{1,5},{5... | collective-permute-start | bytes 884744 | tf_op jit(solution)/shard_map/ppermute | solution.py:192
  82.1 10.2 %collective-permute-start.8 = (bf16[6,4,48,128]{3,2,1,0:T(8,128)(2,1)S(1)}, bf16[6,4,48,128]{3,2,1,0:T(8,128)(2,1)S(1)}, u32[]{:S(2)}, u32[]{:S(2)}) collective-permute-start(bf16[6,4,48,128]{3,2,1,0:T(8,128)(2,1)S(1)} %copy-done.6), channel_id=1, source_target_pairs={{0,4},{4,0},{8,12},{12,8},{16,20},{20,16},{24,28},{28,24},{1,5},{5... | collective-permute-start | bytes 884744 | tf_op jit(solution)/shard_map/ppermute | solution.py:192
  82.8 9.4 %collective-permute-start.9 = (bf16[6,4,48,128]{3,2,1,0:T(8,128)(2,1)S(1)}, bf16[6,4,48,128]{3,2,1,0:T(8,128)(2,1)S(1)}, u32[]{:S(2)}, u32[]{:S(2)}) collective-permute-start(bf16[6,4,48,128]{3,2,1,0:T(8,128)(2,1)S(1)} %copy-done.10), channel_id=1, source_target_pairs={{0,4},{4,0},{8,12},{12,8},{16,20},{20,16},{24,28},{28,24},{1,5},{5... | collective-permute-start | bytes 884744 | tf_op jit(solution)/shard_map/ppermute | solution.py:192
  82.8 9.4 %collective-permute-start.10 = (bf16[6,4,48,128]{3,2,1,0:T(8,128)(2,1)}, bf16[6,4,48,128]{3,2,1,0:T(8,128)(2,1)S(1)}, u32[]{:S(2)}, u32[]{:S(2)}) collective-permute-start(bf16[6,4,48,128]{3,2,1,0:T(8,128)(2,1)} %collective-permute-done.6.refs_2_), channel_id=1, source_target_pairs={{0,4},{4,0},{8,12},{12,8},{16,20},{20,16},{24,28},{28,24},{1,5},{5... | collective-permute-start | bytes 884744 | tf_op jit(solution)/shard_map/ppermute | solution.py:192
  83.3 8.9 %collective-permute-start.11 = (bf16[6,4,48,128]{3,2,1,0:T(8,128)(2,1)}, bf16[6,4,48,128]{3,2,1,0:T(8,128)(2,1)S(1)}, u32[]{:S(2)}, u32[]{:S(2)}) collective-permute-start(bf16[6,4,48,128]{3,2,1,0:T(8,128)(2,1)} %collective-permute-done.7.refs_3_), channel_id=1, source_target_pairs={{0,4},{4,0},{8,12},{12,8},{16,20},{20,16},{24,28},{28,24},{1,5},{5... | collective-permute-start | bytes 884744 | tf_op jit(solution)/shard_map/ppermute | solution.py:192
  (14 other events, 156.5 us)

commit v3 on v2

--- a/solution.py
+++ b/solution.py
@@ -10,7 +10,7 @@
 REACH = 3
 SUBLANES = 16
 SPREAD_GAP = 8
-CUTS = (48, 96)
+CUTS = (48, 112)
 
 
 SCALAR = pl.BlockSpec(memory_space=pltpu.SMEM)
@@ -68,9 +68,9 @@
     return above, weight_ref[band, 1], below
 
 
-def fill_window(window, place, weights, r, sides):
-    chips = len(sides[0])
-    shard_rows, per_source, _, c = sides[0][0].shape
+def fill_window(window, place, weights, r, kept, got):
+    chips = len(kept)
+    shard_rows, per_source, _, c = kept[0].shape
     half = chips * per_source
     first = lax.rem(place, 2) * ((shard_rows - 2) // 2) + r
     for k in range(chips):
@@ -79,7 +79,13 @@
             for n in range(per_source):
                 value = None
                 for i in range(3):
-                    term = weights[i] * sides[side][k][first + i, n].astype(jnp.float32)
+                    if side == 0:
+                        row = kept[k][first + i, n]
+                    elif len(got[0].shape) == 5:
+                        row = got[0][k, r + i, n]
+                    else:
+                        row = got[k][first + i, n]
+                    term = weights[i] * row.astype(jnp.float32)
                     value = term if value is None else value + term
                 e = lax.rem(source * (per_source // 2) + (n + REACH) // 2, half)
                 lane = (n + REACH) % 2 * c
@@ -99,11 +105,11 @@
 
 
 def first_kernel(chips, where_ref, slot_ref, weight_ref, *refs):
-    kept, got, (filt_ref, out_ref, window) = refs[:chips], refs[chips : 2 * chips], refs[2 * chips :]
+    kept, got, (filt_ref, out_ref, window) = refs[:chips], refs[chips:-3], refs[-3:]
     r, b = pl.program_id(0), pl.program_id(1)
     rows = (kept[0].shape[0] - 2) // 2
     weights = row_weights(where_ref, slot_ref, weight_ref, r, b, rows, 2 * rows * chips)
-    fill_window(window, where_ref[0], weights, r, (kept, got))
+    fill_window(window, where_ref[0], weights, r, kept, got)
     half, depth, width = out_ref.shape[2:]
     step = 4
     for j in range(0, half, step):
@@ -117,7 +123,7 @@
     r, b = pl.program_id(0), pl.program_id(1)
     rows = (kept[0].shape[0] - 2) // 2
     weights = row_weights(where_ref, slot_ref, weight_ref, r, b, rows, 2 * rows * chips)
-    fill_window(window, where_ref[0], weights, r, (kept, got))
+    fill_window(window, where_ref[0], weights, r, kept, got)
     levels, blocks, c = out_ref.shape[2:]
     half, depth = blocks // 2, window.shape[1]
     padded = vert_ref.shape[1]
@@ -232,16 +238,22 @@
 
 
 def along_lat(own):
-    order = sorted(range(1, lax.axis_size("lat")), key=lambda j: j == 1)
-    got = {j: swapped(own, "lat", j) for j in order}
-    return [own] + [got[j] for j in sorted(got)]
+    pieces = {0: own}
+    step = lax.axis_size("lat") // 2
+    while step:
+        pieces.update({j | step: swapped(piece, "lat", step) for j, piece in list(pieces.items())})
+        step //= 2
+    return [pieces[j] for j in range(len(pieces))]
 
 
 def along_lon(sends):
     order = sorted(range(1, len(sends)), key=lambda k: -k)
     got = {k: swapped(sends[k], "lon", 2 * k) for k in order}
-    kept = [sends[0]] + [got[k] for k in sorted(got)]
-    return kept, [swapped(m, "lon", 1) for m in kept]
+    return [sends[0]] + [got[k] for k in sorted(got)]
+
+
+def after(value, *marks):
+    return lax.optimization_barrier((value, marks))[0]
 
 
 def on_device(grad_field, lat_weights, block_offsets, filters, vertical, slot_of_band):
@@ -260,15 +272,20 @@
 
     own = jnp.pad(grad_field.astype(jnp.bfloat16), ((0, 0), (0, 0), (0, extra), (0, 0)))
     parts = [own[:, :, lo:hi] for lo, hi in zip(cuts, cuts[1:])]
+    last = len(parts) - 1
     pieces = []
     for part in parts:
-        if pieces:
-            part, _ = lax.optimization_barrier((part, pieces[-1][2]))
-        pieces.append(along_lat(part))
-    sides = [along_lon(sorted_rows(where, piece)) for piece in pieces]
-    done = [first_part(scalars, kept, got, filt, rows) for kept, got in sides[:-1]]
-    kept, got = sides[-1]
-    result = last_part(scalars, kept, got, filt, vert, done, rows, levels)
+        pieces.append(along_lat(after(part, pieces[-1][2]) if pieces else part))
+    sends = [sorted_rows(where, piece) for piece in pieces]
+    kept = [along_lon(send) for send in sends]
+    done = []
+    for i in range(last):
+        here = after(kept[i], sends[i + 1])
+        got = [swapped(m, "lon", 1) for m in here]
+        done.append(first_part(scalars, here, got, filt, rows))
+    here = kept[last][:1] + after(kept[last][1:], *done)
+    got = [swapped(m, "lon", 1) for m in here]
+    result = last_part(scalars, here, got, filt, vert, done, rows, levels)
     return result.transpose(0, 1, 3, 2, 4)
 
 

time: 103 us -> 94.8 us (0.920)
  starting transfers between devices: 36.3 us -> 26.9 us
  waiting for transfers between devices: 31.8 us -> 35.6 us
  Pallas kernels: 26.9 us -> 23.3 us
  local copies, waits for them, and re-layouts: 7.07 us -> 8.44 us
    ppermute x30, starting transfers between devices: 36.3 us -> 26.9 us  [swapped(): lax.ppermute(value, axis, [(i, i ^ by) for i in range(lax.axis_size(axis))])]
    ppermute x30, waiting for transfers between devices: 31.8 us -> 35.6 us  [swapped(): lax.ppermute(value, axis, [(i, i ^ by) for i in range(lax.axis_size(axis))])]
    pallas_call x1, Pallas kernels: 10.1 us -> 6.52 us  [last_part(): pl.pallas_call(functools.partial(last_kernel, len(kept)), grid=(rows, gro...]
    unnamed x35 -> x51, local copies, waits for them, and re-layouts: 7.01 us -> 8.39 us
    pallas_call x3, Pallas kernels: 7.21 us -> 6.04 us  [sorted_rows(): pl.pallas_call(sort_kernel, in_specs=[SCALAR] + [anywhere] * len(pieces),...]
    pallas_call x2, Pallas kernels: 8.79 us -> 9.94 us  [first_part(): pl.pallas_call(functools.partial(first_kernel, len(kept)), grid=(rows, gr...]
  transfers between devices with their start and end apart: 30 -> 30, of which waited for: 8 -> 11; matrix products, arithmetic and copies ran while one was open for 1% -> 2% of each run, Pallas kernels for 16% -> 18%
where the time goes in v3:
time: 94.8 us; the launch traced here: 94.6 us
  waiting for transfers between devices  35.6 us (38%)
  starting transfers between devices  26.9 us (28%)
  Pallas kernels  23.3 us (25%)
  local copies, waits for them, and re-layouts  8.44 us (9%)
    ppermute x30, waiting for transfers between devices, swapped(): lax.ppermute(value, axis, [(i, i ^ by) for i in range(lax.axis_size(axis))])  35.6 us
    ppermute x30, starting transfers between devices, swapped(): lax.ppermute(value, axis, [(i, i ^ by) for i in range(lax.axis_size(axis))])  26.9 us
    pallas_call x2, Pallas kernels, first_part(): pl.pallas_call(functools.partial(first_kernel, len(kept)), grid=(rows, gr...  9.94 us
    unnamed x51, local copies, waits for them, and re-layouts  8.39 us
    pallas_call x1, Pallas kernels, last_part(): pl.pallas_call(functools.partial(last_kernel, len(kept)), grid=(rows, gro...  6.52 us
    pallas_call x3, Pallas kernels, sorted_rows(): pl.pallas_call(sort_kernel, in_specs=[SCALAR] + [anywhere] * len(pieces),...  6.04 us
  transfers between devices with their start and end apart: 30, of which 11 were waited for; matrix products, arithmetic and copies ran while one was open for 2% of the time, Pallas kernels for 18%

profile of v3, /device:TPU:0, one launch (start us, length us, event | category | flops | bytes accessed | tf_op | source)
XLA Modules:
  0.0 94.6 jit_solution(13966996789893272697)
XLA Ops:
  0.0 1.4 %copy.13 = bf16[4,4,137,128]{3,2,1,0:T(8,128)(2,1)S(1)} copy(f32[4,4,137,128]{3,1,2,0:T(4,128)} %param.6) | data formatting | bytes 1683456 | tf_op args[0]
  1.4 4.1 %collective-permute-start = (bf16[4,4,48,128]{3,2,1,0:T(8,128)(2,1)S(1)}, bf16[4,4,48,128]{3,2,1,0:T(8,128)(2,1)S(1)}, u32[]{:S(2)}, u32[]{:S(2)}) collective-permute-start(bf16[4,4,48,128]{3,2,1,0:T(8,128)(2,1)S(1)} %slice.15.refs_0_), channel_id=1, source_target_pairs={{0,2},{1,3},{2,0},{3,1},{4,6},{5,7},{6,4},{7,5},{8,10},{9,11},{10,... | collective-permute-start | bytes 589832 | tf_op jit(solution)/shard_map/ppermute | solution.py:198
  5.5 9.1 %collective-permute-done.refs_2_ = bf16[4,4,48,128]{3,2,1,0:T(8,128)(2,1)S(1)} collective-permute-done((bf16[4,4,48,128]{3,2,1,0:T(8,128)(2,1)S(1)}, bf16[4,4,48,128]{3,2,1,0:T(8,128)(2,1)S(1)}, u32[]{:S(2)}, u32[]{:S(2)}) %collective-permute-start) | collective-permute-done | bytes 196640 | tf_op jit(solution)/shard_map/ppermute | solution.py:198
  14.6 4.1 %collective-permute-start.8 = (bf16[4,4,48,128]{3,2,1,0:T(8,128)(2,1)S(1)}, bf16[4,4,48,128]{3,2,1,0:T(8,128)(2,1)S(1)}, u32[]{:S(2)}, u32[]{:S(2)}) collective-permute-start(bf16[4,4,48,128]{3,2,1,0:T(8,128)(2,1)S(1)} %slice.15.refs_0_), channel_id=1, source_target_pairs={{0,1},{1,0},{2,3},{3,2},{4,5},{5,4},{6,7},{7,6},{8,9},{9,8},{10,11... | collective-permute-start | bytes 589832 | tf_op jit(solution)/shard_map/ppermute | solution.py:198
  18.7 2.0 %collective-permute-start.13 = (bf16[4,4,64,128]{3,2,1,0:T(8,128)(2,1)S(1)}, bf16[4,4,64,128]{3,2,1,0:T(8,128)(2,1)S(1)}, u32[]{:S(2)}, u32[]{:S(2)}) collective-permute-start(bf16[4,4,64,128]{3,2,1,0:T(8,128)(2,1)S(1)} %slice.14.refs_0_), channel_id=1, source_target_pairs={{0,1},{1,0},{2,3},{3,2},{4,5},{5,4},{6,7},{7,6},{8,9},{9,8},{10,11... | collective-permute-start | bytes 786440 | tf_op jit(solution)/shard_map/ppermute | solution.py:198
  20.7 8.0 %collective-permute-done.1.refs_2_ = bf16[4,4,64,128]{3,2,1,0:T(8,128)(2,1)S(1)} collective-permute-done((bf16[4,4,64,128]{3,2,1,0:T(8,128)(2,1)S(1)}, bf16[4,4,64,128]{3,2,1,0:T(8,128)(2,1)S(1)}, u32[]{:S(2)}, u32[]{:S(2)}) %collective-permute-start.1) | collective-permute-done | bytes 262176 | tf_op jit(solution)/shard_map/ppermute | solution.py:198
  28.8 3.7 %collective-permute-done.9.refs_3_ = bf16[4,4,48,128]{3,2,1,0:T(8,128)(2,1)S(1)} collective-permute-done((bf16[4,4,48,128]{3,2,1,0:T(8,128)(2,1)S(1)}, bf16[4,4,48,128]{3,2,1,0:T(8,128)(2,1)S(1)}, u32[]{:S(2)}, u32[]{:S(2)}) %collective-permute-start.9) | collective-permute-done | bytes 196640 | tf_op jit(solution)/shard_map/ppermute | solution.py:198
  32.5 2.4 %shard_map.65 = (bf16[6,4,48,128]{3,2,1,0:T(8,128)(2,1)S(1)}, bf16[6,4,48,128]{3,2,1,0:T(8,128)(2,1)S(1)}, bf16[6,4,48,128]{3,2,1,0:T(8,128)(2,1)S(1)}, bf16[6,4,48,128]{3,2,1,0:T(8,128)(2,1)S(1)}) custom-call(s32[4]{0:T(128)S(1)} %pad_add_fusion.where_ref, bf16[4,4,48,128]{3,2,1,0:T(8,128)(2,1)S(1)} %slice.15.refs_0_, ...), custom_call_target="tpu_custom_call" | custom-call | bytes 3000000 | tf_op jit(solution)/shard_map/pallas_call | solution.py:229
  35.0 1.3 %collective-permute-start.10 = (bf16[6,4,48,128]{3,2,1,0:T(8,128)(2,1)S(1)}, bf16[6,4,48,128]{3,2,1,0:T(8,128)(2,1)S(1)}, u32[]{:S(2)}, u32[]{:S(2)}) collective-permute-start(bf16[6,4,48,128]{3,2,1,0:T(8,128)(2,1)S(1)} %get-tuple-element.39), channel_id=1, source_target_pairs={{0,8},{4,12},{8,0},{12,4},{16,24},{20,28},{24,16},{28,20},{1,9},{5... | collective-permute-start | bytes 884744 | tf_op jit(solution)/shard_map/ppermute | solution.py:198
  36.3 1.5 %collective-permute-start.11 = (bf16[6,4,48,128]{3,2,1,0:T(8,128)(2,1)S(1)}, bf16[6,4,48,128]{3,2,1,0:T(8,128)(2,1)S(1)}, u32[]{:S(2)}, u32[]{:S(2)}) collective-permute-start(bf16[6,4,48,128]{3,2,1,0:T(8,128)(2,1)S(1)} %get-tuple-element.40), channel_id=1, source_target_pairs={{0,16},{4,20},{8,24},{12,28},{16,0},{20,4},{24,8},{28,12},{1,17},{... | collective-permute-start | bytes 884744 | tf_op jit(solution)/shard_map/ppermute | solution.py:198
  37.8 0.7 collective-permute-start.12
  38.6 1.8 %collective-permute-start.3 = (bf16[4,4,32,128]{3,2,1,0:T(8,128)(2,1)S(1)}, bf16[4,4,32,128]{3,2,1,0:T(8,128)(2,1)S(1)}, u32[]{:S(2)}, u32[]{:S(2)}) collective-permute-start(bf16[4,4,32,128]{3,2,1,0:T(8,128)(2,1)S(1)} %pad_slice_fusion.refs_0_), channel_id=1, source_target_pairs={{0,2},{1,3},{2,0},{3,1},{4,6},{5,7},{6,4},{7,5},{8,10},{9,11},{10,... | collective-permute-start | bytes 393224 | tf_op jit(solution)/shard_map/ppermute | solution.py:198
  40.4 5.2 %collective-permute-done.14.refs_3_ = bf16[4,4,64,128]{3,2,1,0:T(8,128)(2,1)S(1)} collective-permute-done((bf16[4,4,64,128]{3,2,1,0:T(8,128)(2,1)S(1)}, bf16[4,4,64,128]{3,2,1,0:T(8,128)(2,1)S(1)}, u32[]{:S(2)}, u32[]{:S(2)}) %collective-permute-start.14) | collective-permute-done | bytes 262176 | tf_op jit(solution)/shard_map/ppermute | solution.py:198
  45.6 1.7 %shard_map.66 = (bf16[6,4,64,128]{3,2,1,0:T(8,128)(2,1)S(1)}, bf16[6,4,64,128]{3,2,1,0:T(8,128)(2,1)S(1)}, bf16[6,4,64,128]{3,2,1,0:T(8,128)(2,1)S(1)}, bf16[6,4,64,128]{3,2,1,0:T(8,128)(2,1)S(1)}) custom-call(s32[4]{0:T(128)S(1)} %pad_add_fusion.where_ref, bf16[4,4,64,128]{3,2,1,0:T(8,128)(2,1)S(1)} %slice.14.refs_0_, ...), custom_call_target="tpu_custom_call" | custom-call | bytes 3000000 | tf_op jit(solution)/shard_map/pallas_call | solution.py:229
  47.2 1.4 %collective-permute-start.19 = (bf16[6,4,64,128]{3,2,1,0:T(8,128)(2,1)S(1)}, bf16[6,4,64,128]{3,2,1,0:T(8,128)(2,1)S(1)}, u32[]{:S(2)}, u32[]{:S(2)}) collective-permute-start(bf16[6,4,64,128]{3,2,1,0:T(8,128)(2,1)S(1)} %get-tuple-element.43), channel_id=1, source_target_pairs={{0,8},{4,12},{8,0},{12,4},{16,24},{20,28},{24,16},{28,20},{1,9},{5... | collective-permute-start | bytes 1179656 | tf_op jit(solution)/shard_map/ppermute | solution.py:198
  48.6 1.5 %collective-permute-start.20 = (bf16[6,4,64,128]{3,2,1,0:T(8,128)(2,1)S(1)}, bf16[6,4,64,128]{3,2,1,0:T(8,128)(2,1)S(1)}, u32[]{:S(2)}, u32[]{:S(2)}) collective-permute-start(bf16[6,4,64,128]{3,2,1,0:T(8,128)(2,1)S(1)} %get-tuple-element.44), channel_id=1, source_target_pairs={{0,16},{4,20},{8,24},{12,28},{16,0},{20,4},{24,8},{28,12},{1,17},{... | collective-permute-start | bytes 1179656 | tf_op jit(solution)/shard_map/ppermute | solution.py:198
  50.8 2.0 %collective-permute-start.4 = (bf16[4,4,32,128]{3,2,1,0:T(8,128)(2,1)S(1)}, bf16[4,4,32,128]{3,2,1,0:T(8,128)(2,1)S(1)}, u32[]{:S(2)}, u32[]{:S(2)}) collective-permute-start(bf16[4,4,32,128]{3,2,1,0:T(8,128)(2,1)S(1)} %collective-permute-done.3.refs_2_), channel_id=1, source_target_pairs={{0,1},{1,0},{2,3},{3,2},{4,5},{5,4},{6,7},{7,6},{8,9},{9,8},{10,11... | collective-permute-start | bytes 393224 | tf_op jit(solution)/shard_map/ppermute | solution.py:198
  52.8 2.9 %collective-permute-done.2.refs_1_ = bf16[4,4,32,128]{3,2,1,0:T(8,128)(2,1)S(1)} collective-permute-done((bf16[4,4,32,128]{3,2,1,0:T(8,128)(2,1)S(1)}, bf16[4,4,32,128]{3,2,1,0:T(8,128)(2,1)S(1)}, u32[]{:S(2)}, u32[]{:S(2)}) %collective-permute-start.2) | collective-permute-done | bytes 131104 | tf_op jit(solution)/shard_map/ppermute | solution.py:198
  55.8 1.4 %collective-permute-done.4.refs_3_ = bf16[4,4,32,128]{3,2,1,0:T(8,128)(2,1)S(1)} collective-permute-done((bf16[4,4,32,128]{3,2,1,0:T(8,128)(2,1)S(1)}, bf16[4,4,32,128]{3,2,1,0:T(8,128)(2,1)S(1)}, u32[]{:S(2)}, u32[]{:S(2)}) %collective-permute-start.4) | collective-permute-done | bytes 131104 | tf_op jit(solution)/shard_map/ppermute | solution.py:198
  57.2 2.2 %collective-permute-done.19.refs_1_ = bf16[6,4,64,128]{3,2,1,0:T(8,128)(2,1)S(1)} collective-permute-done((bf16[6,4,64,128]{3,2,1,0:T(8,128)(2,1)S(1)}, bf16[6,4,64,128]{3,2,1,0:T(8,128)(2,1)S(1)}, u32[]{:S(2)}, u32[]{:S(2)}) %collective-permute-start.19) | collective-permute-done | bytes 393248 | tf_op jit(solution)/shard_map/ppermute | solution.py:198
  60.1 1.9 %shard_map.64 = (bf16[6,4,32,128]{3,2,1,0:T(8,128)(2,1)S(1)}, bf16[6,4,32,128]{3,2,1,0:T(8,128)(2,1)S(1)}, bf16[6,4,32,128]{3,2,1,0:T(8,128)(2,1)S(1)}, bf16[6,4,32,128]{3,2,1,0:T(8,128)(2,1)S(1)}) custom-call(s32[4]{0:T(128)S(1)} %pad_add_fusion.where_ref, bf16[4,4,32,128]{3,2,1,0:T(8,128)(2,1)S(1)} %pad_slice_fusion.refs_0_, ...), custom_call_target="tpu_custom_call" | custom-call | bytes 3000000 | tf_op jit(solution)/shard_map/pallas_call | solution.py:229
  64.7 1.9 %collective-permute-done.20.refs_2_ = bf16[6,4,64,128]{3,2,1,0:T(8,128)(2,1)S(1)} collective-permute-done((bf16[6,4,64,128]{3,2,1,0:T(8,128)(2,1)S(1)}, bf16[6,4,64,128]{3,2,1,0:T(8,128)(2,1)S(1)}, u32[]{:S(2)}, u32[]{:S(2)}) %collective-permute-start.20) | collective-permute-done | bytes 393248 | tf_op jit(solution)/shard_map/ppermute | solution.py:198
  67.1 0.7 copy-done.9
  69.1 0.7 copy-done.13
  70.0 1.3 %copy.8.vertical_ref = bf16[8,137,137]{2,1,0:T(8,128)(2,1)S(1)} copy(bf16[8,137,137]{2,0,1:T(8,128)(2,1)} %param.10) | data formatting | bytes 600608 | tf_op args[4]
  71.3 0.8 shard_map.67
  72.1 1.3 %collective-permute-start.5 = (bf16[6,4,32,128]{3,2,1,0:T(8,128)(2,1)S(1)}, bf16[6,4,32,128]{3,2,1,0:T(8,128)(2,1)S(1)}, u32[]{:S(2)}, u32[]{:S(2)}) collective-permute-start(bf16[6,4,32,128]{3,2,1,0:T(8,128)(2,1)S(1)} %copy-done.22), channel_id=1, source_target_pairs={{0,8},{4,12},{8,0},{12,4},{16,24},{20,28},{24,16},{28,20},{1,9},{5... | collective-permute-start | bytes 589832 | tf_op jit(solution)/shard_map/ppermute | solution.py:198
  73.4 0.8 collective-permute-start.6
  74.3 1.4 %collective-permute-start.7 = (bf16[6,4,32,128]{3,2,1,0:T(8,128)(2,1)S(1)}, bf16[6,4,32,128]{3,2,1,0:T(8,128)(2,1)S(1)}, u32[]{:S(2)}, u32[]{:S(2)}) collective-permute-start(bf16[6,4,32,128]{3,2,1,0:T(8,128)(2,1)S(1)} %copy-done.18), channel_id=1, source_target_pairs={{0,24},{4,28},{8,16},{12,20},{16,8},{20,12},{24,0},{28,4},{1,25},{... | collective-permute-start | bytes 589832 | tf_op jit(solution)/shard_map/ppermute | solution.py:198
  75.7 4.5 %shard_map.68.refs_10_ = bf16[2,2,16,48,256]{4,3,2,1,0:T(8,128)(2,1)S(1)} custom-call(s32[4]{0:T(128)S(1)} %pad_add_fusion.where_ref, s32[8]{0:T(128)S(1)} %copy-done.2, f32[8,3]{1,0:T(8,128)S(1)} %copy.11.weight_ref, bf16[6,4,48,128]{3,2,1,0:T(8,128)(2,1)S(1)} %copy-done.4, bf16[6,4,48,128]{3,2,1,0:T(8,128)(2,1)S(1)} %copy-done.6, ...), custom_call_target="tpu_custom_call" | custom-call | flops 2000000000 | bytes 8000000 | tf_op jit(solution)/shard_map/pallas_call | solution.py:161
  80.3 5.4 %shard_map.69.refs_11_ = bf16[2,2,16,64,256]{4,3,2,1,0:T(8,128)(2,1)S(1)} custom-call(s32[4]{0:T(128)S(1)} %pad_add_fusion.where_ref, s32[8]{0:T(128)S(1)} %copy-done.2, f32[8,3]{1,0:T(8,128)S(1)} %copy.11.weight_ref, bf16[6,4,64,128]{3,2,1,0:T(8,128)(2,1)S(1)} %get-tuple-element.51.refs_0_, bf16[6,4,64,128]{3,2,1,0:T(8,128)(2,1)S(1)} %collective-permute-done.19.refs_1_, ...), custom_call_target="tpu_custom_call" | custom-call | flops 2000000000 | bytes 8000000 | tf_op jit(solution)/shard_map/pallas_call | solution.py:161
  88.1 6.5 %shard_map.70 = bf16[2,2,137,32,128]{4,3,2,1,0:T(8,128)(2,1)} custom-call(s32[4]{0:T(128)S(1)} %pad_add_fusion.where_ref, s32[8]{0:T(128)S(1)} %copy-done.2, f32[8,3]{1,0:T(8,128)S(1)} %copy.11.weight_ref, bf16[6,4,32,128]{3,2,1,0:T(8,128)(2,1)S(1)} %copy-done.16, bf16[6,4,32,128]{3,2,1,0:T(8,128)(2,1)S(1)} %collective-permute-done.5.refs_1_, ...), custom_call_target="tpu_custom_call" | custom-call | flops 4000000000 | bytes 12000000 | tf_op jit(solution)/shard_map/pallas_call | solution.py:179
  (90 shorter events, 8.5 us)
Async XLA Ops:
  1.4 13.2 %collective-permute-start = (bf16[4,4,48,128]{3,2,1,0:T(8,128)(2,1)S(1)}, bf16[4,4,48,128]{3,2,1,0:T(8,128)(2,1)S(1)}, u32[]{:S(2)}, u32[]{:S(2)}) collective-permute-start(bf16[4,4,48,128]{3,2,1,0:T(8,128)(2,1)S(1)} %slice.15.refs_0_), channel_id=1, source_target_pairs={{0,2},{1,3},{2,0},{3,1},{4,6},{5,7},{6,4},{7,5},{8,10},{9,11},{10,... | collective-permute-start | bytes 589832 | tf_op jit(solution)/shard_map/ppermute | solution.py:198
  5.5 64.3 %copy-start.23 = (f32[8,3]{0,1:T(4,128)S(1)}, f32[8,3]{0,1:T(4,128)}, u32[]{:S(2)}) copy-start(f32[8,3]{0,1:T(4,128)} %param.7) | copy-start | bytes 292
  14.6 14.1 %collective-permute-start.1 = (bf16[4,4,64,128]{3,2,1,0:T(8,128)(2,1)S(1)}, bf16[4,4,64,128]{3,2,1,0:T(8,128)(2,1)S(1)}, u32[]{:S(2)}, u32[]{:S(2)}) collective-permute-start(bf16[4,4,64,128]{3,2,1,0:T(8,128)(2,1)S(1)} %slice.14.refs_0_), channel_id=1, source_target_pairs={{0,2},{1,3},{2,0},{3,1},{4,6},{5,7},{6,4},{7,5},{8,10},{9,11},{10,... | collective-permute-start | bytes 786440 | tf_op jit(solution)/shard_map/ppermute | solution.py:198
  14.6 14.2 %collective-permute-start.8 = (bf16[4,4,48,128]{3,2,1,0:T(8,128)(2,1)S(1)}, bf16[4,4,48,128]{3,2,1,0:T(8,128)(2,1)S(1)}, u32[]{:S(2)}, u32[]{:S(2)}) collective-permute-start(bf16[4,4,48,128]{3,2,1,0:T(8,128)(2,1)S(1)} %slice.15.refs_0_), channel_id=1, source_target_pairs={{0,1},{1,0},{2,3},{3,2},{4,5},{5,4},{6,7},{7,6},{8,9},{9,8},{10,11... | collective-permute-start | bytes 589832 | tf_op jit(solution)/shard_map/ppermute | solution.py:198
  18.7 13.8 %collective-permute-start.9 = (bf16[4,4,48,128]{3,2,1,0:T(8,128)(2,1)S(1)}, bf16[4,4,48,128]{3,2,1,0:T(8,128)(2,1)S(1)}, u32[]{:S(2)}, u32[]{:S(2)}) collective-permute-start(bf16[4,4,48,128]{3,2,1,0:T(8,128)(2,1)S(1)} %collective-permute-done.refs_2_), channel_id=1, source_target_pairs={{0,1},{1,0},{2,3},{3,2},{4,5},{5,4},{6,7},{7,6},{8,9},{9,8},{10,11... | collective-permute-start | bytes 589832 | tf_op jit(solution)/shard_map/ppermute | solution.py:198
  18.7 19.8 %collective-permute-start.13 = (bf16[4,4,64,128]{3,2,1,0:T(8,128)(2,1)S(1)}, bf16[4,4,64,128]{3,2,1,0:T(8,128)(2,1)S(1)}, u32[]{:S(2)}, u32[]{:S(2)}) collective-permute-start(bf16[4,4,64,128]{3,2,1,0:T(8,128)(2,1)S(1)} %slice.14.refs_0_), channel_id=1, source_target_pairs={{0,1},{1,0},{2,3},{3,2},{4,5},{5,4},{6,7},{7,6},{8,9},{9,8},{10,11... | collective-permute-start | bytes 786440 | tf_op jit(solution)/shard_map/ppermute | solution.py:198
  28.7 16.8 %collective-permute-start.14 = (bf16[4,4,64,128]{3,2,1,0:T(8,128)(2,1)S(1)}, bf16[4,4,64,128]{3,2,1,0:T(8,128)(2,1)S(1)}, u32[]{:S(2)}, u32[]{:S(2)}) collective-permute-start(bf16[4,4,64,128]{3,2,1,0:T(8,128)(2,1)S(1)} %collective-permute-done.1.refs_2_), channel_id=1, source_target_pairs={{0,1},{1,0},{2,3},{3,2},{4,5},{5,4},{6,7},{7,6},{8,9},{9,8},{10,11... | collective-permute-start | bytes 786440 | tf_op jit(solution)/shard_map/ppermute | solution.py:198
  35.0 34.1 %copy-start.3 = (bf16[6,4,48,128]{3,2,1,0:T(8,128)(2,1)}, bf16[6,4,48,128]{3,2,1,0:T(8,128)(2,1)S(1)}, u32[]{:S(2)}) copy-start(bf16[6,4,48,128]{3,2,1,0:T(8,128)(2,1)S(1)} %get-tuple-element.46.refs_0_) | copy-start | bytes 884740
  35.0 15.2 %collective-permute-start.10 = (bf16[6,4,48,128]{3,2,1,0:T(8,128)(2,1)S(1)}, bf16[6,4,48,128]{3,2,1,0:T(8,128)(2,1)S(1)}, u32[]{:S(2)}, u32[]{:S(2)}) collective-permute-start(bf16[6,4,48,128]{3,2,1,0:T(8,128)(2,1)S(1)} %get-tuple-element.39), channel_id=1, source_target_pairs={{0,8},{4,12},{8,0},{12,4},{16,24},{20,28},{24,16},{28,20},{1,9},{5... | collective-permute-start | bytes 884744 | tf_op jit(solution)/shard_map/ppermute | solution.py:198
  36.3 14.5 %collective-permute-start.11 = (bf16[6,4,48,128]{3,2,1,0:T(8,128)(2,1)S(1)}, bf16[6,4,48,128]{3,2,1,0:T(8,128)(2,1)S(1)}, u32[]{:S(2)}, u32[]{:S(2)}) collective-permute-start(bf16[6,4,48,128]{3,2,1,0:T(8,128)(2,1)S(1)} %get-tuple-element.40), channel_id=1, source_target_pairs={{0,16},{4,20},{8,24},{12,28},{16,0},{20,4},{24,8},{28,12},{1,17},{... | collective-permute-start | bytes 884744 | tf_op jit(solution)/shard_map/ppermute | solution.py:198
  37.8 13.0 %collective-permute-start.12 = (bf16[6,4,48,128]{3,2,1,0:T(8,128)(2,1)S(1)}, bf16[6,4,48,128]{3,2,1,0:T(8,128)(2,1)}, u32[]{:S(2)}, u32[]{:S(2)}) collective-permute-start(bf16[6,4,48,128]{3,2,1,0:T(8,128)(2,1)S(1)} %get-tuple-element.41), channel_id=1, source_target_pairs={{0,24},{4,28},{8,16},{12,20},{16,8},{20,12},{24,0},{28,4},{1,25},{... | collective-permute-start | bytes 884744 | tf_op jit(solution)/shard_map/ppermute | solution.py:198
  38.6 10.0 %collective-permute-start.3 = (bf16[4,4,32,128]{3,2,1,0:T(8,128)(2,1)S(1)}, bf16[4,4,32,128]{3,2,1,0:T(8,128)(2,1)S(1)}, u32[]{:S(2)}, u32[]{:S(2)}) collective-permute-start(bf16[4,4,32,128]{3,2,1,0:T(8,128)(2,1)S(1)} %pad_slice_fusion.refs_0_), channel_id=1, source_target_pairs={{0,2},{1,3},{2,0},{3,1},{4,6},{5,7},{6,4},{7,5},{8,10},{9,11},{10,... | collective-permute-start | bytes 393224 | tf_op jit(solution)/shard_map/ppermute | solution.py:198
  47.2 12.1 %collective-permute-start.19 = (bf16[6,4,64,128]{3,2,1,0:T(8,128)(2,1)S(1)}, bf16[6,4,64,128]{3,2,1,0:T(8,128)(2,1)S(1)}, u32[]{:S(2)}, u32[]{:S(2)}) collective-permute-start(bf16[6,4,64,128]{3,2,1,0:T(8,128)(2,1)S(1)} %get-tuple-element.43), channel_id=1, source_target_pairs={{0,8},{4,12},{8,0},{12,4},{16,24},{20,28},{24,16},{28,20},{1,9},{5... | collective-permute-start | bytes 1179656 | tf_op jit(solution)/shard_map/ppermute | solution.py:198
  48.6 17.9 %collective-permute-start.20 = (bf16[6,4,64,128]{3,2,1,0:T(8,128)(2,1)S(1)}, bf16[6,4,64,128]{3,2,1,0:T(8,128)(2,1)S(1)}, u32[]{:S(2)}, u32[]{:S(2)}) collective-permute-start(bf16[6,4,64,128]{3,2,1,0:T(8,128)(2,1)S(1)} %get-tuple-element.44), channel_id=1, source_target_pairs={{0,16},{4,20},{8,24},{12,28},{16,0},{20,4},{24,8},{28,12},{1,17},{... | collective-permute-start | bytes 1179656 | tf_op jit(solution)/shard_map/ppermute | solution.py:198
  50.2 16.4 %collective-permute-start.21 = (bf16[6,4,64,128]{3,2,1,0:T(8,128)(2,1)S(1)}, bf16[6,4,64,128]{3,2,1,0:T(8,128)(2,1)S(1)}, u32[]{:S(2)}, u32[]{:S(2)}) collective-permute-start(bf16[6,4,64,128]{3,2,1,0:T(8,128)(2,1)S(1)} %get-tuple-element.45), channel_id=1, source_target_pairs={{0,24},{4,28},{8,16},{12,20},{16,8},{20,12},{24,0},{28,4},{1,25},{... | collective-permute-start | bytes 1179656 | tf_op jit(solution)/shard_map/ppermute | solution.py:198
  50.8 5.0 %collective-permute-start.2 = (bf16[4,4,32,128]{3,2,1,0:T(8,128)(2,1)S(1)}, bf16[4,4,32,128]{3,2,1,0:T(8,128)(2,1)S(1)}, u32[]{:S(2)}, u32[]{:S(2)}) collective-permute-start(bf16[4,4,32,128]{3,2,1,0:T(8,128)(2,1)S(1)} %pad_slice_fusion.refs_0_), channel_id=1, source_target_pairs={{0,1},{1,0},{2,3},{3,2},{4,5},{5,4},{6,7},{7,6},{8,9},{9,8},{10,11... | collective-permute-start | bytes 393224 | tf_op jit(solution)/shard_map/ppermute | solution.py:198
  50.8 6.4 %collective-permute-start.4 = (bf16[4,4,32,128]{3,2,1,0:T(8,128)(2,1)S(1)}, bf16[4,4,32,128]{3,2,1,0:T(8,128)(2,1)S(1)}, u32[]{:S(2)}, u32[]{:S(2)}) collective-permute-start(bf16[4,4,32,128]{3,2,1,0:T(8,128)(2,1)S(1)} %collective-permute-done.3.refs_2_), channel_id=1, source_target_pairs={{0,1},{1,0},{2,3},{3,2},{4,5},{5,4},{6,7},{7,6},{8,9},{9,8},{10,11... | collective-permute-start | bytes 393224 | tf_op jit(solution)/shard_map/ppermute | solution.py:198
  55.8 11.3 %collective-permute-start.15 = (bf16[6,4,48,128]{3,2,1,0:T(8,128)(2,1)S(1)}, bf16[6,4,48,128]{3,2,1,0:T(8,128)(2,1)S(1)}, u32[]{:S(2)}, u32[]{:S(2)}) collective-permute-start(bf16[6,4,48,128]{3,2,1,0:T(8,128)(2,1)S(1)} %get-tuple-element.46.refs_0_), channel_id=1, source_target_pairs={{0,4},{4,0},{8,12},{12,8},{16,20},{20,16},{24,28},{28,24},{1,5},{5... | collective-permute-start | bytes 884744 | tf_op jit(solution)/shard_map/ppermute | solution.py:198
  57.2 10.7 %collective-permute-start.16 = (bf16[6,4,48,128]{3,2,1,0:T(8,128)(2,1)S(1)}, bf16[6,4,48,128]{3,2,1,0:T(8,128)(2,1)S(1)}, u32[]{:S(2)}, u32[]{:S(2)}) collective-permute-start(bf16[6,4,48,128]{3,2,1,0:T(8,128)(2,1)S(1)} %collective-permute-done.10.refs_1_), channel_id=1, source_target_pairs={{0,4},{4,0},{8,12},{12,8},{16,20},{20,16},{24,28},{28,24},{1,5},{5... | collective-permute-start | bytes 884744 | tf_op jit(solution)/shard_map/ppermute | solution.py:198
  59.4 9.7 %collective-permute-start.17 = (bf16[6,4,48,128]{3,2,1,0:T(8,128)(2,1)S(1)}, bf16[6,4,48,128]{3,2,1,0:T(8,128)(2,1)S(1)}, u32[]{:S(2)}, u32[]{:S(2)}) collective-permute-start(bf16[6,4,48,128]{3,2,1,0:T(8,128)(2,1)S(1)} %collective-permute-done.11.refs_2_), channel_id=1, source_target_pairs={{0,4},{4,0},{8,12},{12,8},{16,20},{20,16},{24,28},{28,24},{1,5},{5... | collective-permute-start | bytes 884744 | tf_op jit(solution)/shard_map/ppermute | solution.py:198
  66.6 6.8 %collective-permute-start.22 = (bf16[6,4,64,128]{3,2,1,0:T(8,128)(2,1)S(1)}, bf16[6,4,64,128]{3,2,1,0:T(8,128)(2,1)S(1)}, u32[]{:S(2)}, u32[]{:S(2)}) collective-permute-start(bf16[6,4,64,128]{3,2,1,0:T(8,128)(2,1)S(1)} %get-tuple-element.51.refs_0_), channel_id=1, source_target_pairs={{0,4},{4,0},{8,12},{12,8},{16,20},{20,16},{24,28},{28,24},{1,5},{5... | collective-permute-start | bytes 1179656 | tf_op jit(solution)/shard_map/ppermute | solution.py:198
  66.6 7.7 %collective-permute-start.23 = (bf16[6,4,64,128]{3,2,1,0:T(8,128)(2,1)S(1)}, bf16[6,4,64,128]{3,2,1,0:T(8,128)(2,1)}, u32[]{:S(2)}, u32[]{:S(2)}) collective-permute-start(bf16[6,4,64,128]{3,2,1,0:T(8,128)(2,1)S(1)} %collective-permute-done.19.refs_1_), channel_id=1, source_target_pairs={{0,4},{4,0},{8,12},{12,8},{16,20},{20,16},{24,28},{28,24},{1,5},{5... | collective-permute-start | bytes 1179656 | tf_op jit(solution)/shard_map/ppermute | solution.py:198
  67.8 4.3 %collective-permute-start.18 = (bf16[6,4,48,128]{3,2,1,0:T(8,128)(2,1)}, bf16[6,4,48,128]{3,2,1,0:T(8,128)(2,1)}, u32[]{:S(2)}, u32[]{:S(2)}) collective-permute-start(bf16[6,4,48,128]{3,2,1,0:T(8,128)(2,1)} %collective-permute-done.12.refs_3_), channel_id=1, source_target_pairs={{0,4},{4,0},{8,12},{12,8},{16,20},{20,16},{24,28},{28,24},{1,5},{5... | collective-permute-start | bytes 884744 | tf_op jit(solution)/shard_map/ppermute | solution.py:198
  68.6 11.7 %collective-permute-start.24 = (bf16[6,4,64,128]{3,2,1,0:T(8,128)(2,1)S(1)}, bf16[6,4,64,128]{3,2,1,0:T(8,128)(2,1)}, u32[]{:S(2)}, u32[]{:S(2)}) collective-permute-start(bf16[6,4,64,128]{3,2,1,0:T(8,128)(2,1)S(1)} %collective-permute-done.20.refs_2_), channel_id=1, source_target_pairs={{0,4},{4,0},{8,12},{12,8},{16,20},{20,16},{24,28},{28,24},{1,5},{5... | collective-permute-start | bytes 1179656 | tf_op jit(solution)/shard_map/ppermute | solution.py:198
  69.8 10.5 %collective-permute-start.25 = (bf16[6,4,64,128]{3,2,1,0:T(8,128)(2,1)S(1)}, bf16[6,4,64,128]{3,2,1,0:T(8,128)(2,1)}, u32[]{:S(2)}, u32[]{:S(2)}) collective-permute-start(bf16[6,4,64,128]{3,2,1,0:T(8,128)(2,1)S(1)} %collective-permute-done.21.refs_3_), channel_id=1, source_target_pairs={{0,4},{4,0},{8,12},{12,8},{16,20},{20,16},{24,28},{28,24},{1,5},{5... | collective-permute-start | bytes 1179656 | tf_op jit(solution)/shard_map/ppermute | solution.py:198
  72.1 13.7 %collective-permute-start.5 = (bf16[6,4,32,128]{3,2,1,0:T(8,128)(2,1)S(1)}, bf16[6,4,32,128]{3,2,1,0:T(8,128)(2,1)S(1)}, u32[]{:S(2)}, u32[]{:S(2)}) collective-permute-start(bf16[6,4,32,128]{3,2,1,0:T(8,128)(2,1)S(1)} %copy-done.22), channel_id=1, source_target_pairs={{0,8},{4,12},{8,0},{12,4},{16,24},{20,28},{24,16},{28,20},{1,9},{5... | collective-permute-start | bytes 589832 | tf_op jit(solution)/shard_map/ppermute | solution.py:198
  73.4 12.4 %collective-permute-start.6 = (bf16[6,4,32,128]{3,2,1,0:T(8,128)(2,1)S(1)}, bf16[6,4,32,128]{3,2,1,0:T(8,128)(2,1)S(1)}, u32[]{:S(2)}, u32[]{:S(2)}) collective-permute-start(bf16[6,4,32,128]{3,2,1,0:T(8,128)(2,1)S(1)} %copy-done.20), channel_id=1, source_target_pairs={{0,16},{4,20},{8,24},{12,28},{16,0},{20,4},{24,8},{28,12},{1,17},{... | collective-permute-start | bytes 589832 | tf_op jit(solution)/shard_map/ppermute | solution.py:198
  74.3 11.6 %collective-permute-start.7 = (bf16[6,4,32,128]{3,2,1,0:T(8,128)(2,1)S(1)}, bf16[6,4,32,128]{3,2,1,0:T(8,128)(2,1)S(1)}, u32[]{:S(2)}, u32[]{:S(2)}) collective-permute-start(bf16[6,4,32,128]{3,2,1,0:T(8,128)(2,1)S(1)} %copy-done.18), channel_id=1, source_target_pairs={{0,24},{4,28},{8,16},{12,20},{16,8},{20,12},{24,0},{28,4},{1,25},{... | collective-permute-start | bytes 589832 | tf_op jit(solution)/shard_map/ppermute | solution.py:198
  80.3 6.6 %collective-permute-start.26 = (bf16[6,4,32,128]{3,2,1,0:T(8,128)(2,1)S(1)}, bf16[6,4,32,128]{3,2,1,0:T(8,128)(2,1)S(1)}, u32[]{:S(2)}, u32[]{:S(2)}) collective-permute-start(bf16[6,4,32,128]{3,2,1,0:T(8,128)(2,1)S(1)} %copy-done.16), channel_id=1, source_target_pairs={{0,4},{4,0},{8,12},{12,8},{16,20},{20,16},{24,28},{28,24},{1,5},{5... | collective-permute-start | bytes 589832 | tf_op jit(solution)/shard_map/ppermute | solution.py:198
  85.8 1.6 %collective-permute-start.27 = (bf16[6,4,32,128]{3,2,1,0:T(8,128)(2,1)S(1)}, bf16[6,4,32,128]{3,2,1,0:T(8,128)(2,1)S(1)}, u32[]{:S(2)}, u32[]{:S(2)}) collective-permute-start(bf16[6,4,32,128]{3,2,1,0:T(8,128)(2,1)S(1)} %collective-permute-done.5.refs_1_), channel_id=1, source_target_pairs={{0,4},{4,0},{8,12},{12,8},{16,20},{20,16},{24,28},{28,24},{1,5},{5... | collective-permute-start | bytes 589832 | tf_op jit(solution)/shard_map/ppermute | solution.py:198
  86.3 1.4 %collective-permute-start.28 = (bf16[6,4,32,128]{3,2,1,0:T(8,128)(2,1)S(1)}, bf16[6,4,32,128]{3,2,1,0:T(8,128)(2,1)S(1)}, u32[]{:S(2)}, u32[]{:S(2)}) collective-permute-start(bf16[6,4,32,128]{3,2,1,0:T(8,128)(2,1)S(1)} %collective-permute-done.6.refs_2_), channel_id=1, source_target_pairs={{0,4},{4,0},{8,12},{12,8},{16,20},{20,16},{24,28},{28,24},{1,5},{5... | collective-permute-start | bytes 589832 | tf_op jit(solution)/shard_map/ppermute | solution.py:198
  86.4 1.6 %collective-permute-start.29 = (bf16[6,4,32,128]{3,2,1,0:T(8,128)(2,1)S(1)}, bf16[6,4,32,128]{3,2,1,0:T(8,128)(2,1)S(1)}, u32[]{:S(2)}, u32[]{:S(2)}) collective-permute-start(bf16[6,4,32,128]{3,2,1,0:T(8,128)(2,1)S(1)} %collective-permute-done.7.refs_3_), channel_id=1, source_target_pairs={{0,4},{4,0},{8,12},{12,8},{16,20},{20,16},{24,28},{28,24},{1,5},{5... | collective-permute-start | bytes 589832 | tf_op jit(solution)/shard_map/ppermute | solution.py:198
  (22 other events, 174.2 us)

commit v4 on v3

--- a/solution.py
+++ b/solution.py
@@ -9,6 +9,7 @@
 
 REACH = 3
 SUBLANES = 16
+LANES = 128
 SPREAD_GAP = 8
 CUTS = (48, 112)
 
@@ -28,9 +29,13 @@
     return band
 
 
-def table_kernel(where_ref, slot_ref, offset_ref, filter_ref, vertical_ref, filt_out, vert_out):
+def table_kernel(where_ref, slot_ref, offset_ref, filter_ref, vertical_ref, filt_out, vert_out, lines):
     group, _, c, _ = filt_out.shape
-    levels = vertical_ref.shape[1]
+    levels, bands, _ = vertical_ref.shape
+    strips = [(lo, min(LANES, levels - lo)) for lo in range(0, levels, LANES)]
+    for i, (lo, size) in enumerate(strips):
+        strip = vertical_ref[:, :, lo : lo + size].astype(jnp.float32)
+        lines[i, :, :size] = strip.reshape(levels * bands, size)
     filt_out[...] = jnp.zeros_like(filt_out)
     vert_out[...] = jnp.zeros_like(vert_out)
     for g in range(group):
@@ -39,11 +44,13 @@
             n = offset_ref[band, k] + REACH
             for h in range(2):
                 filt_out[g, n + h, :, h * c : (h + 1) * c] = filter_ref[band, k]
-        vert_out[g, :levels, :levels] = vertical_ref[band]
+        for i, (lo, size) in enumerate(strips):
+            strip = lines[i, pl.ds(band, levels, stride=bands), :]
+            vert_out[g, :levels, lo : lo + size] = strip[:, :size].astype(vert_out.dtype)
 
 
 def owned_tables(where, slot_of_band, block_offsets, filters, vertical, group, padded):
-    c = filters.shape[-1]
+    c, levels = filters.shape[-1], vertical.shape[-1]
     vmem = pl.BlockSpec(memory_space=pltpu.VMEM)
     filt, vert = pl.pallas_call(
         table_kernel,
@@ -53,9 +60,10 @@
             jax.ShapeDtypeStruct((group, 2 * REACH + 2, c, 2 * c), filters.dtype),
             jax.ShapeDtypeStruct((group, padded, padded), vertical.dtype),
         ],
+        scratch_shapes=[pltpu.VMEM((pl.cdiv(levels, LANES), vertical.shape[0] * levels, LANES), jnp.float32)],
         compiler_params=PARAMS,
         cost_estimate=pl.CostEstimate(flops=0, bytes_accessed=4_000_000, transcendentals=0),
-    )(where, slot_of_band, block_offsets, filters, vertical)
+    )(where, slot_of_band, block_offsets, filters, vertical.transpose(1, 0, 2))
     return filt.reshape(group, REACH + 1, 2 * c, 2 * c), vert
 
 
@@ -63,9 +71,9 @@
     group = slot_ref.shape[0] // where_ref[3]
     band = band_of(slot_ref, where_ref[1] * group + b)
     row = where_ref[0] * rows + r
-    above = jnp.where(row > 0, weight_ref[band, 0], 0.0)
-    below = jnp.where(row + 1 < row_total, weight_ref[band, 2], 0.0)
-    return above, weight_ref[band, 1], below
+    above = jnp.where(row > 0, weight_ref[0, band], 0.0)
+    below = jnp.where(row + 1 < row_total, weight_ref[2, band], 0.0)
+    return above, weight_ref[1, band], below
 
 
 def fill_window(window, place, weights, r, kept, got):
@@ -267,7 +275,7 @@
 
     place = [lax.axis_index("lon"), lax.axis_index("lat"), jnp.int32(lons), jnp.int32(lats)]
     where = jnp.stack(place).astype(jnp.int32)
-    scalars = (where, slot_of_band, lat_weights)
+    scalars = (where, slot_of_band, lat_weights.T)
     filt, vert = owned_tables(where, slot_of_band, block_offsets, filters, vertical, group, padded)
 
     own = jnp.pad(grad_field.astype(jnp.bfloat16), ((0, 0), (0, 0), (0, extra), (0, 0)))

time: 94.8 us -> 90.2 us (0.951)
  local copies, waits for them, and re-layouts: 8.44 us -> 2.35 us
  waiting for transfers between devices: 35.6 us -> 37.9 us
  Pallas kernels: 23.3 us -> 22.1 us
    unnamed x51 -> x13, local copies, waits for them, and re-layouts: 8.39 us -> 1.39 us
    ppermute x30, waiting for transfers between devices: 35.6 us -> 37.9 us  [swapped(): lax.ppermute(value, axis, [(i, i ^ by) for i in range(lax.axis_size(axis))])]
    pallas_call x2, Pallas kernels: 9.94 us -> 8.65 us  [first_part(): pl.pallas_call(functools.partial(first_kernel, len(kept)), grid=(rows, gr...]
  transfers between devices with their start and end apart: 30 -> 30, of which waited for: 11 -> 13; matrix products, arithmetic and copies ran while one was open for 2% -> 1% of each run, Pallas kernels for 18% -> 17%
where the time goes in v4:
time: 90.2 us; the launch traced here: 90.1 us
  waiting for transfers between devices  37.9 us (42%)
  starting transfers between devices  27.4 us (30%)
  Pallas kernels  22.1 us (25%)
  local copies, waits for them, and re-layouts  2.35 us (3%)
    ppermute x30, waiting for transfers between devices, swapped(): lax.ppermute(value, axis, [(i, i ^ by) for i in range(lax.axis_size(axis))])  37.9 us
    ppermute x30, starting transfers between devices, swapped(): lax.ppermute(value, axis, [(i, i ^ by) for i in range(lax.axis_size(axis))])  27.4 us
    pallas_call x2, Pallas kernels, first_part(): pl.pallas_call(functools.partial(first_kernel, len(kept)), grid=(rows, gr...  8.65 us
    pallas_call x1, Pallas kernels, last_part(): pl.pallas_call(functools.partial(last_kernel, len(kept)), grid=(rows, gro...  6.48 us
    pallas_call x3, Pallas kernels, sorted_rows(): pl.pallas_call(sort_kernel, in_specs=[SCALAR] + [anywhere] * len(pieces),...  6.04 us
  transfers between devices with their start and end apart: 30, of which 13 were waited for; matrix products, arithmetic and copies ran while one was open for 1% of the time, Pallas kernels for 17%

profile of v4, /device:TPU:0, one launch (start us, length us, event | category | flops | bytes accessed | tf_op | source)
XLA Modules:
  0.0 90.1 jit_solution(11360458431072465128)
XLA Ops:
  0.0 1.4 %copy.9 = bf16[4,4,137,128]{3,2,1,0:T(8,128)(2,1)S(1)} copy(f32[4,4,137,128]{3,1,2,0:T(4,128)} %param.6) | data formatting | bytes 1683456 | tf_op args[0]
  1.4 4.1 %collective-permute-start = (bf16[4,4,48,128]{3,2,1,0:T(8,128)(2,1)S(1)}, bf16[4,4,48,128]{3,2,1,0:T(8,128)(2,1)S(1)}, u32[]{:S(2)}, u32[]{:S(2)}) collective-permute-start(bf16[4,4,48,128]{3,2,1,0:T(8,128)(2,1)S(1)} %slice.15.refs_0_), channel_id=1, source_target_pairs={{0,2},{1,3},{2,0},{3,1},{4,6},{5,7},{6,4},{7,5},{8,10},{9,11},{10,... | collective-permute-start | bytes 589832 | tf_op jit(solution)/shard_map/ppermute | solution.py:206
  5.6 9.0 %collective-permute-done.refs_2_ = bf16[4,4,48,128]{3,2,1,0:T(8,128)(2,1)S(1)} collective-permute-done((bf16[4,4,48,128]{3,2,1,0:T(8,128)(2,1)S(1)}, bf16[4,4,48,128]{3,2,1,0:T(8,128)(2,1)S(1)}, u32[]{:S(2)}, u32[]{:S(2)}) %collective-permute-start) | collective-permute-done | bytes 196640 | tf_op jit(solution)/shard_map/ppermute | solution.py:206
  14.6 4.1 %collective-permute-start.8 = (bf16[4,4,48,128]{3,2,1,0:T(8,128)(2,1)S(1)}, bf16[4,4,48,128]{3,2,1,0:T(8,128)(2,1)S(1)}, u32[]{:S(2)}, u32[]{:S(2)}) collective-permute-start(bf16[4,4,48,128]{3,2,1,0:T(8,128)(2,1)S(1)} %slice.15.refs_0_), channel_id=1, source_target_pairs={{0,1},{1,0},{2,3},{3,2},{4,5},{5,4},{6,7},{7,6},{8,9},{9,8},{10,11... | collective-permute-start | bytes 589832 | tf_op jit(solution)/shard_map/ppermute | solution.py:206
  18.7 2.0 %collective-permute-start.13 = (bf16[4,4,64,128]{3,2,1,0:T(8,128)(2,1)S(1)}, bf16[4,4,64,128]{3,2,1,0:T(8,128)(2,1)S(1)}, u32[]{:S(2)}, u32[]{:S(2)}) collective-permute-start(bf16[4,4,64,128]{3,2,1,0:T(8,128)(2,1)S(1)} %slice.14.refs_0_), channel_id=1, source_target_pairs={{0,1},{1,0},{2,3},{3,2},{4,5},{5,4},{6,7},{7,6},{8,9},{9,8},{10,11... | collective-permute-start | bytes 786440 | tf_op jit(solution)/shard_map/ppermute | solution.py:206
  20.7 8.0 %collective-permute-done.1.refs_2_ = bf16[4,4,64,128]{3,2,1,0:T(8,128)(2,1)S(1)} collective-permute-done((bf16[4,4,64,128]{3,2,1,0:T(8,128)(2,1)S(1)}, bf16[4,4,64,128]{3,2,1,0:T(8,128)(2,1)S(1)}, u32[]{:S(2)}, u32[]{:S(2)}) %collective-permute-start.1) | collective-permute-done | bytes 262176 | tf_op jit(solution)/shard_map/ppermute | solution.py:206
  28.8 3.7 %collective-permute-done.9.refs_3_ = bf16[4,4,48,128]{3,2,1,0:T(8,128)(2,1)S(1)} collective-permute-done((bf16[4,4,48,128]{3,2,1,0:T(8,128)(2,1)S(1)}, bf16[4,4,48,128]{3,2,1,0:T(8,128)(2,1)S(1)}, u32[]{:S(2)}, u32[]{:S(2)}) %collective-permute-start.9) | collective-permute-done | bytes 196640 | tf_op jit(solution)/shard_map/ppermute | solution.py:206
  32.5 2.4 %shard_map.65 = (bf16[6,4,48,128]{3,2,1,0:T(8,128)(2,1)S(1)}, bf16[6,4,48,128]{3,2,1,0:T(8,128)(2,1)S(1)}, bf16[6,4,48,128]{3,2,1,0:T(8,128)(2,1)S(1)}, bf16[6,4,48,128]{3,2,1,0:T(8,128)(2,1)S(1)}) custom-call(s32[4]{0:T(128)S(1)} %pad_add_fusion.where_ref, bf16[4,4,48,128]{3,2,1,0:T(8,128)(2,1)S(1)} %slice.15.refs_0_, ...), custom_call_target="tpu_custom_call" | custom-call | bytes 3000000 | tf_op jit(solution)/shard_map/pallas_call | solution.py:237
  35.0 1.3 %collective-permute-start.10 = (bf16[6,4,48,128]{3,2,1,0:T(8,128)(2,1)S(1)}, bf16[6,4,48,128]{3,2,1,0:T(8,128)(2,1)S(1)}, u32[]{:S(2)}, u32[]{:S(2)}) collective-permute-start(bf16[6,4,48,128]{3,2,1,0:T(8,128)(2,1)S(1)} %get-tuple-element.39), channel_id=1, source_target_pairs={{0,8},{4,12},{8,0},{12,4},{16,24},{20,28},{24,16},{28,20},{1,9},{5... | collective-permute-start | bytes 884744 | tf_op jit(solution)/shard_map/ppermute | solution.py:206
  36.3 1.5 %collective-permute-start.11 = (bf16[6,4,48,128]{3,2,1,0:T(8,128)(2,1)S(1)}, bf16[6,4,48,128]{3,2,1,0:T(8,128)(2,1)S(1)}, u32[]{:S(2)}, u32[]{:S(2)}) collective-permute-start(bf16[6,4,48,128]{3,2,1,0:T(8,128)(2,1)S(1)} %get-tuple-element.40), channel_id=1, source_target_pairs={{0,16},{4,20},{8,24},{12,28},{16,0},{20,4},{24,8},{28,12},{1,17},{... | collective-permute-start | bytes 884744 | tf_op jit(solution)/shard_map/ppermute | solution.py:206
  37.8 0.7 collective-permute-start.12
  38.5 0.9 %pad_slice_fusion.refs_0_ = bf16[4,4,32,128]{3,2,1,0:T(8,128)(2,1)S(1)} fusion(bf16[4,4,137,128]{3,2,1,0:T(8,128)(2,1)} %copy-done.5), kind=kLoop, calls=%fused_computation.1 | loop fusion | bytes 692224 | tf_op jit(solution)/shard_map/slice | solution.py:282
  39.5 1.8 %collective-permute-start.3 = (bf16[4,4,32,128]{3,2,1,0:T(8,128)(2,1)S(1)}, bf16[4,4,32,128]{3,2,1,0:T(8,128)(2,1)S(1)}, u32[]{:S(2)}, u32[]{:S(2)}) collective-permute-start(bf16[4,4,32,128]{3,2,1,0:T(8,128)(2,1)S(1)} %pad_slice_fusion.refs_0_), channel_id=1, source_target_pairs={{0,2},{1,3},{2,0},{3,1},{4,6},{5,7},{6,4},{7,5},{8,10},{9,11},{10,... | collective-permute-start | bytes 393224 | tf_op jit(solution)/shard_map/ppermute | solution.py:206
  41.3 3.2 %collective-permute-done.14.refs_3_ = bf16[4,4,64,128]{3,2,1,0:T(8,128)(2,1)S(1)} collective-permute-done((bf16[4,4,64,128]{3,2,1,0:T(8,128)(2,1)S(1)}, bf16[4,4,64,128]{3,2,1,0:T(8,128)(2,1)S(1)}, u32[]{:S(2)}, u32[]{:S(2)}) %collective-permute-start.14) | collective-permute-done | bytes 262176 | tf_op jit(solution)/shard_map/ppermute | solution.py:206
  44.5 1.7 %shard_map.66 = (bf16[6,4,64,128]{3,2,1,0:T(8,128)(2,1)S(1)}, bf16[6,4,64,128]{3,2,1,0:T(8,128)(2,1)S(1)}, bf16[6,4,64,128]{3,2,1,0:T(8,128)(2,1)S(1)}, bf16[6,4,64,128]{3,2,1,0:T(8,128)(2,1)S(1)}) custom-call(s32[4]{0:T(128)S(1)} %pad_add_fusion.where_ref, bf16[4,4,64,128]{3,2,1,0:T(8,128)(2,1)S(1)} %slice.14.refs_0_, ...), custom_call_target="tpu_custom_call" | custom-call | bytes 3000000 | tf_op jit(solution)/shard_map/pallas_call | solution.py:237
  46.1 1.3 %collective-permute-start.19 = (bf16[6,4,64,128]{3,2,1,0:T(8,128)(2,1)S(1)}, bf16[6,4,64,128]{3,2,1,0:T(8,128)(2,1)S(1)}, u32[]{:S(2)}, u32[]{:S(2)}) collective-permute-start(bf16[6,4,64,128]{3,2,1,0:T(8,128)(2,1)S(1)} %get-tuple-element.43), channel_id=1, source_target_pairs={{0,8},{4,12},{8,0},{12,4},{16,24},{20,28},{24,16},{28,20},{1,9},{5... | collective-permute-start | bytes 1179656 | tf_op jit(solution)/shard_map/ppermute | solution.py:206
  48.1 1.4 %collective-permute-start.20 = (bf16[6,4,64,128]{3,2,1,0:T(8,128)(2,1)S(1)}, bf16[6,4,64,128]{3,2,1,0:T(8,128)(2,1)S(1)}, u32[]{:S(2)}, u32[]{:S(2)}) collective-permute-start(bf16[6,4,64,128]{3,2,1,0:T(8,128)(2,1)S(1)} %get-tuple-element.44), channel_id=1, source_target_pairs={{0,16},{4,20},{8,24},{12,28},{16,0},{20,4},{24,8},{28,12},{1,17},{... | collective-permute-start | bytes 1179656 | tf_op jit(solution)/shard_map/ppermute | solution.py:206
  49.5 1.4 %collective-permute-start.21 = (bf16[6,4,64,128]{3,2,1,0:T(8,128)(2,1)S(1)}, bf16[6,4,64,128]{3,2,1,0:T(8,128)(2,1)S(1)}, u32[]{:S(2)}, u32[]{:S(2)}) collective-permute-start(bf16[6,4,64,128]{3,2,1,0:T(8,128)(2,1)S(1)} %get-tuple-element.45), channel_id=1, source_target_pairs={{0,24},{4,28},{8,16},{12,20},{16,8},{20,12},{24,0},{28,4},{1,25},{... | collective-permute-start | bytes 1179656 | tf_op jit(solution)/shard_map/ppermute | solution.py:206
  50.9 2.0 %collective-permute-start.4 = (bf16[4,4,32,128]{3,2,1,0:T(8,128)(2,1)S(1)}, bf16[4,4,32,128]{3,2,1,0:T(8,128)(2,1)S(1)}, u32[]{:S(2)}, u32[]{:S(2)}) collective-permute-start(bf16[4,4,32,128]{3,2,1,0:T(8,128)(2,1)S(1)} %collective-permute-done.3.refs_2_), channel_id=1, source_target_pairs={{0,1},{1,0},{2,3},{3,2},{4,5},{5,4},{6,7},{7,6},{8,9},{9,8},{10,11... | collective-permute-start | bytes 393224 | tf_op jit(solution)/shard_map/ppermute | solution.py:206
  53.0 2.9 %collective-permute-done.2.refs_1_ = bf16[4,4,32,128]{3,2,1,0:T(8,128)(2,1)S(1)} collective-permute-done((bf16[4,4,32,128]{3,2,1,0:T(8,128)(2,1)S(1)}, bf16[4,4,32,128]{3,2,1,0:T(8,128)(2,1)S(1)}, u32[]{:S(2)}, u32[]{:S(2)}) %collective-permute-start.2) | collective-permute-done | bytes 131104 | tf_op jit(solution)/shard_map/ppermute | solution.py:206
  55.9 1.4 %collective-permute-done.4.refs_3_ = bf16[4,4,32,128]{3,2,1,0:T(8,128)(2,1)S(1)} collective-permute-done((bf16[4,4,32,128]{3,2,1,0:T(8,128)(2,1)S(1)}, bf16[4,4,32,128]{3,2,1,0:T(8,128)(2,1)S(1)}, u32[]{:S(2)}, u32[]{:S(2)}) %collective-permute-start.4) | collective-permute-done | bytes 131104 | tf_op jit(solution)/shard_map/ppermute | solution.py:206
  57.3 1.0 %collective-permute-done.19.refs_1_ = bf16[6,4,64,128]{3,2,1,0:T(8,128)(2,1)S(1)} collective-permute-done((bf16[6,4,64,128]{3,2,1,0:T(8,128)(2,1)S(1)}, bf16[6,4,64,128]{3,2,1,0:T(8,128)(2,1)S(1)}, u32[]{:S(2)}, u32[]{:S(2)}) %collective-permute-start.19) | collective-permute-done | bytes 393248 | tf_op jit(solution)/shard_map/ppermute | solution.py:206
  58.3 1.9 %shard_map.64 = (bf16[6,4,32,128]{3,2,1,0:T(8,128)(2,1)S(1)}, bf16[6,4,32,128]{3,2,1,0:T(8,128)(2,1)S(1)}, bf16[6,4,32,128]{3,2,1,0:T(8,128)(2,1)S(1)}, bf16[6,4,32,128]{3,2,1,0:T(8,128)(2,1)S(1)}) custom-call(s32[4]{0:T(128)S(1)} %pad_add_fusion.where_ref, bf16[4,4,32,128]{3,2,1,0:T(8,128)(2,1)S(1)} %pad_slice_fusion.refs_0_, ...), custom_call_target="tpu_custom_call" | custom-call | bytes 3000000 | tf_op jit(solution)/shard_map/pallas_call | solution.py:237
  60.2 6.1 %collective-permute-done.20.refs_2_ = bf16[6,4,64,128]{3,2,1,0:T(8,128)(2,1)S(1)} collective-permute-done((bf16[6,4,64,128]{3,2,1,0:T(8,128)(2,1)S(1)}, bf16[6,4,64,128]{3,2,1,0:T(8,128)(2,1)S(1)}, u32[]{:S(2)}, u32[]{:S(2)}) %collective-permute-start.20) | collective-permute-done | bytes 393248 | tf_op jit(solution)/shard_map/ppermute | solution.py:206
  67.5 0.9 %shard_map.67 = (bf16[2,8,128,256]{3,2,1,0:T(8,128)(2,1)S(1)}, bf16[2,144,144]{2,1,0:T(8,128)(2,1)S(1)}) custom-call(s32[4]{0:T(128)S(1)} %pad_add_fusion.where_ref, s32[8]{0:T(128)S(1)} %copy-done.3, s32[8,5]{1,0:T(8,128)S(1)} %copy-done.2, bf16[8,5,128,128]{3,2,1,0:T(8,128)(2,1)S(1)} %copy-done, bf16[137,8,137]{2,1,0:T(8,128)(2,1)S(1)} %bitcast.6), custom_call_target="tpu_custom_call" | custom-call | bytes 4000000 | tf_op jit(solution)/shard_map/pallas_call | solution.py:55
  68.4 0.7 collective-permute-done.18.refs_7_
  69.1 1.2 %collective-permute-start.5 = (bf16[6,4,32,128]{3,2,1,0:T(8,128)(2,1)S(1)}, bf16[6,4,32,128]{3,2,1,0:T(8,128)(2,1)S(1)}, u32[]{:S(2)}, u32[]{:S(2)}) collective-permute-start(bf16[6,4,32,128]{3,2,1,0:T(8,128)(2,1)S(1)} %get-tuple-element.35), channel_id=1, source_target_pairs={{0,8},{4,12},{8,0},{12,4},{16,24},{20,28},{24,16},{28,20},{1,9},{5... | collective-permute-start | bytes 589832 | tf_op jit(solution)/shard_map/ppermute | solution.py:206
  70.3 0.8 collective-permute-start.6
  71.1 1.4 %collective-permute-start.7 = (bf16[6,4,32,128]{3,2,1,0:T(8,128)(2,1)S(1)}, bf16[6,4,32,128]{3,2,1,0:T(8,128)(2,1)S(1)}, u32[]{:S(2)}, u32[]{:S(2)}) collective-permute-start(bf16[6,4,32,128]{3,2,1,0:T(8,128)(2,1)S(1)} %get-tuple-element.37), channel_id=1, source_target_pairs={{0,24},{4,28},{8,16},{12,20},{16,8},{20,12},{24,0},{28,4},{1,25},{... | collective-permute-start | bytes 589832 | tf_op jit(solution)/shard_map/ppermute | solution.py:206
  72.6 3.9 %shard_map.68.refs_10_ = bf16[2,2,16,48,256]{4,3,2,1,0:T(8,128)(2,1)S(1)} custom-call(s32[4]{0:T(128)S(1)} %pad_add_fusion.where_ref, s32[8]{0:T(128)S(1)} %copy-done.3, f32[3,8]{1,0:T(4,128)S(1)} %bitcast.10, bf16[6,4,48,128]{3,2,1,0:T(8,128)(2,1)S(1)} %get-tuple-element.46.refs_0_, bf16[6,4,48,128]{3,2,1,0:T(8,128)(2,1)S(1)} %collective-permute-done.10.refs_1_, ...), custom_call_target="tpu_custom_call" | custom-call | flops 2000000000 | bytes 8000000 | tf_op jit(solution)/shard_map/pallas_call | solution.py:169
  76.6 4.7 %shard_map.69.refs_11_ = bf16[2,2,16,64,256]{4,3,2,1,0:T(8,128)(2,1)S(1)} custom-call(s32[4]{0:T(128)S(1)} %pad_add_fusion.where_ref, s32[8]{0:T(128)S(1)} %copy-done.3, f32[3,8]{1,0:T(4,128)S(1)} %bitcast.11, bf16[6,4,64,128]{3,2,1,0:T(8,128)(2,1)S(1)} %get-tuple-element.51.refs_0_, bf16[6,4,64,128]{3,2,1,0:T(8,128)(2,1)S(1)} %collective-permute-done.19.refs_1_, ...), custom_call_target="tpu_custom_call" | custom-call | flops 2000000000 | bytes 8000000 | tf_op jit(solution)/shard_map/pallas_call | solution.py:169
  83.6 6.5 %shard_map.70 = bf16[2,2,137,32,128]{4,3,2,1,0:T(8,128)(2,1)} custom-call(s32[4]{0:T(128)S(1)} %pad_add_fusion.where_ref, s32[8]{0:T(128)S(1)} %copy-done.3, f32[3,8]{1,0:T(4,128)S(1)} %bitcast.12, bf16[6,4,32,128]{3,2,1,0:T(8,128)(2,1)S(1)} %get-tuple-element.34.refs_0_, bf16[6,4,32,128]{3,2,1,0:T(8,128)(2,1)S(1)} %collective-permute-done.5.refs_1_, ...), custom_call_target="tpu_custom_call" | custom-call | flops 4000000000 | bytes 12000000 | tf_op jit(solution)/shard_map/pallas_call | solution.py:187
  (52 shorter events, 4.3 us)
Async XLA Ops:
  1.4 13.2 %collective-permute-start = (bf16[4,4,48,128]{3,2,1,0:T(8,128)(2,1)S(1)}, bf16[4,4,48,128]{3,2,1,0:T(8,128)(2,1)S(1)}, u32[]{:S(2)}, u32[]{:S(2)}) collective-permute-start(bf16[4,4,48,128]{3,2,1,0:T(8,128)(2,1)S(1)} %slice.15.refs_0_), channel_id=1, source_target_pairs={{0,2},{1,3},{2,0},{3,1},{4,6},{5,7},{6,4},{7,5},{8,10},{9,11},{10,... | collective-permute-start | bytes 589832 | tf_op jit(solution)/shard_map/ppermute | solution.py:206
  5.5 61.9 %copy-start = (bf16[8,5,128,128]{3,2,1,0:T(8,128)(2,1)S(1)}, bf16[8,5,128,128]{3,2,1,0:T(8,128)(2,1)}, u32[]{:S(2)}) copy-start(bf16[8,5,128,128]{3,2,1,0:T(8,128)(2,1)} %filter_ref.1) | copy-start | bytes 3932164
  5.5 61.9 %copy-start.1 = (bf16[8,137,137]{2,0,1:T(8,128)(2,1)S(1)}, bf16[8,137,137]{2,0,1:T(8,128)(2,1)}, u32[]{:S(2)}) copy-start(bf16[8,137,137]{2,0,1:T(8,128)(2,1)} %param.10) | copy-start | bytes 900916
  14.6 14.1 %collective-permute-start.1 = (bf16[4,4,64,128]{3,2,1,0:T(8,128)(2,1)S(1)}, bf16[4,4,64,128]{3,2,1,0:T(8,128)(2,1)S(1)}, u32[]{:S(2)}, u32[]{:S(2)}) collective-permute-start(bf16[4,4,64,128]{3,2,1,0:T(8,128)(2,1)S(1)} %slice.14.refs_0_), channel_id=1, source_target_pairs={{0,2},{1,3},{2,0},{3,1},{4,6},{5,7},{6,4},{7,5},{8,10},{9,11},{10,... | collective-permute-start | bytes 786440 | tf_op jit(solution)/shard_map/ppermute | solution.py:206
  14.6 14.2 %collective-permute-start.8 = (bf16[4,4,48,128]{3,2,1,0:T(8,128)(2,1)S(1)}, bf16[4,4,48,128]{3,2,1,0:T(8,128)(2,1)S(1)}, u32[]{:S(2)}, u32[]{:S(2)}) collective-permute-start(bf16[4,4,48,128]{3,2,1,0:T(8,128)(2,1)S(1)} %slice.15.refs_0_), channel_id=1, source_target_pairs={{0,1},{1,0},{2,3},{3,2},{4,5},{5,4},{6,7},{7,6},{8,9},{9,8},{10,11... | collective-permute-start | bytes 589832 | tf_op jit(solution)/shard_map/ppermute | solution.py:206
  18.7 13.8 %collective-permute-start.9 = (bf16[4,4,48,128]{3,2,1,0:T(8,128)(2,1)S(1)}, bf16[4,4,48,128]{3,2,1,0:T(8,128)(2,1)S(1)}, u32[]{:S(2)}, u32[]{:S(2)}) collective-permute-start(bf16[4,4,48,128]{3,2,1,0:T(8,128)(2,1)S(1)} %collective-permute-done.refs_2_), channel_id=1, source_target_pairs={{0,1},{1,0},{2,3},{3,2},{4,5},{5,4},{6,7},{7,6},{8,9},{9,8},{10,11... | collective-permute-start | bytes 589832 | tf_op jit(solution)/shard_map/ppermute | solution.py:206
  18.7 20.7 %collective-permute-start.13 = (bf16[4,4,64,128]{3,2,1,0:T(8,128)(2,1)S(1)}, bf16[4,4,64,128]{3,2,1,0:T(8,128)(2,1)S(1)}, u32[]{:S(2)}, u32[]{:S(2)}) collective-permute-start(bf16[4,4,64,128]{3,2,1,0:T(8,128)(2,1)S(1)} %slice.14.refs_0_), channel_id=1, source_target_pairs={{0,1},{1,0},{2,3},{3,2},{4,5},{5,4},{6,7},{7,6},{8,9},{9,8},{10,11... | collective-permute-start | bytes 786440 | tf_op jit(solution)/shard_map/ppermute | solution.py:206
  28.7 15.7 %collective-permute-start.14 = (bf16[4,4,64,128]{3,2,1,0:T(8,128)(2,1)S(1)}, bf16[4,4,64,128]{3,2,1,0:T(8,128)(2,1)S(1)}, u32[]{:S(2)}, u32[]{:S(2)}) collective-permute-start(bf16[4,4,64,128]{3,2,1,0:T(8,128)(2,1)S(1)} %collective-permute-done.1.refs_2_), channel_id=1, source_target_pairs={{0,1},{1,0},{2,3},{3,2},{4,5},{5,4},{6,7},{7,6},{8,9},{9,8},{10,11... | collective-permute-start | bytes 786440 | tf_op jit(solution)/shard_map/ppermute | solution.py:206
  35.0 14.5 %collective-permute-start.10 = (bf16[6,4,48,128]{3,2,1,0:T(8,128)(2,1)S(1)}, bf16[6,4,48,128]{3,2,1,0:T(8,128)(2,1)S(1)}, u32[]{:S(2)}, u32[]{:S(2)}) collective-permute-start(bf16[6,4,48,128]{3,2,1,0:T(8,128)(2,1)S(1)} %get-tuple-element.39), channel_id=1, source_target_pairs={{0,8},{4,12},{8,0},{12,4},{16,24},{20,28},{24,16},{28,20},{1,9},{5... | collective-permute-start | bytes 884744 | tf_op jit(solution)/shard_map/ppermute | solution.py:206
  36.3 14.6 %collective-permute-start.11 = (bf16[6,4,48,128]{3,2,1,0:T(8,128)(2,1)S(1)}, bf16[6,4,48,128]{3,2,1,0:T(8,128)(2,1)S(1)}, u32[]{:S(2)}, u32[]{:S(2)}) collective-permute-start(bf16[6,4,48,128]{3,2,1,0:T(8,128)(2,1)S(1)} %get-tuple-element.40), channel_id=1, source_target_pairs={{0,16},{4,20},{8,24},{12,28},{16,0},{20,4},{24,8},{28,12},{1,17},{... | collective-permute-start | bytes 884744 | tf_op jit(solution)/shard_map/ppermute | solution.py:206
  37.8 13.1 %collective-permute-start.12 = (bf16[6,4,48,128]{3,2,1,0:T(8,128)(2,1)S(1)}, bf16[6,4,48,128]{3,2,1,0:T(8,128)(2,1)S(1)}, u32[]{:S(2)}, u32[]{:S(2)}) collective-permute-start(bf16[6,4,48,128]{3,2,1,0:T(8,128)(2,1)S(1)} %get-tuple-element.41), channel_id=1, source_target_pairs={{0,24},{4,28},{8,16},{12,20},{16,8},{20,12},{24,0},{28,4},{1,25},{... | collective-permute-start | bytes 884744 | tf_op jit(solution)/shard_map/ppermute | solution.py:206
  39.5 8.6 %collective-permute-start.3 = (bf16[4,4,32,128]{3,2,1,0:T(8,128)(2,1)S(1)}, bf16[4,4,32,128]{3,2,1,0:T(8,128)(2,1)S(1)}, u32[]{:S(2)}, u32[]{:S(2)}) collective-permute-start(bf16[4,4,32,128]{3,2,1,0:T(8,128)(2,1)S(1)} %pad_slice_fusion.refs_0_), channel_id=1, source_target_pairs={{0,2},{1,3},{2,0},{3,1},{4,6},{5,7},{6,4},{7,5},{8,10},{9,11},{10,... | collective-permute-start | bytes 393224 | tf_op jit(solution)/shard_map/ppermute | solution.py:206
  46.1 12.1 %collective-permute-start.19 = (bf16[6,4,64,128]{3,2,1,0:T(8,128)(2,1)S(1)}, bf16[6,4,64,128]{3,2,1,0:T(8,128)(2,1)S(1)}, u32[]{:S(2)}, u32[]{:S(2)}) collective-permute-start(bf16[6,4,64,128]{3,2,1,0:T(8,128)(2,1)S(1)} %get-tuple-element.43), channel_id=1, source_target_pairs={{0,8},{4,12},{8,0},{12,4},{16,24},{20,28},{24,16},{28,20},{1,9},{5... | collective-permute-start | bytes 1179656 | tf_op jit(solution)/shard_map/ppermute | solution.py:206
  48.1 18.3 %collective-permute-start.20 = (bf16[6,4,64,128]{3,2,1,0:T(8,128)(2,1)S(1)}, bf16[6,4,64,128]{3,2,1,0:T(8,128)(2,1)S(1)}, u32[]{:S(2)}, u32[]{:S(2)}) collective-permute-start(bf16[6,4,64,128]{3,2,1,0:T(8,128)(2,1)S(1)} %get-tuple-element.44), channel_id=1, source_target_pairs={{0,16},{4,20},{8,24},{12,28},{16,0},{20,4},{24,8},{28,12},{1,17},{... | collective-permute-start | bytes 1179656 | tf_op jit(solution)/shard_map/ppermute | solution.py:206
  49.5 16.9 %collective-permute-start.21 = (bf16[6,4,64,128]{3,2,1,0:T(8,128)(2,1)S(1)}, bf16[6,4,64,128]{3,2,1,0:T(8,128)(2,1)S(1)}, u32[]{:S(2)}, u32[]{:S(2)}) collective-permute-start(bf16[6,4,64,128]{3,2,1,0:T(8,128)(2,1)S(1)} %get-tuple-element.45), channel_id=1, source_target_pairs={{0,24},{4,28},{8,16},{12,20},{16,8},{20,12},{24,0},{28,4},{1,25},{... | collective-permute-start | bytes 1179656 | tf_op jit(solution)/shard_map/ppermute | solution.py:206
  50.9 5.0 %collective-permute-start.2 = (bf16[4,4,32,128]{3,2,1,0:T(8,128)(2,1)S(1)}, bf16[4,4,32,128]{3,2,1,0:T(8,128)(2,1)S(1)}, u32[]{:S(2)}, u32[]{:S(2)}) collective-permute-start(bf16[4,4,32,128]{3,2,1,0:T(8,128)(2,1)S(1)} %pad_slice_fusion.refs_0_), channel_id=1, source_target_pairs={{0,1},{1,0},{2,3},{3,2},{4,5},{5,4},{6,7},{7,6},{8,9},{9,8},{10,11... | collective-permute-start | bytes 393224 | tf_op jit(solution)/shard_map/ppermute | solution.py:206
  50.9 6.4 %collective-permute-start.4 = (bf16[4,4,32,128]{3,2,1,0:T(8,128)(2,1)S(1)}, bf16[4,4,32,128]{3,2,1,0:T(8,128)(2,1)S(1)}, u32[]{:S(2)}, u32[]{:S(2)}) collective-permute-start(bf16[4,4,32,128]{3,2,1,0:T(8,128)(2,1)S(1)} %collective-permute-done.3.refs_2_), channel_id=1, source_target_pairs={{0,1},{1,0},{2,3},{3,2},{4,5},{5,4},{6,7},{7,6},{8,9},{9,8},{10,11... | collective-permute-start | bytes 393224 | tf_op jit(solution)/shard_map/ppermute | solution.py:206
  55.9 11.0 %collective-permute-start.15 = (bf16[6,4,48,128]{3,2,1,0:T(8,128)(2,1)S(1)}, bf16[6,4,48,128]{3,2,1,0:T(8,128)(2,1)S(1)}, u32[]{:S(2)}, u32[]{:S(2)}) collective-permute-start(bf16[6,4,48,128]{3,2,1,0:T(8,128)(2,1)S(1)} %get-tuple-element.46.refs_0_), channel_id=1, source_target_pairs={{0,4},{4,0},{8,12},{12,8},{16,20},{20,16},{24,28},{28,24},{1,5},{5... | collective-permute-start | bytes 884744 | tf_op jit(solution)/shard_map/ppermute | solution.py:206
  57.3 9.6 %collective-permute-start.16 = (bf16[6,4,48,128]{3,2,1,0:T(8,128)(2,1)S(1)}, bf16[6,4,48,128]{3,2,1,0:T(8,128)(2,1)S(1)}, u32[]{:S(2)}, u32[]{:S(2)}) collective-permute-start(bf16[6,4,48,128]{3,2,1,0:T(8,128)(2,1)S(1)} %collective-permute-done.10.refs_1_), channel_id=1, source_target_pairs={{0,4},{4,0},{8,12},{12,8},{16,20},{20,16},{24,28},{28,24},{1,5},{5... | collective-permute-start | bytes 884744 | tf_op jit(solution)/shard_map/ppermute | solution.py:206
  58.3 9.1 %collective-permute-start.17 = (bf16[6,4,48,128]{3,2,1,0:T(8,128)(2,1)S(1)}, bf16[6,4,48,128]{3,2,1,0:T(8,128)(2,1)S(1)}, u32[]{:S(2)}, u32[]{:S(2)}) collective-permute-start(bf16[6,4,48,128]{3,2,1,0:T(8,128)(2,1)S(1)} %collective-permute-done.11.refs_2_), channel_id=1, source_target_pairs={{0,4},{4,0},{8,12},{12,8},{16,20},{20,16},{24,28},{28,24},{1,5},{5... | collective-permute-start | bytes 884744 | tf_op jit(solution)/shard_map/ppermute | solution.py:206
  66.3 3.9 %collective-permute-start.22 = (bf16[6,4,64,128]{3,2,1,0:T(8,128)(2,1)S(1)}, bf16[6,4,64,128]{3,2,1,0:T(8,128)(2,1)S(1)}, u32[]{:S(2)}, u32[]{:S(2)}) collective-permute-start(bf16[6,4,64,128]{3,2,1,0:T(8,128)(2,1)S(1)} %get-tuple-element.51.refs_0_), channel_id=1, source_target_pairs={{0,4},{4,0},{8,12},{12,8},{16,20},{20,16},{24,28},{28,24},{1,5},{5... | collective-permute-start | bytes 1179656 | tf_op jit(solution)/shard_map/ppermute | solution.py:206
  66.3 4.8 %collective-permute-start.23 = (bf16[6,4,64,128]{3,2,1,0:T(8,128)(2,1)S(1)}, bf16[6,4,64,128]{3,2,1,0:T(8,128)(2,1)S(1)}, u32[]{:S(2)}, u32[]{:S(2)}) collective-permute-start(bf16[6,4,64,128]{3,2,1,0:T(8,128)(2,1)S(1)} %collective-permute-done.19.refs_1_), channel_id=1, source_target_pairs={{0,4},{4,0},{8,12},{12,8},{16,20},{20,16},{24,28},{28,24},{1,5},{5... | collective-permute-start | bytes 1179656 | tf_op jit(solution)/shard_map/ppermute | solution.py:206
  66.9 2.2 %collective-permute-start.18 = (bf16[6,4,48,128]{3,2,1,0:T(8,128)(2,1)S(1)}, bf16[6,4,48,128]{3,2,1,0:T(8,128)(2,1)S(1)}, u32[]{:S(2)}, u32[]{:S(2)}) collective-permute-start(bf16[6,4,48,128]{3,2,1,0:T(8,128)(2,1)S(1)} %collective-permute-done.12.refs_3_), channel_id=1, source_target_pairs={{0,4},{4,0},{8,12},{12,8},{16,20},{20,16},{24,28},{28,24},{1,5},{5... | collective-permute-start | bytes 884744 | tf_op jit(solution)/shard_map/ppermute | solution.py:206
  66.9 9.6 %collective-permute-start.24 = (bf16[6,4,64,128]{3,2,1,0:T(8,128)(2,1)S(1)}, bf16[6,4,64,128]{3,2,1,0:T(8,128)(2,1)S(1)}, u32[]{:S(2)}, u32[]{:S(2)}) collective-permute-start(bf16[6,4,64,128]{3,2,1,0:T(8,128)(2,1)S(1)} %collective-permute-done.20.refs_2_), channel_id=1, source_target_pairs={{0,4},{4,0},{8,12},{12,8},{16,20},{20,16},{24,28},{28,24},{1,5},{5... | collective-permute-start | bytes 1179656 | tf_op jit(solution)/shard_map/ppermute | solution.py:206
  67.4 9.2 %collective-permute-start.25 = (bf16[6,4,64,128]{3,2,1,0:T(8,128)(2,1)S(1)}, bf16[6,4,64,128]{3,2,1,0:T(8,128)(2,1)S(1)}, u32[]{:S(2)}, u32[]{:S(2)}) collective-permute-start(bf16[6,4,64,128]{3,2,1,0:T(8,128)(2,1)S(1)} %collective-permute-done.21.refs_3_), channel_id=1, source_target_pairs={{0,4},{4,0},{8,12},{12,8},{16,20},{20,16},{24,28},{28,24},{1,5},{5... | collective-permute-start | bytes 1179656 | tf_op jit(solution)/shard_map/ppermute | solution.py:206
  69.1 12.3 %collective-permute-start.5 = (bf16[6,4,32,128]{3,2,1,0:T(8,128)(2,1)S(1)}, bf16[6,4,32,128]{3,2,1,0:T(8,128)(2,1)S(1)}, u32[]{:S(2)}, u32[]{:S(2)}) collective-permute-start(bf16[6,4,32,128]{3,2,1,0:T(8,128)(2,1)S(1)} %get-tuple-element.35), channel_id=1, source_target_pairs={{0,8},{4,12},{8,0},{12,4},{16,24},{20,28},{24,16},{28,20},{1,9},{5... | collective-permute-start | bytes 589832 | tf_op jit(solution)/shard_map/ppermute | solution.py:206
  70.3 11.0 %collective-permute-start.6 = (bf16[6,4,32,128]{3,2,1,0:T(8,128)(2,1)S(1)}, bf16[6,4,32,128]{3,2,1,0:T(8,128)(2,1)S(1)}, u32[]{:S(2)}, u32[]{:S(2)}) collective-permute-start(bf16[6,4,32,128]{3,2,1,0:T(8,128)(2,1)S(1)} %get-tuple-element.36), channel_id=1, source_target_pairs={{0,16},{4,20},{8,24},{12,28},{16,0},{20,4},{24,8},{28,12},{1,17},{... | collective-permute-start | bytes 589832 | tf_op jit(solution)/shard_map/ppermute | solution.py:206
  71.1 10.2 %collective-permute-start.7 = (bf16[6,4,32,128]{3,2,1,0:T(8,128)(2,1)S(1)}, bf16[6,4,32,128]{3,2,1,0:T(8,128)(2,1)S(1)}, u32[]{:S(2)}, u32[]{:S(2)}) collective-permute-start(bf16[6,4,32,128]{3,2,1,0:T(8,128)(2,1)S(1)} %get-tuple-element.37), channel_id=1, source_target_pairs={{0,24},{4,28},{8,16},{12,20},{16,8},{20,12},{24,0},{28,4},{1,25},{... | collective-permute-start | bytes 589832 | tf_op jit(solution)/shard_map/ppermute | solution.py:206
  76.5 5.9 %collective-permute-start.26 = (bf16[6,4,32,128]{3,2,1,0:T(8,128)(2,1)S(1)}, bf16[6,4,32,128]{3,2,1,0:T(8,128)(2,1)S(1)}, u32[]{:S(2)}, u32[]{:S(2)}) collective-permute-start(bf16[6,4,32,128]{3,2,1,0:T(8,128)(2,1)S(1)} %get-tuple-element.34.refs_0_), channel_id=1, source_target_pairs={{0,4},{4,0},{8,12},{12,8},{16,20},{20,16},{24,28},{28,24},{1,5},{5... | collective-permute-start | bytes 589832 | tf_op jit(solution)/shard_map/ppermute | solution.py:206
  81.4 1.6 %collective-permute-start.27 = (bf16[6,4,32,128]{3,2,1,0:T(8,128)(2,1)S(1)}, bf16[6,4,32,128]{3,2,1,0:T(8,128)(2,1)S(1)}, u32[]{:S(2)}, u32[]{:S(2)}) collective-permute-start(bf16[6,4,32,128]{3,2,1,0:T(8,128)(2,1)S(1)} %collective-permute-done.5.refs_1_), channel_id=1, source_target_pairs={{0,4},{4,0},{8,12},{12,8},{16,20},{20,16},{24,28},{28,24},{1,5},{5... | collective-permute-start | bytes 589832 | tf_op jit(solution)/shard_map/ppermute | solution.py:206
  81.9 1.4 %collective-permute-start.28 = (bf16[6,4,32,128]{3,2,1,0:T(8,128)(2,1)S(1)}, bf16[6,4,32,128]{3,2,1,0:T(8,128)(2,1)S(1)}, u32[]{:S(2)}, u32[]{:S(2)}) collective-permute-start(bf16[6,4,32,128]{3,2,1,0:T(8,128)(2,1)S(1)} %collective-permute-done.6.refs_2_), channel_id=1, source_target_pairs={{0,4},{4,0},{8,12},{12,8},{16,20},{20,16},{24,28},{28,24},{1,5},{5... | collective-permute-start | bytes 589832 | tf_op jit(solution)/shard_map/ppermute | solution.py:206
  81.9 1.6 %collective-permute-start.29 = (bf16[6,4,32,128]{3,2,1,0:T(8,128)(2,1)S(1)}, bf16[6,4,32,128]{3,2,1,0:T(8,128)(2,1)S(1)}, u32[]{:S(2)}, u32[]{:S(2)}) collective-permute-start(bf16[6,4,32,128]{3,2,1,0:T(8,128)(2,1)S(1)} %collective-permute-done.7.refs_3_), channel_id=1, source_target_pairs={{0,4},{4,0},{8,12},{12,8},{16,20},{20,16},{24,28},{28,24},{1,5},{5... | collective-permute-start | bytes 589832 | tf_op jit(solution)/shard_map/ppermute | solution.py:206
  (4 other events, 161.0 us)

commit v5 on v4

--- a/solution.py
+++ b/solution.py
@@ -11,7 +11,7 @@
 SUBLANES = 16
 LANES = 128
 SPREAD_GAP = 8
-CUTS = (48, 112)
+CUTS = (48, 96)
 
 
 SCALAR = pl.BlockSpec(memory_space=pltpu.SMEM)
@@ -62,7 +62,7 @@
         ],
         scratch_shapes=[pltpu.VMEM((pl.cdiv(levels, LANES), vertical.shape[0] * levels, LANES), jnp.float32)],
         compiler_params=PARAMS,
-        cost_estimate=pl.CostEstimate(flops=0, bytes_accessed=4_000_000, transcendentals=0),
+        cost_estimate=pl.CostEstimate(flops=0, bytes_accessed=4000000, transcendentals=0),
     )(where, slot_of_band, block_offsets, filters, vertical.transpose(1, 0, 2))
     return filt.reshape(group, REACH + 1, 2 * c, 2 * c), vert
 
@@ -81,6 +81,12 @@
     shard_rows, per_source, _, c = kept[0].shape
     half = chips * per_source
     first = lax.rem(place, 2) * ((shard_rows - 2) // 2) + r
+
+    def row_of(side, k, i, n):
+        if side == 0:
+            return kept[k][first + i, n]
+        return got[0][k, r + i, n] if len(got) == 1 else got[k][first + i, n]
+
     for k in range(chips):
         for side in range(2):
             source = (place ^ (2 * k)) ^ side
@@ -174,7 +180,7 @@
         out_shape=out,
         scratch_shapes=[pltpu.VMEM((half + taps - 1, depth, width), jnp.bfloat16)],
         compiler_params=PARAMS,
-        cost_estimate=pl.CostEstimate(flops=2_000_000_000, bytes_accessed=8_000_000, transcendentals=0),
+        cost_estimate=pl.CostEstimate(flops=2000000000, bytes_accessed=8000000, transcendentals=0),
     )(*scalars, *kept, *got, filt)
 
 
@@ -241,7 +247,7 @@
         out_shape=[out] * len(pieces),
         scratch_shapes=[pltpu.SemaphoreType.DMA((len(pieces), 3))],
         compiler_params=PARAMS,
-        cost_estimate=pl.CostEstimate(flops=0, bytes_accessed=3_000_000, transcendentals=0),
+        cost_estimate=pl.CostEstimate(flops=0, bytes_accessed=3000000, transcendentals=0),
     )(where, *pieces)
 
 
@@ -258,6 +264,33 @@
     order = sorted(range(1, len(sends)), key=lambda k: -k)
     got = {k: swapped(sends[k], "lon", 2 * k) for k in order}
     return [sends[0]] + [got[k] for k in sorted(got)]
+
+
+def give_kernel(where_ref, *refs):
+    kept, (out_ref, sems) = refs[:-2], refs[-2:]
+    count = out_ref.shape[1]
+    first = (1 - where_ref[0] % 2) * (count - 2)
+    copies = [
+        pltpu.make_async_copy(m.at[pl.ds(first, count)], out_ref.at[k], sems.at[k]) for k, m in enumerate(kept)
+    ]
+    for copy in copies:
+        copy.start()
+    for copy in copies:
+        copy.wait()
+
+
+def given_rows(where, kept):
+    shape = kept[0].shape
+    anywhere = pl.BlockSpec(memory_space=pl.ANY)
+    return pl.pallas_call(
+        give_kernel,
+        in_specs=[SCALAR] + [anywhere] * len(kept),
+        out_specs=anywhere,
+        out_shape=jax.ShapeDtypeStruct((len(kept), shape[0] // 2 + 1) + shape[1:], kept[0].dtype),
+        scratch_shapes=[pltpu.SemaphoreType.DMA((len(kept),))],
+        compiler_params=PARAMS,
+        cost_estimate=pl.CostEstimate(flops=0, bytes_accessed=2_000_000, transcendentals=0),
+    )(where, *kept)
 
 
 def after(value, *marks):
@@ -289,7 +322,7 @@
     done = []
     for i in range(last):
         here = after(kept[i], sends[i + 1])
-        got = [swapped(m, "lon", 1) for m in here]
+        got = [swapped(given_rows(where, here), "lon", 1)]
         done.append(first_part(scalars, here, got, filt, rows))
     here = kept[last][:1] + after(kept[last][1:], *done)
     got = [swapped(m, "lon", 1) for m in here]

time: 90.2 us -> 88.1 us (0.977)
  waiting for transfers between devices: 37.9 us -> 30 us
  Pallas kernels: 22.1 us -> 28.9 us
    ppermute x30 -> x24, waiting for transfers between devices: 37.9 us -> 30 us  [swapped(): lax.ppermute(value, axis, [(i, i ^ by) for i in range(lax.axis_size(axis))])]
    pallas_call x0 -> x2, Pallas kernels: none -> 3.21 us  [given_rows(): pl.pallas_call(give_kernel, in_specs=[SCALAR] + [anywhere] * len(kept), o...]
    pallas_call x1, Pallas kernels: 6.48 us -> 9.56 us  [last_part(): pl.pallas_call(functools.partial(last_kernel, len(kept)), grid=(rows, gro...]
    pallas_call x3, Pallas kernels: 6.04 us -> 7.31 us  [sorted_rows(): pl.pallas_call(sort_kernel, in_specs=[SCALAR] + [anywhere] * len(pieces),...]
    ppermute x30 -> x24, starting transfers between devices: 27.4 us -> 26.9 us  [swapped(): lax.ppermute(value, axis, [(i, i ^ by) for i in range(lax.axis_size(axis))])]
  transfers between devices with their start and end apart: 30 -> 24, of which waited for: 13 -> 8; matrix products, arithmetic and copies ran while one was open for 1% -> 0% of each run, Pallas kernels for 17% -> 22%
where the time goes in v5:
time: 88.1 us; the launch traced here: 87.6 us
  waiting for transfers between devices  30 us (34%)
  Pallas kernels  28.9 us (33%)
  starting transfers between devices  26.9 us (31%)
  local copies, waits for them, and re-layouts  1.45 us (2%)
    ppermute x24, waiting for transfers between devices, swapped(): lax.ppermute(value, axis, [(i, i ^ by) for i in range(lax.axis_size(axis))])  30 us
    ppermute x24, starting transfers between devices, swapped(): lax.ppermute(value, axis, [(i, i ^ by) for i in range(lax.axis_size(axis))])  26.9 us
    pallas_call x1, Pallas kernels, last_part(): pl.pallas_call(functools.partial(last_kernel, len(kept)), grid=(rows, gro...  9.56 us
    pallas_call x2, Pallas kernels, first_part(): pl.pallas_call(functools.partial(first_kernel, len(kept)), grid=(rows, gr...  7.86 us
    pallas_call x3, Pallas kernels, sorted_rows(): pl.pallas_call(sort_kernel, in_specs=[SCALAR] + [anywhere] * len(pieces),...  7.31 us
    pallas_call x2, Pallas kernels, given_rows(): pl.pallas_call(give_kernel, in_specs=[SCALAR] + [anywhere] * len(kept), o...  3.21 us
  transfers between devices with their start and end apart: 24, of which 8 were waited for; matrix products, arithmetic and copies ran while one was open for 0% of the time, Pallas kernels for 22%

profile of v5, /device:TPU:0, one launch (start us, length us, event | category | flops | bytes accessed | tf_op | source)
XLA Modules:
  0.0 87.6 jit_solution(10724121410235752288)
XLA Ops:
  0.0 1.4 %copy.9 = bf16[4,4,137,128]{3,2,1,0:T(8,128)(2,1)S(1)} copy(f32[4,4,137,128]{3,1,2,0:T(4,128)} %param.6) | data formatting | bytes 1683456 | tf_op args[0]
  1.4 4.1 %collective-permute-start = (bf16[4,4,48,128]{3,2,1,0:T(8,128)(2,1)S(1)}, bf16[4,4,48,128]{3,2,1,0:T(8,128)(2,1)S(1)}, u32[]{:S(2)}, u32[]{:S(2)}) collective-permute-start(bf16[4,4,48,128]{3,2,1,0:T(8,128)(2,1)S(1)} %get-tuple-element.59.refs_0_), channel_id=1, source_target_pairs={{0,2},{1,3},{2,0},{3,1},{4,6},{5,7},{6,4},{7,5},{8,10},{9,11},{10,... | collective-permute-start | bytes 589832 | tf_op jit(solution)/shard_map/ppermute | solution.py:212
  5.5 1.6 %collective-permute-start.8 = (bf16[4,4,48,128]{3,2,1,0:T(8,128)(2,1)S(1)}, bf16[4,4,48,128]{3,2,1,0:T(8,128)(2,1)S(1)}, u32[]{:S(2)}, u32[]{:S(2)}) collective-permute-start(bf16[4,4,48,128]{3,2,1,0:T(8,128)(2,1)S(1)} %get-tuple-element.59.refs_0_), channel_id=1, source_target_pairs={{0,1},{1,0},{2,3},{3,2},{4,5},{5,4},{6,7},{7,6},{8,9},{9,8},{10,11... | collective-permute-start | bytes 589832 | tf_op jit(solution)/shard_map/ppermute | solution.py:212
  7.1 7.6 %collective-permute-done.refs_2_ = bf16[4,4,48,128]{3,2,1,0:T(8,128)(2,1)S(1)} collective-permute-done((bf16[4,4,48,128]{3,2,1,0:T(8,128)(2,1)S(1)}, bf16[4,4,48,128]{3,2,1,0:T(8,128)(2,1)S(1)}, u32[]{:S(2)}, u32[]{:S(2)}) %collective-permute-start) | collective-permute-done | bytes 196640 | tf_op jit(solution)/shard_map/ppermute | solution.py:212
  14.8 0.6 collective-permute-start.9
  15.4 3.4 %collective-permute-start.1 = (bf16[4,4,48,128]{3,2,1,0:T(8,128)(2,1)S(1)}, bf16[4,4,48,128]{3,2,1,0:T(8,128)(2,1)S(1)}, u32[]{:S(2)}, u32[]{:S(2)}) collective-permute-start(bf16[4,4,48,128]{3,2,1,0:T(8,128)(2,1)S(1)} %get-tuple-element.32.refs_0_), channel_id=1, source_target_pairs={{0,2},{1,3},{2,0},{3,1},{4,6},{5,7},{6,4},{7,5},{8,10},{9,11},{10,... | collective-permute-start | bytes 589832 | tf_op jit(solution)/shard_map/ppermute | solution.py:212
  18.8 7.2 %collective-permute-done.9.refs_3_ = bf16[4,4,48,128]{3,2,1,0:T(8,128)(2,1)S(1)} collective-permute-done((bf16[4,4,48,128]{3,2,1,0:T(8,128)(2,1)S(1)}, bf16[4,4,48,128]{3,2,1,0:T(8,128)(2,1)S(1)}, u32[]{:S(2)}, u32[]{:S(2)}) %collective-permute-start.9) | collective-permute-done | bytes 196640 | tf_op jit(solution)/shard_map/ppermute | solution.py:212
  26.0 2.4 %shard_map.65 = (bf16[6,4,48,128]{3,2,1,0:T(8,128)(2,1)S(1)}, bf16[6,4,48,128]{3,2,1,0:T(8,128)(2,1)S(1)}, bf16[6,4,48,128]{3,2,1,0:T(8,128)(2,1)S(1)}, bf16[6,4,48,128]{3,2,1,0:T(8,128)(2,1)S(1)}) custom-call(s32[4]{0:T(128)S(1)} %pad_add_fusion.where_ref, bf16[4,4,48,128]{3,2,1,0:T(8,128)(2,1)S(1)} %get-tuple-element.59.refs_0_, ...), custom_call_target="tpu_custom_call" | custom-call | bytes 3000000 | tf_op jit(solution)/shard_map/pallas_call | solution.py:243
  28.5 1.0 %collective-permute-start.10 = (bf16[6,4,48,128]{3,2,1,0:T(8,128)(2,1)S(1)}, bf16[6,4,48,128]{3,2,1,0:T(8,128)(2,1)S(1)}, u32[]{:S(2)}, u32[]{:S(2)}) collective-permute-start(bf16[6,4,48,128]{3,2,1,0:T(8,128)(2,1)S(1)} %get-tuple-element.39), channel_id=1, source_target_pairs={{0,8},{4,12},{8,0},{12,4},{16,24},{20,28},{24,16},{28,20},{1,9},{5... | collective-permute-start | bytes 884744 | tf_op jit(solution)/shard_map/ppermute | solution.py:212
  29.5 1.5 %collective-permute-start.11 = (bf16[6,4,48,128]{3,2,1,0:T(8,128)(2,1)S(1)}, bf16[6,4,48,128]{3,2,1,0:T(8,128)(2,1)S(1)}, u32[]{:S(2)}, u32[]{:S(2)}) collective-permute-start(bf16[6,4,48,128]{3,2,1,0:T(8,128)(2,1)S(1)} %get-tuple-element.40), channel_id=1, source_target_pairs={{0,16},{4,20},{8,24},{12,28},{16,0},{20,4},{24,8},{28,12},{1,17},{... | collective-permute-start | bytes 884744 | tf_op jit(solution)/shard_map/ppermute | solution.py:212
  31.0 4.2 %collective-permute-start.3 = (bf16[4,4,48,128]{3,2,1,0:T(8,128)(2,1)S(1)}, bf16[4,4,48,128]{3,2,1,0:T(8,128)(2,1)S(1)}, u32[]{:S(2)}, u32[]{:S(2)}) collective-permute-start(bf16[4,4,48,128]{3,2,1,0:T(8,128)(2,1)S(1)} %get-tuple-element.33.refs_0_), channel_id=1, source_target_pairs={{0,2},{1,3},{2,0},{3,1},{4,6},{5,7},{6,4},{7,5},{8,10},{9,11},{10,... | collective-permute-start | bytes 589832 | tf_op jit(solution)/shard_map/ppermute | solution.py:212
  35.2 0.5 collective-permute-start.12
  35.7 5.3 %collective-permute-done.14.refs_3_ = bf16[4,4,48,128]{3,2,1,0:T(8,128)(2,1)S(1)} collective-permute-done((bf16[4,4,48,128]{3,2,1,0:T(8,128)(2,1)S(1)}, bf16[4,4,48,128]{3,2,1,0:T(8,128)(2,1)S(1)}, u32[]{:S(2)}, u32[]{:S(2)}) %collective-permute-start.14) | collective-permute-done | bytes 196640 | tf_op jit(solution)/shard_map/ppermute | solution.py:212
  41.1 2.4 %shard_map.66 = (bf16[6,4,48,128]{3,2,1,0:T(8,128)(2,1)S(1)}, bf16[6,4,48,128]{3,2,1,0:T(8,128)(2,1)S(1)}, bf16[6,4,48,128]{3,2,1,0:T(8,128)(2,1)S(1)}, bf16[6,4,48,128]{3,2,1,0:T(8,128)(2,1)S(1)}) custom-call(s32[4]{0:T(128)S(1)} %pad_add_fusion.where_ref, bf16[4,4,48,128]{3,2,1,0:T(8,128)(2,1)S(1)} %get-tuple-element.32.refs_0_, ...), custom_call_target="tpu_custom_call" | custom-call | bytes 3000000 | tf_op jit(solution)/shard_map/pallas_call | solution.py:243
  43.5 0.1 collective-permute-start.16
  43.7 3.4 %collective-permute-start.18 = (bf16[6,4,48,128]{3,2,1,0:T(8,128)(2,1)S(1)}, bf16[6,4,48,128]{3,2,1,0:T(8,128)(2,1)S(1)}, u32[]{:S(2)}, u32[]{:S(2)}) collective-permute-start(bf16[6,4,48,128]{3,2,1,0:T(8,128)(2,1)S(1)} %get-tuple-element.45), channel_id=1, source_target_pairs={{0,24},{4,28},{8,16},{12,20},{16,8},{20,12},{24,0},{28,4},{1,25},{... | collective-permute-start | bytes 884744 | tf_op jit(solution)/shard_map/ppermute | solution.py:212
  47.1 2.0 %collective-permute-start.4 = (bf16[4,4,48,128]{3,2,1,0:T(8,128)(2,1)S(1)}, bf16[4,4,48,128]{3,2,1,0:T(8,128)(2,1)S(1)}, u32[]{:S(2)}, u32[]{:S(2)}) collective-permute-start(bf16[4,4,48,128]{3,2,1,0:T(8,128)(2,1)S(1)} %collective-permute-done.3.refs_2_), channel_id=1, source_target_pairs={{0,1},{1,0},{2,3},{3,2},{4,5},{5,4},{6,7},{7,6},{8,9},{9,8},{10,11... | collective-permute-start | bytes 589832 | tf_op jit(solution)/shard_map/ppermute | solution.py:212
  49.1 1.6 %shard_map.67 = bf16[4,4,4,48,128]{4,3,2,1,0:T(8,128)(2,1)S(1)} custom-call(s32[4]{0:T(128)S(1)} %pad_add_fusion.where_ref, bf16[6,4,48,128]{3,2,1,0:T(8,128)(2,1)S(1)} %get-tuple-element.46.refs_0_, bf16[6,4,48,128]{3,2,1,0:T(8,128)(2,1)S(1)} %collective-permute-done.10.refs_1_, bf16[6,4,48,128]{3,2,1,0:T(8,128)(2,1)S(1)} %collective-permute-done.11.refs_2_, ...), custom_call_target="tpu_custom_call" | custom-call | bytes 2000000 | tf_op jit(solution)/shard_map/pallas_call | solution.py:285
  50.9 1.9 %collective-permute-done.4.refs_3_ = bf16[4,4,48,128]{3,2,1,0:T(8,128)(2,1)S(1)} collective-permute-done((bf16[4,4,48,128]{3,2,1,0:T(8,128)(2,1)S(1)}, bf16[4,4,48,128]{3,2,1,0:T(8,128)(2,1)S(1)}, u32[]{:S(2)}, u32[]{:S(2)}) %collective-permute-start.4) | collective-permute-done | bytes 196640 | tf_op jit(solution)/shard_map/ppermute | solution.py:212
  52.8 2.4 %shard_map.64 = (bf16[6,4,48,128]{3,2,1,0:T(8,128)(2,1)S(1)}, bf16[6,4,48,128]{3,2,1,0:T(8,128)(2,1)S(1)}, bf16[6,4,48,128]{3,2,1,0:T(8,128)(2,1)S(1)}, bf16[6,4,48,128]{3,2,1,0:T(8,128)(2,1)S(1)}) custom-call(s32[4]{0:T(128)S(1)} %pad_add_fusion.where_ref, bf16[4,4,48,128]{3,2,1,0:T(8,128)(2,1)S(1)} %get-tuple-element.33.refs_0_, ...), custom_call_target="tpu_custom_call" | custom-call | bytes 3000000 | tf_op jit(solution)/shard_map/pallas_call | solution.py:243
  55.2 1.6 %shard_map.70 = bf16[4,4,4,48,128]{4,3,2,1,0:T(8,128)(2,1)S(1)} custom-call(s32[4]{0:T(128)S(1)} %pad_add_fusion.where_ref, bf16[6,4,48,128]{3,2,1,0:T(8,128)(2,1)S(1)} %get-tuple-element.51.refs_0_, bf16[6,4,48,128]{3,2,1,0:T(8,128)(2,1)S(1)} %collective-permute-done.16.refs_1_, bf16[6,4,48,128]{3,2,1,0:T(8,128)(2,1)S(1)} %collective-permute-done.17.refs_2_, ...), custom_call_target="tpu_custom_call" | custom-call | bytes 2000000 | tf_op jit(solution)/shard_map/pallas_call | solution.py:285
  57.0 0.9 %shard_map.68 = (bf16[2,8,128,256]{3,2,1,0:T(8,128)(2,1)S(1)}, bf16[2,144,144]{2,1,0:T(8,128)(2,1)S(1)}) custom-call(s32[4]{0:T(128)S(1)} %pad_add_fusion.where_ref, s32[8]{0:T(128)S(1)} %copy-done.3, s32[8,5]{1,0:T(8,128)S(1)} %copy-done.2, bf16[8,5,128,128]{3,2,1,0:T(8,128)(2,1)S(1)} %copy-done, bf16[137,8,137]{2,1,0:T(8,128)(2,1)S(1)} %bitcast.6), custom_call_target="tpu_custom_call" | custom-call | bytes 4000000 | tf_op jit(solution)/shard_map/pallas_call | solution.py:55
  57.9 2.3 %collective-permute-start.5 = (bf16[6,4,48,128]{3,2,1,0:T(8,128)(2,1)S(1)}, bf16[6,4,48,128]{3,2,1,0:T(8,128)(2,1)S(1)}, u32[]{:S(2)}, u32[]{:S(2)}) collective-permute-start(bf16[6,4,48,128]{3,2,1,0:T(8,128)(2,1)S(1)} %get-tuple-element.35), channel_id=1, source_target_pairs={{0,8},{4,12},{8,0},{12,4},{16,24},{20,28},{24,16},{28,20},{1,9},{5... | collective-permute-start | bytes 884744 | tf_op jit(solution)/shard_map/ppermute | solution.py:212
  60.2 1.5 %collective-permute-start.7 = (bf16[6,4,48,128]{3,2,1,0:T(8,128)(2,1)S(1)}, bf16[6,4,48,128]{3,2,1,0:T(8,128)(2,1)S(1)}, u32[]{:S(2)}, u32[]{:S(2)}) collective-permute-start(bf16[6,4,48,128]{3,2,1,0:T(8,128)(2,1)S(1)} %get-tuple-element.37), channel_id=1, source_target_pairs={{0,24},{4,28},{8,16},{12,20},{16,8},{20,12},{24,0},{28,4},{1,25},{... | collective-permute-start | bytes 884744 | tf_op jit(solution)/shard_map/ppermute | solution.py:212
  61.7 3.9 %shard_map.69.refs_10_ = bf16[2,2,16,48,256]{4,3,2,1,0:T(8,128)(2,1)S(1)} custom-call(s32[4]{0:T(128)S(1)} %pad_add_fusion.where_ref, s32[8]{0:T(128)S(1)} %copy-done.3, f32[3,8]{1,0:T(4,128)S(1)} %bitcast.10, bf16[6,4,48,128]{3,2,1,0:T(8,128)(2,1)S(1)} %get-tuple-element.46.refs_0_, bf16[6,4,48,128]{3,2,1,0:T(8,128)(2,1)S(1)} %collective-permute-done.10.refs_1_, ...), custom_call_target="tpu_custom_call" | custom-call | flops 2000000000 | bytes 8000000 | tf_op jit(solution)/shard_map/pallas_call | solution.py:175
  65.7 3.9 %shard_map.71.refs_11_ = bf16[2,2,16,48,256]{4,3,2,1,0:T(8,128)(2,1)S(1)} custom-call(s32[4]{0:T(128)S(1)} %pad_add_fusion.where_ref, s32[8]{0:T(128)S(1)} %copy-done.3, f32[3,8]{1,0:T(4,128)S(1)} %bitcast.11, bf16[6,4,48,128]{3,2,1,0:T(8,128)(2,1)S(1)} %get-tuple-element.51.refs_0_, bf16[6,4,48,128]{3,2,1,0:T(8,128)(2,1)S(1)} %collective-permute-done.16.refs_1_, ...), custom_call_target="tpu_custom_call" | custom-call | flops 2000000000 | bytes 8000000 | tf_op jit(solution)/shard_map/pallas_call | solution.py:175
  69.6 6.0 %collective-permute-done.6.refs_2_ = bf16[6,4,48,128]{3,2,1,0:T(8,128)(2,1)S(1)} collective-permute-done((bf16[6,4,48,128]{3,2,1,0:T(8,128)(2,1)S(1)}, bf16[6,4,48,128]{3,2,1,0:T(8,128)(2,1)S(1)}, u32[]{:S(2)}, u32[]{:S(2)}) %collective-permute-start.6) | collective-permute-done | bytes 294944 | tf_op jit(solution)/shard_map/ppermute | solution.py:212
  75.6 0.5 collective-permute-start.22
  76.1 1.1 %collective-permute-done.21.refs_5_ = bf16[6,4,48,128]{3,2,1,0:T(8,128)(2,1)S(1)} collective-permute-done((bf16[6,4,48,128]{3,2,1,0:T(8,128)(2,1)S(1)}, bf16[6,4,48,128]{3,2,1,0:T(8,128)(2,1)S(1)}, u32[]{:S(2)}, u32[]{:S(2)}) %collective-permute-start.21) | collective-permute-done | bytes 294944 | tf_op jit(solution)/shard_map/ppermute | solution.py:212
  77.2 0.4 collective-permute-done.22.refs_6_
  77.6 0.4 collective-permute-done.23.refs_7_
  78.0 9.6 %shard_map.72 = bf16[2,2,137,32,128]{4,3,2,1,0:T(8,128)(2,1)} custom-call(s32[4]{0:T(128)S(1)} %pad_add_fusion.where_ref, s32[8]{0:T(128)S(1)} %copy-done.3, f32[3,8]{1,0:T(4,128)S(1)} %bitcast.12, bf16[6,4,48,128]{3,2,1,0:T(8,128)(2,1)S(1)} %get-tuple-element.34.refs_0_, bf16[6,4,48,128]{3,2,1,0:T(8,128)(2,1)S(1)} %collective-permute-done.5.refs_1_, ...), custom_call_target="tpu_custom_call" | custom-call | flops 4000000000 | bytes 12000000 | tf_op jit(solution)/shard_map/pallas_call | solution.py:193
  (38 shorter events, 0.4 us)
Async XLA Ops:
  1.4 13.3 %collective-permute-start = (bf16[4,4,48,128]{3,2,1,0:T(8,128)(2,1)S(1)}, bf16[4,4,48,128]{3,2,1,0:T(8,128)(2,1)S(1)}, u32[]{:S(2)}, u32[]{:S(2)}) collective-permute-start(bf16[4,4,48,128]{3,2,1,0:T(8,128)(2,1)S(1)} %get-tuple-element.59.refs_0_), channel_id=1, source_target_pairs={{0,2},{1,3},{2,0},{3,1},{4,6},{5,7},{6,4},{7,5},{8,10},{9,11},{10,... | collective-permute-start | bytes 589832 | tf_op jit(solution)/shard_map/ppermute | solution.py:212
  5.5 13.3 %collective-permute-start.8 = (bf16[4,4,48,128]{3,2,1,0:T(8,128)(2,1)S(1)}, bf16[4,4,48,128]{3,2,1,0:T(8,128)(2,1)S(1)}, u32[]{:S(2)}, u32[]{:S(2)}) collective-permute-start(bf16[4,4,48,128]{3,2,1,0:T(8,128)(2,1)S(1)} %get-tuple-element.59.refs_0_), channel_id=1, source_target_pairs={{0,1},{1,0},{2,3},{3,2},{4,5},{5,4},{6,7},{7,6},{8,9},{9,8},{10,11... | collective-permute-start | bytes 589832 | tf_op jit(solution)/shard_map/ppermute | solution.py:212
  14.8 11.3 %collective-permute-start.9 = (bf16[4,4,48,128]{3,2,1,0:T(8,128)(2,1)S(1)}, bf16[4,4,48,128]{3,2,1,0:T(8,128)(2,1)S(1)}, u32[]{:S(2)}, u32[]{:S(2)}) collective-permute-start(bf16[4,4,48,128]{3,2,1,0:T(8,128)(2,1)S(1)} %collective-permute-done.refs_2_), channel_id=1, source_target_pairs={{0,1},{1,0},{2,3},{3,2},{4,5},{5,4},{6,7},{7,6},{8,9},{9,8},{10,11... | collective-permute-start | bytes 589832 | tf_op jit(solution)/shard_map/ppermute | solution.py:212
  15.4 15.6 %collective-permute-start.1 = (bf16[4,4,48,128]{3,2,1,0:T(8,128)(2,1)S(1)}, bf16[4,4,48,128]{3,2,1,0:T(8,128)(2,1)S(1)}, u32[]{:S(2)}, u32[]{:S(2)}) collective-permute-start(bf16[4,4,48,128]{3,2,1,0:T(8,128)(2,1)S(1)} %get-tuple-element.32.refs_0_), channel_id=1, source_target_pairs={{0,2},{1,3},{2,0},{3,1},{4,6},{5,7},{6,4},{7,5},{8,10},{9,11},{10,... | collective-permute-start | bytes 589832 | tf_op jit(solution)/shard_map/ppermute | solution.py:212
  18.7 16.5 %collective-permute-start.13 = (bf16[4,4,48,128]{3,2,1,0:T(8,128)(2,1)S(1)}, bf16[4,4,48,128]{3,2,1,0:T(8,128)(2,1)S(1)}, u32[]{:S(2)}, u32[]{:S(2)}) collective-permute-start(bf16[4,4,48,128]{3,2,1,0:T(8,128)(2,1)S(1)} %get-tuple-element.32.refs_0_), channel_id=1, source_target_pairs={{0,1},{1,0},{2,3},{3,2},{4,5},{5,4},{6,7},{7,6},{8,9},{9,8},{10,11... | collective-permute-start | bytes 589832 | tf_op jit(solution)/shard_map/ppermute | solution.py:212
  28.5 15.2 %collective-permute-start.10 = (bf16[6,4,48,128]{3,2,1,0:T(8,128)(2,1)S(1)}, bf16[6,4,48,128]{3,2,1,0:T(8,128)(2,1)S(1)}, u32[]{:S(2)}, u32[]{:S(2)}) collective-permute-start(bf16[6,4,48,128]{3,2,1,0:T(8,128)(2,1)S(1)} %get-tuple-element.39), channel_id=1, source_target_pairs={{0,8},{4,12},{8,0},{12,4},{16,24},{20,28},{24,16},{28,20},{1,9},{5... | collective-permute-start | bytes 884744 | tf_op jit(solution)/shard_map/ppermute | solution.py:212
  29.5 14.2 %collective-permute-start.11 = (bf16[6,4,48,128]{3,2,1,0:T(8,128)(2,1)S(1)}, bf16[6,4,48,128]{3,2,1,0:T(8,128)(2,1)S(1)}, u32[]{:S(2)}, u32[]{:S(2)}) collective-permute-start(bf16[6,4,48,128]{3,2,1,0:T(8,128)(2,1)S(1)} %get-tuple-element.40), channel_id=1, source_target_pairs={{0,16},{4,20},{8,24},{12,28},{16,0},{20,4},{24,8},{28,12},{1,17},{... | collective-permute-start | bytes 884744 | tf_op jit(solution)/shard_map/ppermute | solution.py:212
  31.0 10.1 %collective-permute-start.14 = (bf16[4,4,48,128]{3,2,1,0:T(8,128)(2,1)S(1)}, bf16[4,4,48,128]{3,2,1,0:T(8,128)(2,1)S(1)}, u32[]{:S(2)}, u32[]{:S(2)}) collective-permute-start(bf16[4,4,48,128]{3,2,1,0:T(8,128)(2,1)S(1)} %collective-permute-done.1.refs_2_), channel_id=1, source_target_pairs={{0,1},{1,0},{2,3},{3,2},{4,5},{5,4},{6,7},{7,6},{8,9},{9,8},{10,11... | collective-permute-start | bytes 589832 | tf_op jit(solution)/shard_map/ppermute | solution.py:212
  31.0 12.5 %collective-permute-start.3 = (bf16[4,4,48,128]{3,2,1,0:T(8,128)(2,1)S(1)}, bf16[4,4,48,128]{3,2,1,0:T(8,128)(2,1)S(1)}, u32[]{:S(2)}, u32[]{:S(2)}) collective-permute-start(bf16[4,4,48,128]{3,2,1,0:T(8,128)(2,1)S(1)} %get-tuple-element.33.refs_0_), channel_id=1, source_target_pairs={{0,2},{1,3},{2,0},{3,1},{4,6},{5,7},{6,4},{7,5},{8,10},{9,11},{10,... | collective-permute-start | bytes 589832 | tf_op jit(solution)/shard_map/ppermute | solution.py:212
  35.2 11.9 %collective-permute-start.12 = (bf16[6,4,48,128]{3,2,1,0:T(8,128)(2,1)S(1)}, bf16[6,4,48,128]{3,2,1,0:T(8,128)(2,1)S(1)}, u32[]{:S(2)}, u32[]{:S(2)}) collective-permute-start(bf16[6,4,48,128]{3,2,1,0:T(8,128)(2,1)S(1)} %get-tuple-element.41), channel_id=1, source_target_pairs={{0,24},{4,28},{8,16},{12,20},{16,8},{20,12},{24,0},{28,4},{1,25},{... | collective-permute-start | bytes 884744 | tf_op jit(solution)/shard_map/ppermute | solution.py:212
  41.1 9.7 %collective-permute-start.2 = (bf16[4,4,48,128]{3,2,1,0:T(8,128)(2,1)S(1)}, bf16[4,4,48,128]{3,2,1,0:T(8,128)(2,1)S(1)}, u32[]{:S(2)}, u32[]{:S(2)}) collective-permute-start(bf16[4,4,48,128]{3,2,1,0:T(8,128)(2,1)S(1)} %get-tuple-element.33.refs_0_), channel_id=1, source_target_pairs={{0,1},{1,0},{2,3},{3,2},{4,5},{5,4},{6,7},{7,6},{8,9},{9,8},{10,11... | collective-permute-start | bytes 589832 | tf_op jit(solution)/shard_map/ppermute | solution.py:212
  43.5 11.7 %collective-permute-start.16 = (bf16[6,4,48,128]{3,2,1,0:T(8,128)(2,1)S(1)}, bf16[6,4,48,128]{3,2,1,0:T(8,128)(2,1)S(1)}, u32[]{:S(2)}, u32[]{:S(2)}) collective-permute-start(bf16[6,4,48,128]{3,2,1,0:T(8,128)(2,1)S(1)} %get-tuple-element.43), channel_id=1, source_target_pairs={{0,8},{4,12},{8,0},{12,4},{16,24},{20,28},{24,16},{28,20},{1,9},{5... | collective-permute-start | bytes 884744 | tf_op jit(solution)/shard_map/ppermute | solution.py:212
  43.7 11.6 %collective-permute-start.17 = (bf16[6,4,48,128]{3,2,1,0:T(8,128)(2,1)S(1)}, bf16[6,4,48,128]{3,2,1,0:T(8,128)(2,1)S(1)}, u32[]{:S(2)}, u32[]{:S(2)}) collective-permute-start(bf16[6,4,48,128]{3,2,1,0:T(8,128)(2,1)S(1)} %get-tuple-element.44), channel_id=1, source_target_pairs={{0,16},{4,20},{8,24},{12,28},{16,0},{20,4},{24,8},{28,12},{1,17},{... | collective-permute-start | bytes 884744 | tf_op jit(solution)/shard_map/ppermute | solution.py:212
  43.7 11.5 %collective-permute-start.18 = (bf16[6,4,48,128]{3,2,1,0:T(8,128)(2,1)S(1)}, bf16[6,4,48,128]{3,2,1,0:T(8,128)(2,1)S(1)}, u32[]{:S(2)}, u32[]{:S(2)}) collective-permute-start(bf16[6,4,48,128]{3,2,1,0:T(8,128)(2,1)S(1)} %get-tuple-element.45), channel_id=1, source_target_pairs={{0,24},{4,28},{8,16},{12,20},{16,8},{20,12},{24,0},{28,4},{1,25},{... | collective-permute-start | bytes 884744 | tf_op jit(solution)/shard_map/ppermute | solution.py:212
  47.1 5.7 %collective-permute-start.4 = (bf16[4,4,48,128]{3,2,1,0:T(8,128)(2,1)S(1)}, bf16[4,4,48,128]{3,2,1,0:T(8,128)(2,1)S(1)}, u32[]{:S(2)}, u32[]{:S(2)}) collective-permute-start(bf16[4,4,48,128]{3,2,1,0:T(8,128)(2,1)S(1)} %collective-permute-done.3.refs_2_), channel_id=1, source_target_pairs={{0,1},{1,0},{2,3},{3,2},{4,5},{5,4},{6,7},{7,6},{8,9},{9,8},{10,11... | collective-permute-start | bytes 589832 | tf_op jit(solution)/shard_map/ppermute | solution.py:212
  50.7 6.2 %copy-start = (bf16[8,5,128,128]{3,2,1,0:T(8,128)(2,1)S(1)}, bf16[8,5,128,128]{3,2,1,0:T(8,128)(2,1)}, u32[]{:S(2)}) copy-start(bf16[8,5,128,128]{3,2,1,0:T(8,128)(2,1)} %filter_ref.1) | copy-start | bytes 3932164
  50.7 6.2 %copy-start.1 = (bf16[8,137,137]{2,0,1:T(8,128)(2,1)S(1)}, bf16[8,137,137]{2,0,1:T(8,128)(2,1)}, u32[]{:S(2)}) copy-start(bf16[8,137,137]{2,0,1:T(8,128)(2,1)} %param.10) | copy-start | bytes 900916
  50.7 6.2 %copy-start.2 = (s32[8,5]{1,0:T(8,128)S(1)}, s32[8,5]{1,0:T(8,128)}, u32[]{:S(2)}) copy-start(s32[8,5]{1,0:T(8,128)} %offset_ref.1) | copy-start | bytes 484
  50.8 6.2 %copy-start.3 = (s32[8]{0:T(128)S(1)}, s32[8]{0:T(128)}, u32[]{:S(2)}) copy-start(s32[8]{0:T(128)} %slot_ref.7) | copy-start | bytes 100
  50.8 10.9 %collective-permute-start.15 = (bf16[4,4,4,48,128]{4,3,2,1,0:T(8,128)(2,1)S(1)}, bf16[4,4,4,48,128]{4,3,2,1,0:T(8,128)(2,1)S(1)}, u32[]{:S(2)}, u32[]{:S(2)}) collective-permute-start(bf16[4,4,4,48,128]{4,3,2,1,0:T(8,128)(2,1)S(1)} %shard_map.67), channel_id=1, source_target_pairs={{0,4},{4,0},{8,12},{12,8},{16,20},{20,16},{24,28},{28,24},{1,5},{5... | collective-permute-start | bytes 2359304 | tf_op jit(solution)/shard_map/ppermute | solution.py:212
  55.2 6.5 %copy-start.4 = (f32[8,3]{0,1:T(4,128)S(1)}, f32[8,3]{0,1:T(4,128)}, u32[]{:S(2)}) copy-start(f32[8,3]{0,1:T(4,128)} %param.7) | copy-start | bytes 292
  56.9 8.8 %collective-permute-start.19 = (bf16[4,4,4,48,128]{4,3,2,1,0:T(8,128)(2,1)S(1)}, bf16[4,4,4,48,128]{4,3,2,1,0:T(8,128)(2,1)S(1)}, u32[]{:S(2)}, u32[]{:S(2)}) collective-permute-start(bf16[4,4,4,48,128]{4,3,2,1,0:T(8,128)(2,1)S(1)} %shard_map.70), channel_id=1, source_target_pairs={{0,4},{4,0},{8,12},{12,8},{16,20},{20,16},{24,28},{28,24},{1,5},{5... | collective-permute-start | bytes 2359304 | tf_op jit(solution)/shard_map/ppermute | solution.py:212
  57.9 11.7 %collective-permute-start.5 = (bf16[6,4,48,128]{3,2,1,0:T(8,128)(2,1)S(1)}, bf16[6,4,48,128]{3,2,1,0:T(8,128)(2,1)S(1)}, u32[]{:S(2)}, u32[]{:S(2)}) collective-permute-start(bf16[6,4,48,128]{3,2,1,0:T(8,128)(2,1)S(1)} %get-tuple-element.35), channel_id=1, source_target_pairs={{0,8},{4,12},{8,0},{12,4},{16,24},{20,28},{24,16},{28,20},{1,9},{5... | collective-permute-start | bytes 884744 | tf_op jit(solution)/shard_map/ppermute | solution.py:212
  60.2 15.4 %collective-permute-start.6 = (bf16[6,4,48,128]{3,2,1,0:T(8,128)(2,1)S(1)}, bf16[6,4,48,128]{3,2,1,0:T(8,128)(2,1)S(1)}, u32[]{:S(2)}, u32[]{:S(2)}) collective-permute-start(bf16[6,4,48,128]{3,2,1,0:T(8,128)(2,1)S(1)} %get-tuple-element.36), channel_id=1, source_target_pairs={{0,16},{4,20},{8,24},{12,28},{16,0},{20,4},{24,8},{28,12},{1,17},{... | collective-permute-start | bytes 884744 | tf_op jit(solution)/shard_map/ppermute | solution.py:212
  60.2 15.4 %collective-permute-start.7 = (bf16[6,4,48,128]{3,2,1,0:T(8,128)(2,1)S(1)}, bf16[6,4,48,128]{3,2,1,0:T(8,128)(2,1)S(1)}, u32[]{:S(2)}, u32[]{:S(2)}) collective-permute-start(bf16[6,4,48,128]{3,2,1,0:T(8,128)(2,1)S(1)} %get-tuple-element.37), channel_id=1, source_target_pairs={{0,24},{4,28},{8,16},{12,20},{16,8},{20,12},{24,0},{28,4},{1,25},{... | collective-permute-start | bytes 884744 | tf_op jit(solution)/shard_map/ppermute | solution.py:212
  61.7 14.4 %collective-permute-start.20 = (bf16[6,4,48,128]{3,2,1,0:T(8,128)(2,1)S(1)}, bf16[6,4,48,128]{3,2,1,0:T(8,128)(2,1)S(1)}, u32[]{:S(2)}, u32[]{:S(2)}) collective-permute-start(bf16[6,4,48,128]{3,2,1,0:T(8,128)(2,1)S(1)} %get-tuple-element.34.refs_0_), channel_id=1, source_target_pairs={{0,4},{4,0},{8,12},{12,8},{16,20},{20,16},{24,28},{28,24},{1,5},{5... | collective-permute-start | bytes 884744 | tf_op jit(solution)/shard_map/ppermute | solution.py:212
  75.6 1.6 %collective-permute-start.21 = (bf16[6,4,48,128]{3,2,1,0:T(8,128)(2,1)S(1)}, bf16[6,4,48,128]{3,2,1,0:T(8,128)(2,1)S(1)}, u32[]{:S(2)}, u32[]{:S(2)}) collective-permute-start(bf16[6,4,48,128]{3,2,1,0:T(8,128)(2,1)S(1)} %collective-permute-done.5.refs_1_), channel_id=1, source_target_pairs={{0,4},{4,0},{8,12},{12,8},{16,20},{20,16},{24,28},{28,24},{1,5},{5... | collective-permute-start | bytes 884744 | tf_op jit(solution)/shard_map/ppermute | solution.py:212
  75.6 2.0 %collective-permute-start.22 = (bf16[6,4,48,128]{3,2,1,0:T(8,128)(2,1)S(1)}, bf16[6,4,48,128]{3,2,1,0:T(8,128)(2,1)S(1)}, u32[]{:S(2)}, u32[]{:S(2)}) collective-permute-start(bf16[6,4,48,128]{3,2,1,0:T(8,128)(2,1)S(1)} %collective-permute-done.6.refs_2_), channel_id=1, source_target_pairs={{0,4},{4,0},{8,12},{12,8},{16,20},{20,16},{24,28},{28,24},{1,5},{5... | collective-permute-start | bytes 884744 | tf_op jit(solution)/shard_map/ppermute | solution.py:212
  76.1 1.9 %collective-permute-start.23 = (bf16[6,4,48,128]{3,2,1,0:T(8,128)(2,1)S(1)}, bf16[6,4,48,128]{3,2,1,0:T(8,128)(2,1)S(1)}, u32[]{:S(2)}, u32[]{:S(2)}) collective-permute-start(bf16[6,4,48,128]{3,2,1,0:T(8,128)(2,1)S(1)} %collective-permute-done.7.refs_3_), channel_id=1, source_target_pairs={{0,4},{4,0},{8,12},{12,8},{16,20},{20,16},{24,28},{28,24},{1,5},{5... | collective-permute-start | bytes 884744 | tf_op jit(solution)/shard_map/ppermute | solution.py:212

commit v6 on v5

--- a/solution.py
+++ b/solution.py
@@ -81,11 +81,6 @@
     shard_rows, per_source, _, c = kept[0].shape
     half = chips * per_source
     first = lax.rem(place, 2) * ((shard_rows - 2) // 2) + r
-
-    def row_of(side, k, i, n):
-        if side == 0:
-            return kept[k][first + i, n]
-        return got[0][k, r + i, n] if len(got) == 1 else got[k][first + i, n]
 
     for k in range(chips):
         for side in range(2):
@@ -143,14 +138,15 @@
     padded = vert_ref.shape[1]
     pitch = spread.shape[0] // padded
     step = 4
+    later = []
     for j in range(0, half, step):
-        later = filtered(window, filt_ref[0], j, step)
-        for i in range(step):
-            column = [d[0, 0, j + i] for d in done] + [later[i * depth : (i + 1) * depth]]
-            column = jnp.concatenate(column, axis=0)
-            mixed = jnp.dot(vert_ref[0], column, preferred_element_type=jnp.float32)
-            for h in range(2):
-                spread[pl.ds(2 * (j + i) + h, padded, stride=pitch), :] = mixed[:, h * c : (h + 1) * c]
+        later.append(filtered(window, filt_ref[0], j, step))
+    for j in range(half):
+        here = later[j // step][j % step * depth : (j % step + 1) * depth]
+        column = jnp.concatenate([d[0, 0, j] for d in done] + [here], axis=0)
+        mixed = jnp.dot(vert_ref[0], column, preferred_element_type=jnp.float32)
+        for h in range(2):
+            spread[pl.ds(2 * j + h, padded, stride=pitch), :] = mixed[:, h * c : (h + 1) * c]
     for m in range(levels):
         out_ref[0, 0, m] = spread[m * pitch : m * pitch + blocks].astype(jnp.bfloat16)
 
@@ -317,6 +313,7 @@
     pieces = []
     for part in parts:
         pieces.append(along_lat(after(part, pieces[-1][2]) if pieces else part))
+    pieces[0], filt, vert = lax.optimization_barrier((pieces[0], filt, vert))
     sends = [sorted_rows(where, piece) for piece in pieces]
     kept = [along_lon(send) for send in sends]
     done = []

time: 88.1 us -> 84.7 us (0.961)
  Pallas kernels: 28.9 us -> 26.3 us
  waiting for transfers between devices: 30 us -> 29.1 us
    pallas_call x1, Pallas kernels: 9.56 us -> 6.98 us  [last_part(): pl.pallas_call(functools.partial(last_kernel, len(kept)), grid=(rows, gro...]
    ppermute x24, waiting for transfers between devices: 30 us -> 29.1 us  [swapped(): lax.ppermute(value, axis, [(i, i ^ by) for i in range(lax.axis_size(axis))])]
  transfers between devices with their start and end apart: 24 -> 24, of which waited for: 8 -> 8; matrix products, arithmetic and copies ran while one was open for 0% -> 0% of each run, Pallas kernels for 22% -> 23%
where the time goes in v6:
time: 84.7 us; the launch traced here: 84.2 us
  waiting for transfers between devices  29.1 us (34%)
  starting transfers between devices  26.9 us (32%)
  Pallas kernels  26.3 us (31%)
  local copies, waits for them, and re-layouts  1.58 us (2%)
    ppermute x24, waiting for transfers between devices, swapped(): lax.ppermute(value, axis, [(i, i ^ by) for i in range(lax.axis_size(axis))])  29.1 us
    ppermute x24, starting transfers between devices, swapped(): lax.ppermute(value, axis, [(i, i ^ by) for i in range(lax.axis_size(axis))])  26.9 us
    pallas_call x2, Pallas kernels, first_part(): pl.pallas_call(functools.partial(first_kernel, len(kept)), grid=(rows, gr...  7.84 us
    pallas_call x3, Pallas kernels, sorted_rows(): pl.pallas_call(sort_kernel, in_specs=[SCALAR] + [anywhere] * len(pieces),...  7.31 us
    pallas_call x1, Pallas kernels, last_part(): pl.pallas_call(functools.partial(last_kernel, len(kept)), grid=(rows, gro...  6.98 us
    pallas_call x2, Pallas kernels, given_rows(): pl.pallas_call(give_kernel, in_specs=[SCALAR] + [anywhere] * len(kept), o...  3.21 us
  transfers between devices with their start and end apart: 24, of which 8 were waited for; matrix products, arithmetic and copies ran while one was open for 0% of the time, Pallas kernels for 23%

profile of v6, /device:TPU:0, one launch (start us, length us, event | category | flops | bytes accessed | tf_op | source)
XLA Modules:
  0.0 84.2 jit_solution(1620742396612425481)
XLA Ops:
  0.0 1.5 %copy.9 = bf16[4,4,137,128]{3,2,1,0:T(8,128)(2,1)S(1)} copy(f32[4,4,137,128]{3,1,2,0:T(4,128)} %param.6) | data formatting | bytes 1683456 | tf_op args[0]
  1.6 4.1 %collective-permute-start = (bf16[4,4,48,128]{3,2,1,0:T(8,128)(2,1)S(1)}, bf16[4,4,48,128]{3,2,1,0:T(8,128)(2,1)S(1)}, u32[]{:S(2)}, u32[]{:S(2)}) collective-permute-start(bf16[4,4,48,128]{3,2,1,0:T(8,128)(2,1)S(1)} %get-tuple-element.46.refs_0_), channel_id=1, source_target_pairs={{0,2},{1,3},{2,0},{3,1},{4,6},{5,7},{6,4},{7,5},{8,10},{9,11},{10,... | collective-permute-start | bytes 589832 | tf_op jit(solution)/shard_map/ppermute | solution.py:208
  5.7 1.6 %collective-permute-start.8 = (bf16[4,4,48,128]{3,2,1,0:T(8,128)(2,1)S(1)}, bf16[4,4,48,128]{3,2,1,0:T(8,128)(2,1)S(1)}, u32[]{:S(2)}, u32[]{:S(2)}) collective-permute-start(bf16[4,4,48,128]{3,2,1,0:T(8,128)(2,1)S(1)} %get-tuple-element.46.refs_0_), channel_id=1, source_target_pairs={{0,1},{1,0},{2,3},{3,2},{4,5},{5,4},{6,7},{7,6},{8,9},{9,8},{10,11... | collective-permute-start | bytes 589832 | tf_op jit(solution)/shard_map/ppermute | solution.py:208
  7.3 7.6 %collective-permute-done.refs_2_ = bf16[4,4,48,128]{3,2,1,0:T(8,128)(2,1)S(1)} collective-permute-done((bf16[4,4,48,128]{3,2,1,0:T(8,128)(2,1)S(1)}, bf16[4,4,48,128]{3,2,1,0:T(8,128)(2,1)S(1)}, u32[]{:S(2)}, u32[]{:S(2)}) %collective-permute-start) | collective-permute-done | bytes 196640 | tf_op jit(solution)/shard_map/ppermute | solution.py:208
  14.9 0.6 collective-permute-start.9
  15.5 3.4 %collective-permute-start.1 = (bf16[4,4,48,128]{3,2,1,0:T(8,128)(2,1)S(1)}, bf16[4,4,48,128]{3,2,1,0:T(8,128)(2,1)S(1)}, u32[]{:S(2)}, u32[]{:S(2)}) collective-permute-start(bf16[4,4,48,128]{3,2,1,0:T(8,128)(2,1)S(1)} %get-tuple-element.38.refs_0_), channel_id=1, source_target_pairs={{0,2},{1,3},{2,0},{3,1},{4,6},{5,7},{6,4},{7,5},{8,10},{9,11},{10,... | collective-permute-start | bytes 589832 | tf_op jit(solution)/shard_map/ppermute | solution.py:208
  19.0 0.9 %shard_map.65 = (bf16[2,8,128,256]{3,2,1,0:T(8,128)(2,1)S(1)}, bf16[2,144,144]{2,1,0:T(8,128)(2,1)S(1)}) custom-call(s32[4]{0:T(128)S(1)} %pad_add_fusion.where_ref, s32[8]{0:T(128)S(1)} %copy-done.3, s32[8,5]{1,0:T(8,128)S(1)} %copy-done.2, bf16[8,5,128,128]{3,2,1,0:T(8,128)(2,1)S(1)} %copy-done, bf16[137,8,137]{2,1,0:T(8,128)(2,1)S(1)} %bitcast.6), custom_call_target="tpu_custom_call" | custom-call | bytes 4000000 | tf_op jit(solution)/shard_map/pallas_call | solution.py:55
  20.0 6.2 %collective-permute-done.9.refs_3_ = bf16[4,4,48,128]{3,2,1,0:T(8,128)(2,1)S(1)} collective-permute-done((bf16[4,4,48,128]{3,2,1,0:T(8,128)(2,1)S(1)}, bf16[4,4,48,128]{3,2,1,0:T(8,128)(2,1)S(1)}, u32[]{:S(2)}, u32[]{:S(2)}) %collective-permute-start.9) | collective-permute-done | bytes 196640 | tf_op jit(solution)/shard_map/ppermute | solution.py:208
  26.2 2.4 %shard_map.66 = (bf16[6,4,48,128]{3,2,1,0:T(8,128)(2,1)S(1)}, bf16[6,4,48,128]{3,2,1,0:T(8,128)(2,1)S(1)}, bf16[6,4,48,128]{3,2,1,0:T(8,128)(2,1)S(1)}, bf16[6,4,48,128]{3,2,1,0:T(8,128)(2,1)S(1)}) custom-call(s32[4]{0:T(128)S(1)} %pad_add_fusion.where_ref, bf16[4,4,48,128]{3,2,1,0:T(8,128)(2,1)S(1)} %get-tuple-element.46.refs_0_, ...), custom_call_target="tpu_custom_call" | custom-call | bytes 3000000 | tf_op jit(solution)/shard_map/pallas_call | solution.py:239
  28.7 1.0 %collective-permute-start.10 = (bf16[6,4,48,128]{3,2,1,0:T(8,128)(2,1)S(1)}, bf16[6,4,48,128]{3,2,1,0:T(8,128)(2,1)S(1)}, u32[]{:S(2)}, u32[]{:S(2)}) collective-permute-start(bf16[6,4,48,128]{3,2,1,0:T(8,128)(2,1)S(1)} %get-tuple-element.51), channel_id=1, source_target_pairs={{0,8},{4,12},{8,0},{12,4},{16,24},{20,28},{24,16},{28,20},{1,9},{5... | collective-permute-start | bytes 884744 | tf_op jit(solution)/shard_map/ppermute | solution.py:208
  29.6 1.5 %collective-permute-start.11 = (bf16[6,4,48,128]{3,2,1,0:T(8,128)(2,1)S(1)}, bf16[6,4,48,128]{3,2,1,0:T(8,128)(2,1)S(1)}, u32[]{:S(2)}, u32[]{:S(2)}) collective-permute-start(bf16[6,4,48,128]{3,2,1,0:T(8,128)(2,1)S(1)} %get-tuple-element.52), channel_id=1, source_target_pairs={{0,16},{4,20},{8,24},{12,28},{16,0},{20,4},{24,8},{28,12},{1,17},{... | collective-permute-start | bytes 884744 | tf_op jit(solution)/shard_map/ppermute | solution.py:208
  31.2 4.2 %collective-permute-start.3 = (bf16[4,4,48,128]{3,2,1,0:T(8,128)(2,1)S(1)}, bf16[4,4,48,128]{3,2,1,0:T(8,128)(2,1)S(1)}, u32[]{:S(2)}, u32[]{:S(2)}) collective-permute-start(bf16[4,4,48,128]{3,2,1,0:T(8,128)(2,1)S(1)} %get-tuple-element.39.refs_0_), channel_id=1, source_target_pairs={{0,2},{1,3},{2,0},{3,1},{4,6},{5,7},{6,4},{7,5},{8,10},{9,11},{10,... | collective-permute-start | bytes 589832 | tf_op jit(solution)/shard_map/ppermute | solution.py:208
  35.4 0.5 collective-permute-start.12
  35.9 5.3 %collective-permute-done.14.refs_3_ = bf16[4,4,48,128]{3,2,1,0:T(8,128)(2,1)S(1)} collective-permute-done((bf16[4,4,48,128]{3,2,1,0:T(8,128)(2,1)S(1)}, bf16[4,4,48,128]{3,2,1,0:T(8,128)(2,1)S(1)}, u32[]{:S(2)}, u32[]{:S(2)}) %collective-permute-start.14) | collective-permute-done | bytes 196640 | tf_op jit(solution)/shard_map/ppermute | solution.py:208
  41.2 2.4 %shard_map.67 = (bf16[6,4,48,128]{3,2,1,0:T(8,128)(2,1)S(1)}, bf16[6,4,48,128]{3,2,1,0:T(8,128)(2,1)S(1)}, bf16[6,4,48,128]{3,2,1,0:T(8,128)(2,1)S(1)}, bf16[6,4,48,128]{3,2,1,0:T(8,128)(2,1)S(1)}) custom-call(s32[4]{0:T(128)S(1)} %pad_add_fusion.where_ref, bf16[4,4,48,128]{3,2,1,0:T(8,128)(2,1)S(1)} %get-tuple-element.38.refs_0_, ...), custom_call_target="tpu_custom_call" | custom-call | bytes 3000000 | tf_op jit(solution)/shard_map/pallas_call | solution.py:239
  43.7 0.1 collective-permute-start.16
  43.9 3.4 %collective-permute-start.18 = (bf16[6,4,48,128]{3,2,1,0:T(8,128)(2,1)S(1)}, bf16[6,4,48,128]{3,2,1,0:T(8,128)(2,1)S(1)}, u32[]{:S(2)}, u32[]{:S(2)}) collective-permute-start(bf16[6,4,48,128]{3,2,1,0:T(8,128)(2,1)S(1)} %get-tuple-element.57), channel_id=1, source_target_pairs={{0,24},{4,28},{8,16},{12,20},{16,8},{20,12},{24,0},{28,4},{1,25},{... | collective-permute-start | bytes 884744 | tf_op jit(solution)/shard_map/ppermute | solution.py:208
  47.2 2.0 %collective-permute-start.4 = (bf16[4,4,48,128]{3,2,1,0:T(8,128)(2,1)S(1)}, bf16[4,4,48,128]{3,2,1,0:T(8,128)(2,1)S(1)}, u32[]{:S(2)}, u32[]{:S(2)}) collective-permute-start(bf16[4,4,48,128]{3,2,1,0:T(8,128)(2,1)S(1)} %collective-permute-done.3.refs_2_), channel_id=1, source_target_pairs={{0,1},{1,0},{2,3},{3,2},{4,5},{5,4},{6,7},{7,6},{8,9},{9,8},{10,11... | collective-permute-start | bytes 589832 | tf_op jit(solution)/shard_map/ppermute | solution.py:208
  49.3 1.6 %shard_map.68 = bf16[4,4,4,48,128]{4,3,2,1,0:T(8,128)(2,1)S(1)} custom-call(s32[4]{0:T(128)S(1)} %pad_add_fusion.where_ref, bf16[6,4,48,128]{3,2,1,0:T(8,128)(2,1)S(1)} %get-tuple-element.58.refs_0_, bf16[6,4,48,128]{3,2,1,0:T(8,128)(2,1)S(1)} %collective-permute-done.10.refs_1_, bf16[6,4,48,128]{3,2,1,0:T(8,128)(2,1)S(1)} %collective-permute-done.11.refs_2_, ...), custom_call_target="tpu_custom_call" | custom-call | bytes 2000000 | tf_op jit(solution)/shard_map/pallas_call | solution.py:281
  51.0 1.9 %collective-permute-done.4.refs_3_ = bf16[4,4,48,128]{3,2,1,0:T(8,128)(2,1)S(1)} collective-permute-done((bf16[4,4,48,128]{3,2,1,0:T(8,128)(2,1)S(1)}, bf16[4,4,48,128]{3,2,1,0:T(8,128)(2,1)S(1)}, u32[]{:S(2)}, u32[]{:S(2)}) %collective-permute-start.4) | collective-permute-done | bytes 196640 | tf_op jit(solution)/shard_map/ppermute | solution.py:208
  52.9 2.4 %shard_map.64 = (bf16[6,4,48,128]{3,2,1,0:T(8,128)(2,1)S(1)}, bf16[6,4,48,128]{3,2,1,0:T(8,128)(2,1)S(1)}, bf16[6,4,48,128]{3,2,1,0:T(8,128)(2,1)S(1)}, bf16[6,4,48,128]{3,2,1,0:T(8,128)(2,1)S(1)}) custom-call(s32[4]{0:T(128)S(1)} %pad_add_fusion.where_ref, bf16[4,4,48,128]{3,2,1,0:T(8,128)(2,1)S(1)} %get-tuple-element.39.refs_0_, ...), custom_call_target="tpu_custom_call" | custom-call | bytes 3000000 | tf_op jit(solution)/shard_map/pallas_call | solution.py:239
  55.4 1.6 %shard_map.70 = bf16[4,4,4,48,128]{4,3,2,1,0:T(8,128)(2,1)S(1)} custom-call(s32[4]{0:T(128)S(1)} %pad_add_fusion.where_ref, bf16[6,4,48,128]{3,2,1,0:T(8,128)(2,1)S(1)} %get-tuple-element.63.refs_0_, bf16[6,4,48,128]{3,2,1,0:T(8,128)(2,1)S(1)} %collective-permute-done.16.refs_1_, bf16[6,4,48,128]{3,2,1,0:T(8,128)(2,1)S(1)} %collective-permute-done.17.refs_2_, ...), custom_call_target="tpu_custom_call" | custom-call | bytes 2000000 | tf_op jit(solution)/shard_map/pallas_call | solution.py:281
  57.1 2.3 %collective-permute-start.5 = (bf16[6,4,48,128]{3,2,1,0:T(8,128)(2,1)S(1)}, bf16[6,4,48,128]{3,2,1,0:T(8,128)(2,1)S(1)}, u32[]{:S(2)}, u32[]{:S(2)}) collective-permute-start(bf16[6,4,48,128]{3,2,1,0:T(8,128)(2,1)S(1)} %get-tuple-element.41), channel_id=1, source_target_pairs={{0,8},{4,12},{8,0},{12,4},{16,24},{20,28},{24,16},{28,20},{1,9},{5... | collective-permute-start | bytes 884744 | tf_op jit(solution)/shard_map/ppermute | solution.py:208
  59.4 1.5 %collective-permute-start.7 = (bf16[6,4,48,128]{3,2,1,0:T(8,128)(2,1)S(1)}, bf16[6,4,48,128]{3,2,1,0:T(8,128)(2,1)S(1)}, u32[]{:S(2)}, u32[]{:S(2)}) collective-permute-start(bf16[6,4,48,128]{3,2,1,0:T(8,128)(2,1)S(1)} %get-tuple-element.43), channel_id=1, source_target_pairs={{0,24},{4,28},{8,16},{12,20},{16,8},{20,12},{24,0},{28,4},{1,25},{... | collective-permute-start | bytes 884744 | tf_op jit(solution)/shard_map/ppermute | solution.py:208
  60.9 3.9 %shard_map.69.refs_10_ = bf16[2,2,16,48,256]{4,3,2,1,0:T(8,128)(2,1)S(1)} custom-call(s32[4]{0:T(128)S(1)} %pad_add_fusion.where_ref, s32[8]{0:T(128)S(1)} %copy-done.3, f32[3,8]{1,0:T(4,128)S(1)} %bitcast.10, bf16[6,4,48,128]{3,2,1,0:T(8,128)(2,1)S(1)} %get-tuple-element.58.refs_0_, bf16[6,4,48,128]{3,2,1,0:T(8,128)(2,1)S(1)} %collective-permute-done.10.refs_1_, ...), custom_call_target="tpu_custom_call" | custom-call | flops 2000000000 | bytes 8000000 | tf_op jit(solution)/shard_map/pallas_call | solution.py:171
  64.9 3.9 %shard_map.71.refs_11_ = bf16[2,2,16,48,256]{4,3,2,1,0:T(8,128)(2,1)S(1)} custom-call(s32[4]{0:T(128)S(1)} %pad_add_fusion.where_ref, s32[8]{0:T(128)S(1)} %copy-done.3, f32[3,8]{1,0:T(4,128)S(1)} %bitcast.11, bf16[6,4,48,128]{3,2,1,0:T(8,128)(2,1)S(1)} %get-tuple-element.63.refs_0_, bf16[6,4,48,128]{3,2,1,0:T(8,128)(2,1)S(1)} %collective-permute-done.16.refs_1_, ...), custom_call_target="tpu_custom_call" | custom-call | flops 2000000000 | bytes 8000000 | tf_op jit(solution)/shard_map/pallas_call | solution.py:171
  68.8 6.0 %collective-permute-done.6.refs_2_ = bf16[6,4,48,128]{3,2,1,0:T(8,128)(2,1)S(1)} collective-permute-done((bf16[6,4,48,128]{3,2,1,0:T(8,128)(2,1)S(1)}, bf16[6,4,48,128]{3,2,1,0:T(8,128)(2,1)S(1)}, u32[]{:S(2)}, u32[]{:S(2)}) %collective-permute-start.6) | collective-permute-done | bytes 294944 | tf_op jit(solution)/shard_map/ppermute | solution.py:208
  74.8 0.5 collective-permute-start.22
  75.3 1.1 %collective-permute-done.21.refs_5_ = bf16[6,4,48,128]{3,2,1,0:T(8,128)(2,1)S(1)} collective-permute-done((bf16[6,4,48,128]{3,2,1,0:T(8,128)(2,1)S(1)}, bf16[6,4,48,128]{3,2,1,0:T(8,128)(2,1)S(1)}, u32[]{:S(2)}, u32[]{:S(2)}) %collective-permute-start.21) | collective-permute-done | bytes 294944 | tf_op jit(solution)/shard_map/ppermute | solution.py:208
  76.4 0.4 collective-permute-done.22.refs_6_
  76.8 0.4 collective-permute-done.23.refs_7_
  77.2 7.0 %shard_map.72 = bf16[2,2,137,32,128]{4,3,2,1,0:T(8,128)(2,1)} custom-call(s32[4]{0:T(128)S(1)} %pad_add_fusion.where_ref, s32[8]{0:T(128)S(1)} %copy-done.3, f32[3,8]{1,0:T(4,128)S(1)} %bitcast.12, bf16[6,4,48,128]{3,2,1,0:T(8,128)(2,1)S(1)} %get-tuple-element.40.refs_0_, bf16[6,4,48,128]{3,2,1,0:T(8,128)(2,1)S(1)} %collective-permute-done.5.refs_1_, ...), custom_call_target="tpu_custom_call" | custom-call | flops 4000000000 | bytes 12000000 | tf_op jit(solution)/shard_map/pallas_call | solution.py:189
  (38 shorter events, 0.4 us)
Async XLA Ops:
  0.0 19.0 %copy-start.3 = (s32[8]{0:T(128)S(1)}, s32[8]{0:T(128)}, u32[]{:S(2)}) copy-start(s32[8]{0:T(128)} %slot_ref.7) | copy-start | bytes 100
  0.0 19.0 %copy-start.1 = (bf16[8,137,137]{2,0,1:T(8,128)(2,1)S(1)}, bf16[8,137,137]{2,0,1:T(8,128)(2,1)}, u32[]{:S(2)}) copy-start(bf16[8,137,137]{2,0,1:T(8,128)(2,1)} %param.10) | copy-start | bytes 900916
  0.0 19.0 %copy-start = (bf16[8,5,128,128]{3,2,1,0:T(8,128)(2,1)S(1)}, bf16[8,5,128,128]{3,2,1,0:T(8,128)(2,1)}, u32[]{:S(2)}) copy-start(bf16[8,5,128,128]{3,2,1,0:T(8,128)(2,1)} %filter_ref.1) | copy-start | bytes 3932164
  0.0 19.0 %copy-start.2 = (s32[8,5]{1,0:T(8,128)S(1)}, s32[8,5]{1,0:T(8,128)}, u32[]{:S(2)}) copy-start(s32[8,5]{1,0:T(8,128)} %offset_ref.1) | copy-start | bytes 484
  1.6 13.3 %collective-permute-start = (bf16[4,4,48,128]{3,2,1,0:T(8,128)(2,1)S(1)}, bf16[4,4,48,128]{3,2,1,0:T(8,128)(2,1)S(1)}, u32[]{:S(2)}, u32[]{:S(2)}) collective-permute-start(bf16[4,4,48,128]{3,2,1,0:T(8,128)(2,1)S(1)} %get-tuple-element.46.refs_0_), channel_id=1, source_target_pairs={{0,2},{1,3},{2,0},{3,1},{4,6},{5,7},{6,4},{7,5},{8,10},{9,11},{10,... | collective-permute-start | bytes 589832 | tf_op jit(solution)/shard_map/ppermute | solution.py:208
  5.7 14.3 %collective-permute-start.8 = (bf16[4,4,48,128]{3,2,1,0:T(8,128)(2,1)S(1)}, bf16[4,4,48,128]{3,2,1,0:T(8,128)(2,1)S(1)}, u32[]{:S(2)}, u32[]{:S(2)}) collective-permute-start(bf16[4,4,48,128]{3,2,1,0:T(8,128)(2,1)S(1)} %get-tuple-element.46.refs_0_), channel_id=1, source_target_pairs={{0,1},{1,0},{2,3},{3,2},{4,5},{5,4},{6,7},{7,6},{8,9},{9,8},{10,11... | collective-permute-start | bytes 589832 | tf_op jit(solution)/shard_map/ppermute | solution.py:208
  14.9 11.3 %collective-permute-start.9 = (bf16[4,4,48,128]{3,2,1,0:T(8,128)(2,1)S(1)}, bf16[4,4,48,128]{3,2,1,0:T(8,128)(2,1)S(1)}, u32[]{:S(2)}, u32[]{:S(2)}) collective-permute-start(bf16[4,4,48,128]{3,2,1,0:T(8,128)(2,1)S(1)} %collective-permute-done.refs_2_), channel_id=1, source_target_pairs={{0,1},{1,0},{2,3},{3,2},{4,5},{5,4},{6,7},{7,6},{8,9},{9,8},{10,11... | collective-permute-start | bytes 589832 | tf_op jit(solution)/shard_map/ppermute | solution.py:208
  15.5 15.6 %collective-permute-start.1 = (bf16[4,4,48,128]{3,2,1,0:T(8,128)(2,1)S(1)}, bf16[4,4,48,128]{3,2,1,0:T(8,128)(2,1)S(1)}, u32[]{:S(2)}, u32[]{:S(2)}) collective-permute-start(bf16[4,4,48,128]{3,2,1,0:T(8,128)(2,1)S(1)} %get-tuple-element.38.refs_0_), channel_id=1, source_target_pairs={{0,2},{1,3},{2,0},{3,1},{4,6},{5,7},{6,4},{7,5},{8,10},{9,11},{10,... | collective-permute-start | bytes 589832 | tf_op jit(solution)/shard_map/ppermute | solution.py:208
  18.9 16.5 %collective-permute-start.13 = (bf16[4,4,48,128]{3,2,1,0:T(8,128)(2,1)S(1)}, bf16[4,4,48,128]{3,2,1,0:T(8,128)(2,1)S(1)}, u32[]{:S(2)}, u32[]{:S(2)}) collective-permute-start(bf16[4,4,48,128]{3,2,1,0:T(8,128)(2,1)S(1)} %get-tuple-element.38.refs_0_), channel_id=1, source_target_pairs={{0,1},{1,0},{2,3},{3,2},{4,5},{5,4},{6,7},{7,6},{8,9},{9,8},{10,11... | collective-permute-start | bytes 589832 | tf_op jit(solution)/shard_map/ppermute | solution.py:208
  28.7 15.2 %collective-permute-start.10 = (bf16[6,4,48,128]{3,2,1,0:T(8,128)(2,1)S(1)}, bf16[6,4,48,128]{3,2,1,0:T(8,128)(2,1)S(1)}, u32[]{:S(2)}, u32[]{:S(2)}) collective-permute-start(bf16[6,4,48,128]{3,2,1,0:T(8,128)(2,1)S(1)} %get-tuple-element.51), channel_id=1, source_target_pairs={{0,8},{4,12},{8,0},{12,4},{16,24},{20,28},{24,16},{28,20},{1,9},{5... | collective-permute-start | bytes 884744 | tf_op jit(solution)/shard_map/ppermute | solution.py:208
  29.6 14.2 %collective-permute-start.11 = (bf16[6,4,48,128]{3,2,1,0:T(8,128)(2,1)S(1)}, bf16[6,4,48,128]{3,2,1,0:T(8,128)(2,1)S(1)}, u32[]{:S(2)}, u32[]{:S(2)}) collective-permute-start(bf16[6,4,48,128]{3,2,1,0:T(8,128)(2,1)S(1)} %get-tuple-element.52), channel_id=1, source_target_pairs={{0,16},{4,20},{8,24},{12,28},{16,0},{20,4},{24,8},{28,12},{1,17},{... | collective-permute-start | bytes 884744 | tf_op jit(solution)/shard_map/ppermute | solution.py:208
  31.1 10.1 %collective-permute-start.14 = (bf16[4,4,48,128]{3,2,1,0:T(8,128)(2,1)S(1)}, bf16[4,4,48,128]{3,2,1,0:T(8,128)(2,1)S(1)}, u32[]{:S(2)}, u32[]{:S(2)}) collective-permute-start(bf16[4,4,48,128]{3,2,1,0:T(8,128)(2,1)S(1)} %collective-permute-done.1.refs_2_), channel_id=1, source_target_pairs={{0,1},{1,0},{2,3},{3,2},{4,5},{5,4},{6,7},{7,6},{8,9},{9,8},{10,11... | collective-permute-start | bytes 589832 | tf_op jit(solution)/shard_map/ppermute | solution.py:208
  31.2 12.5 %collective-permute-start.3 = (bf16[4,4,48,128]{3,2,1,0:T(8,128)(2,1)S(1)}, bf16[4,4,48,128]{3,2,1,0:T(8,128)(2,1)S(1)}, u32[]{:S(2)}, u32[]{:S(2)}) collective-permute-start(bf16[4,4,48,128]{3,2,1,0:T(8,128)(2,1)S(1)} %get-tuple-element.39.refs_0_), channel_id=1, source_target_pairs={{0,2},{1,3},{2,0},{3,1},{4,6},{5,7},{6,4},{7,5},{8,10},{9,11},{10,... | collective-permute-start | bytes 589832 | tf_op jit(solution)/shard_map/ppermute | solution.py:208
  35.4 11.9 %collective-permute-start.12 = (bf16[6,4,48,128]{3,2,1,0:T(8,128)(2,1)S(1)}, bf16[6,4,48,128]{3,2,1,0:T(8,128)(2,1)S(1)}, u32[]{:S(2)}, u32[]{:S(2)}) collective-permute-start(bf16[6,4,48,128]{3,2,1,0:T(8,128)(2,1)S(1)} %get-tuple-element.53), channel_id=1, source_target_pairs={{0,24},{4,28},{8,16},{12,20},{16,8},{20,12},{24,0},{28,4},{1,25},{... | collective-permute-start | bytes 884744 | tf_op jit(solution)/shard_map/ppermute | solution.py:208
  41.2 9.7 %collective-permute-start.2 = (bf16[4,4,48,128]{3,2,1,0:T(8,128)(2,1)S(1)}, bf16[4,4,48,128]{3,2,1,0:T(8,128)(2,1)S(1)}, u32[]{:S(2)}, u32[]{:S(2)}) collective-permute-start(bf16[4,4,48,128]{3,2,1,0:T(8,128)(2,1)S(1)} %get-tuple-element.39.refs_0_), channel_id=1, source_target_pairs={{0,1},{1,0},{2,3},{3,2},{4,5},{5,4},{6,7},{7,6},{8,9},{9,8},{10,11... | collective-permute-start | bytes 589832 | tf_op jit(solution)/shard_map/ppermute | solution.py:208
  43.7 11.7 %collective-permute-start.16 = (bf16[6,4,48,128]{3,2,1,0:T(8,128)(2,1)S(1)}, bf16[6,4,48,128]{3,2,1,0:T(8,128)(2,1)S(1)}, u32[]{:S(2)}, u32[]{:S(2)}) collective-permute-start(bf16[6,4,48,128]{3,2,1,0:T(8,128)(2,1)S(1)} %get-tuple-element.55), channel_id=1, source_target_pairs={{0,8},{4,12},{8,0},{12,4},{16,24},{20,28},{24,16},{28,20},{1,9},{5... | collective-permute-start | bytes 884744 | tf_op jit(solution)/shard_map/ppermute | solution.py:208
  43.8 11.6 %collective-permute-start.17 = (bf16[6,4,48,128]{3,2,1,0:T(8,128)(2,1)S(1)}, bf16[6,4,48,128]{3,2,1,0:T(8,128)(2,1)S(1)}, u32[]{:S(2)}, u32[]{:S(2)}) collective-permute-start(bf16[6,4,48,128]{3,2,1,0:T(8,128)(2,1)S(1)} %get-tuple-element.56), channel_id=1, source_target_pairs={{0,16},{4,20},{8,24},{12,28},{16,0},{20,4},{24,8},{28,12},{1,17},{... | collective-permute-start | bytes 884744 | tf_op jit(solution)/shard_map/ppermute | solution.py:208
  43.9 11.5 %collective-permute-start.18 = (bf16[6,4,48,128]{3,2,1,0:T(8,128)(2,1)S(1)}, bf16[6,4,48,128]{3,2,1,0:T(8,128)(2,1)S(1)}, u32[]{:S(2)}, u32[]{:S(2)}) collective-permute-start(bf16[6,4,48,128]{3,2,1,0:T(8,128)(2,1)S(1)} %get-tuple-element.57), channel_id=1, source_target_pairs={{0,24},{4,28},{8,16},{12,20},{16,8},{20,12},{24,0},{28,4},{1,25},{... | collective-permute-start | bytes 884744 | tf_op jit(solution)/shard_map/ppermute | solution.py:208
  47.2 5.7 %collective-permute-start.4 = (bf16[4,4,48,128]{3,2,1,0:T(8,128)(2,1)S(1)}, bf16[4,4,48,128]{3,2,1,0:T(8,128)(2,1)S(1)}, u32[]{:S(2)}, u32[]{:S(2)}) collective-permute-start(bf16[4,4,48,128]{3,2,1,0:T(8,128)(2,1)S(1)} %collective-permute-done.3.refs_2_), channel_id=1, source_target_pairs={{0,1},{1,0},{2,3},{3,2},{4,5},{5,4},{6,7},{7,6},{8,9},{9,8},{10,11... | collective-permute-start | bytes 589832 | tf_op jit(solution)/shard_map/ppermute | solution.py:208
  50.9 10.0 %copy-start.4 = (f32[8,3]{0,1:T(4,128)S(1)}, f32[8,3]{0,1:T(4,128)}, u32[]{:S(2)}) copy-start(f32[8,3]{0,1:T(4,128)} %param.7) | copy-start | bytes 292
  50.9 10.0 %collective-permute-start.15 = (bf16[4,4,4,48,128]{4,3,2,1,0:T(8,128)(2,1)S(1)}, bf16[4,4,4,48,128]{4,3,2,1,0:T(8,128)(2,1)S(1)}, u32[]{:S(2)}, u32[]{:S(2)}) collective-permute-start(bf16[4,4,4,48,128]{4,3,2,1,0:T(8,128)(2,1)S(1)} %shard_map.68), channel_id=1, source_target_pairs={{0,4},{4,0},{8,12},{12,8},{16,20},{20,16},{24,28},{28,24},{1,5},{5... | collective-permute-start | bytes 2359304 | tf_op jit(solution)/shard_map/ppermute | solution.py:208
  57.0 7.8 %collective-permute-start.19 = (bf16[4,4,4,48,128]{4,3,2,1,0:T(8,128)(2,1)S(1)}, bf16[4,4,4,48,128]{4,3,2,1,0:T(8,128)(2,1)S(1)}, u32[]{:S(2)}, u32[]{:S(2)}) collective-permute-start(bf16[4,4,4,48,128]{4,3,2,1,0:T(8,128)(2,1)S(1)} %shard_map.70), channel_id=1, source_target_pairs={{0,4},{4,0},{8,12},{12,8},{16,20},{20,16},{24,28},{28,24},{1,5},{5... | collective-permute-start | bytes 2359304 | tf_op jit(solution)/shard_map/ppermute | solution.py:208
  57.1 11.7 %collective-permute-start.5 = (bf16[6,4,48,128]{3,2,1,0:T(8,128)(2,1)S(1)}, bf16[6,4,48,128]{3,2,1,0:T(8,128)(2,1)S(1)}, u32[]{:S(2)}, u32[]{:S(2)}) collective-permute-start(bf16[6,4,48,128]{3,2,1,0:T(8,128)(2,1)S(1)} %get-tuple-element.41), channel_id=1, source_target_pairs={{0,8},{4,12},{8,0},{12,4},{16,24},{20,28},{24,16},{28,20},{1,9},{5... | collective-permute-start | bytes 884744 | tf_op jit(solution)/shard_map/ppermute | solution.py:208
  59.4 15.4 %collective-permute-start.6 = (bf16[6,4,48,128]{3,2,1,0:T(8,128)(2,1)S(1)}, bf16[6,4,48,128]{3,2,1,0:T(8,128)(2,1)S(1)}, u32[]{:S(2)}, u32[]{:S(2)}) collective-permute-start(bf16[6,4,48,128]{3,2,1,0:T(8,128)(2,1)S(1)} %get-tuple-element.42), channel_id=1, source_target_pairs={{0,16},{4,20},{8,24},{12,28},{16,0},{20,4},{24,8},{28,12},{1,17},{... | collective-permute-start | bytes 884744 | tf_op jit(solution)/shard_map/ppermute | solution.py:208
  59.4 15.4 %collective-permute-start.7 = (bf16[6,4,48,128]{3,2,1,0:T(8,128)(2,1)S(1)}, bf16[6,4,48,128]{3,2,1,0:T(8,128)(2,1)S(1)}, u32[]{:S(2)}, u32[]{:S(2)}) collective-permute-start(bf16[6,4,48,128]{3,2,1,0:T(8,128)(2,1)S(1)} %get-tuple-element.43), channel_id=1, source_target_pairs={{0,24},{4,28},{8,16},{12,20},{16,8},{20,12},{24,0},{28,4},{1,25},{... | collective-permute-start | bytes 884744 | tf_op jit(solution)/shard_map/ppermute | solution.py:208
  60.9 14.4 %collective-permute-start.20 = (bf16[6,4,48,128]{3,2,1,0:T(8,128)(2,1)S(1)}, bf16[6,4,48,128]{3,2,1,0:T(8,128)(2,1)S(1)}, u32[]{:S(2)}, u32[]{:S(2)}) collective-permute-start(bf16[6,4,48,128]{3,2,1,0:T(8,128)(2,1)S(1)} %get-tuple-element.40.refs_0_), channel_id=1, source_target_pairs={{0,4},{4,0},{8,12},{12,8},{16,20},{20,16},{24,28},{28,24},{1,5},{5... | collective-permute-start | bytes 884744 | tf_op jit(solution)/shard_map/ppermute | solution.py:208
  74.8 1.6 %collective-permute-start.21 = (bf16[6,4,48,128]{3,2,1,0:T(8,128)(2,1)S(1)}, bf16[6,4,48,128]{3,2,1,0:T(8,128)(2,1)S(1)}, u32[]{:S(2)}, u32[]{:S(2)}) collective-permute-start(bf16[6,4,48,128]{3,2,1,0:T(8,128)(2,1)S(1)} %collective-permute-done.5.refs_1_), channel_id=1, source_target_pairs={{0,4},{4,0},{8,12},{12,8},{16,20},{20,16},{24,28},{28,24},{1,5},{5... | collective-permute-start | bytes 884744 | tf_op jit(solution)/shard_map/ppermute | solution.py:208
  74.8 2.0 %collective-permute-start.22 = (bf16[6,4,48,128]{3,2,1,0:T(8,128)(2,1)S(1)}, bf16[6,4,48,128]{3,2,1,0:T(8,128)(2,1)S(1)}, u32[]{:S(2)}, u32[]{:S(2)}) collective-permute-start(bf16[6,4,48,128]{3,2,1,0:T(8,128)(2,1)S(1)} %collective-permute-done.6.refs_2_), channel_id=1, source_target_pairs={{0,4},{4,0},{8,12},{12,8},{16,20},{20,16},{24,28},{28,24},{1,5},{5... | collective-permute-start | bytes 884744 | tf_op jit(solution)/shard_map/ppermute | solution.py:208
  75.3 1.9 %collective-permute-start.23 = (bf16[6,4,48,128]{3,2,1,0:T(8,128)(2,1)S(1)}, bf16[6,4,48,128]{3,2,1,0:T(8,128)(2,1)S(1)}, u32[]{:S(2)}, u32[]{:S(2)}) collective-permute-start(bf16[6,4,48,128]{3,2,1,0:T(8,128)(2,1)S(1)} %collective-permute-done.7.refs_3_), channel_id=1, source_target_pairs={{0,4},{4,0},{8,12},{12,8},{16,20},{20,16},{24,28},{28,24},{1,5},{5... | collective-permute-start | bytes 884744 | tf_op jit(solution)/shard_map/ppermute | solution.py:208

commit v7 on v6

--- a/solution.py
+++ b/solution.py
@@ -209,39 +209,32 @@
 
 
 def sort_kernel(where_ref, *refs):
-    count = (len(refs) - 1) // 2
-    pieces, outs, sems = refs[:count], refs[count:-1], refs[-1]
+    count = len(refs) // 2
+    pieces, outs = refs[:count], refs[count:]
     shard_rows = pieces[0].shape[0]
     chip, z = where_ref[0] // 2, where_ref[1]
 
-    def copies(k, piece):
-        main = pltpu.make_async_copy(piece, outs[k].at[pl.ds(1, shard_rows)], sems.at[k, 0])
-        above = pltpu.make_async_copy(piece.at[pl.ds(shard_rows - 1, 1)], outs[k].at[pl.ds(0, 1)], sems.at[k, 1])
-        below = pltpu.make_async_copy(piece.at[pl.ds(0, 1)], outs[k].at[pl.ds(shard_rows + 1, 1)], sems.at[k, 2])
-        return main, above, below
-
-    for k in range(count):
+    def lay(out, first, piece, row, length):
+        out[first : first + length] = piece[row : row + length]
+
+    for k, out in enumerate(outs):
         plane = chip ^ k
         for j, piece in enumerate(pieces):
-            main, above, below = copies(k, piece)
-            pl.when((plane ^ z) == j)(main.start)
-            pl.when((jnp.maximum(plane - 1, 0) ^ z) == j)(above.start)
-            pl.when((jnp.minimum(plane + 1, count - 1) ^ z) == j)(below.start)
-    for k in range(count):
-        for copy in copies(k, pieces[0]):
-            copy.wait()
+            below, above = jnp.maximum(plane - 1, 0), jnp.minimum(plane + 1, count - 1)
+            pl.when((plane ^ z) == j)(functools.partial(lay, out, 1, piece, 0, shard_rows))
+            pl.when((below ^ z) == j)(functools.partial(lay, out, 0, piece, shard_rows - 1, 1))
+            pl.when((above ^ z) == j)(functools.partial(lay, out, shard_rows + 1, piece, 0, 1))
 
 
 def sorted_rows(where, pieces):
     shape = pieces[0].shape
     out = jax.ShapeDtypeStruct((shape[0] + 2,) + shape[1:], pieces[0].dtype)
-    anywhere = pl.BlockSpec(memory_space=pl.ANY)
+    vmem = pl.BlockSpec(memory_space=pltpu.VMEM)
     return pl.pallas_call(
         sort_kernel,
-        in_specs=[SCALAR] + [anywhere] * len(pieces),
-        out_specs=[anywhere] * len(pieces),
+        in_specs=[SCALAR] + [vmem] * len(pieces),
+        out_specs=[vmem] * len(pieces),
         out_shape=[out] * len(pieces),
-        scratch_shapes=[pltpu.SemaphoreType.DMA((len(pieces), 3))],
         compiler_params=PARAMS,
         cost_estimate=pl.CostEstimate(flops=0, bytes_accessed=3000000, transcendentals=0),
     )(where, *pieces)
@@ -263,27 +256,21 @@
 
 
 def give_kernel(where_ref, *refs):
-    kept, (out_ref, sems) = refs[:-2], refs[-2:]
+    kept, out_ref = refs[:-1], refs[-1]
     count = out_ref.shape[1]
     first = (1 - where_ref[0] % 2) * (count - 2)
-    copies = [
-        pltpu.make_async_copy(m.at[pl.ds(first, count)], out_ref.at[k], sems.at[k]) for k, m in enumerate(kept)
-    ]
-    for copy in copies:
-        copy.start()
-    for copy in copies:
-        copy.wait()
+    for k, m in enumerate(kept):
+        out_ref[k] = m[pl.ds(first, count)]
 
 
 def given_rows(where, kept):
     shape = kept[0].shape
-    anywhere = pl.BlockSpec(memory_space=pl.ANY)
+    vmem = pl.BlockSpec(memory_space=pltpu.VMEM)
     return pl.pallas_call(
         give_kernel,
-        in_specs=[SCALAR] + [anywhere] * len(kept),
-        out_specs=anywhere,
+        in_specs=[SCALAR] + [vmem] * len(kept),
+        out_specs=vmem,
         out_shape=jax.ShapeDtypeStruct((len(kept), shape[0] // 2 + 1) + shape[1:], kept[0].dtype),
-        scratch_shapes=[pltpu.SemaphoreType.DMA((len(kept),))],
         compiler_params=PARAMS,
         cost_estimate=pl.CostEstimate(flops=0, bytes_accessed=2_000_000, transcendentals=0),
     )(where, *kept)

time: 84.7 us -> 82.1 us (0.969); the launches traced: 84.2 us -> 80.6 us
  Pallas kernels: 26.3 us -> 19.4 us
  waiting for transfers between devices: 29.1 us -> 32.7 us
    pallas_call x5, Pallas kernels: 10.5 us -> 3.68 us  [the longest x3 2.48 us: sorted_rows(): pl.pallas_call(sort_kernel, in_specs=[SCALAR] + [vmem] * len(pieces), out...]
    ppermute x24, waiting for transfers between devices: 29.1 us -> 32.7 us  [swapped(): lax.ppermute(value, axis, [(i, i ^ by) for i in range(lax.axis_size(axis))])]
  transfers between devices with their start and end apart: 24 -> 24, of which waited for: 8 -> 10; matrix products, arithmetic and copies ran while one was open for 0% -> 0% of each run, Pallas kernels for 23% -> 15%
where the time goes in v7:
time: 82.1 us; the launch traced here: 80.6 us
  waiting for transfers between devices  32.7 us (40%)
  starting transfers between devices  26.6 us (32%)
  Pallas kernels  19.4 us (24%)
  local copies, waits for them, and re-layouts  1.58 us (2%)
    ppermute x24, waiting for transfers between devices, swapped(): lax.ppermute(value, axis, [(i, i ^ by) for i in range(lax.axis_size(axis))])  32.7 us
    ppermute x24, starting transfers between devices, swapped(): lax.ppermute(value, axis, [(i, i ^ by) for i in range(lax.axis_size(axis))])  26.6 us
    pallas_call x2, Pallas kernels, first_part(): pl.pallas_call(functools.partial(first_kernel, len(kept)), grid=(rows, gr...  7.83 us
    pallas_call x1, Pallas kernels, last_part(): pl.pallas_call(functools.partial(last_kernel, len(kept)), grid=(rows, gro...  6.98 us
    pallas_call x3, Pallas kernels, sorted_rows(): pl.pallas_call(sort_kernel, in_specs=[SCALAR] + [vmem] * len(pieces), out...  2.48 us
  transfers between devices with their start and end apart: 24, of which 10 were waited for; matrix products, arithmetic and copies ran while one was open for 0% of the time, Pallas kernels for 15%

profile of v7, /device:TPU:0, one launch (start us, length us, event | category | flops | bytes accessed | tf_op | source)
XLA Modules:
  0.0 80.6 jit_solution(760912059416120934)
XLA Ops:
  0.0 1.5 %copy.9 = bf16[4,4,137,128]{3,2,1,0:T(8,128)(2,1)S(1)} copy(f32[4,4,137,128]{3,1,2,0:T(4,128)} %param.6) | data formatting | bytes 1683456 | tf_op args[0]
  1.6 4.1 %collective-permute-start = (bf16[4,4,48,128]{3,2,1,0:T(8,128)(2,1)S(1)}, bf16[4,4,48,128]{3,2,1,0:T(8,128)(2,1)S(1)}, u32[]{:S(2)}, u32[]{:S(2)}) collective-permute-start(bf16[4,4,48,128]{3,2,1,0:T(8,128)(2,1)S(1)} %get-tuple-element.46.refs_0_), channel_id=1, source_target_pairs={{0,2},{1,3},{2,0},{3,1},{4,6},{5,7},{6,4},{7,5},{8,10},{9,11},{10,... | collective-permute-start | bytes 589832 | tf_op jit(solution)/shard_map/ppermute | solution.py:208
  5.7 1.6 %collective-permute-start.8 = (bf16[4,4,48,128]{3,2,1,0:T(8,128)(2,1)S(1)}, bf16[4,4,48,128]{3,2,1,0:T(8,128)(2,1)S(1)}, u32[]{:S(2)}, u32[]{:S(2)}) collective-permute-start(bf16[4,4,48,128]{3,2,1,0:T(8,128)(2,1)S(1)} %get-tuple-element.46.refs_0_), channel_id=1, source_target_pairs={{0,1},{1,0},{2,3},{3,2},{4,5},{5,4},{6,7},{7,6},{8,9},{9,8},{10,11... | collective-permute-start | bytes 589832 | tf_op jit(solution)/shard_map/ppermute | solution.py:208
  7.3 7.6 %collective-permute-done.refs_2_ = bf16[4,4,48,128]{3,2,1,0:T(8,128)(2,1)S(1)} collective-permute-done((bf16[4,4,48,128]{3,2,1,0:T(8,128)(2,1)S(1)}, bf16[4,4,48,128]{3,2,1,0:T(8,128)(2,1)S(1)}, u32[]{:S(2)}, u32[]{:S(2)}) %collective-permute-start) | collective-permute-done | bytes 196640 | tf_op jit(solution)/shard_map/ppermute | solution.py:208
  14.9 0.6 collective-permute-start.9
  15.5 3.4 %collective-permute-start.1 = (bf16[4,4,48,128]{3,2,1,0:T(8,128)(2,1)S(1)}, bf16[4,4,48,128]{3,2,1,0:T(8,128)(2,1)S(1)}, u32[]{:S(2)}, u32[]{:S(2)}) collective-permute-start(bf16[4,4,48,128]{3,2,1,0:T(8,128)(2,1)S(1)} %get-tuple-element.38.refs_0_), channel_id=1, source_target_pairs={{0,2},{1,3},{2,0},{3,1},{4,6},{5,7},{6,4},{7,5},{8,10},{9,11},{10,... | collective-permute-start | bytes 589832 | tf_op jit(solution)/shard_map/ppermute | solution.py:208
  19.0 0.9 %shard_map.65 = (bf16[2,8,128,256]{3,2,1,0:T(8,128)(2,1)S(1)}, bf16[2,144,144]{2,1,0:T(8,128)(2,1)S(1)}) custom-call(s32[4]{0:T(128)S(1)} %pad_add_fusion.where_ref, s32[8]{0:T(128)S(1)} %copy-done.3, s32[8,5]{1,0:T(8,128)S(1)} %copy-done.2, bf16[8,5,128,128]{3,2,1,0:T(8,128)(2,1)S(1)} %copy-done, bf16[137,8,137]{2,1,0:T(8,128)(2,1)S(1)} %bitcast.6), custom_call_target="tpu_custom_call" | custom-call | bytes 4000000 | tf_op jit(solution)/shard_map/pallas_call | solution.py:55
  20.0 6.2 %collective-permute-done.9.refs_3_ = bf16[4,4,48,128]{3,2,1,0:T(8,128)(2,1)S(1)} collective-permute-done((bf16[4,4,48,128]{3,2,1,0:T(8,128)(2,1)S(1)}, bf16[4,4,48,128]{3,2,1,0:T(8,128)(2,1)S(1)}, u32[]{:S(2)}, u32[]{:S(2)}) %collective-permute-start.9) | collective-permute-done | bytes 196640 | tf_op jit(solution)/shard_map/ppermute | solution.py:208
  26.2 0.8 %shard_map.66 = (bf16[6,4,48,128]{3,2,1,0:T(8,128)(2,1)S(1)}, bf16[6,4,48,128]{3,2,1,0:T(8,128)(2,1)S(1)}, bf16[6,4,48,128]{3,2,1,0:T(8,128)(2,1)S(1)}, bf16[6,4,48,128]{3,2,1,0:T(8,128)(2,1)S(1)}) custom-call(s32[4]{0:T(128)S(1)} %pad_add_fusion.where_ref, bf16[4,4,48,128]{3,2,1,0:T(8,128)(2,1)S(1)} %get-tuple-element.46.refs_0_, ...), custom_call_target="tpu_custom_call" | custom-call | bytes 3000000 | tf_op jit(solution)/shard_map/pallas_call | solution.py:233
  27.0 1.0 %collective-permute-start.10 = (bf16[6,4,48,128]{3,2,1,0:T(8,128)(2,1)S(1)}, bf16[6,4,48,128]{3,2,1,0:T(8,128)(2,1)S(1)}, u32[]{:S(2)}, u32[]{:S(2)}) collective-permute-start(bf16[6,4,48,128]{3,2,1,0:T(8,128)(2,1)S(1)} %get-tuple-element.51), channel_id=1, source_target_pairs={{0,8},{4,12},{8,0},{12,4},{16,24},{20,28},{24,16},{28,20},{1,9},{5... | collective-permute-start | bytes 884744 | tf_op jit(solution)/shard_map/ppermute | solution.py:208
  28.0 1.5 %collective-permute-start.11 = (bf16[6,4,48,128]{3,2,1,0:T(8,128)(2,1)S(1)}, bf16[6,4,48,128]{3,2,1,0:T(8,128)(2,1)S(1)}, u32[]{:S(2)}, u32[]{:S(2)}) collective-permute-start(bf16[6,4,48,128]{3,2,1,0:T(8,128)(2,1)S(1)} %get-tuple-element.52), channel_id=1, source_target_pairs={{0,16},{4,20},{8,24},{12,28},{16,0},{20,4},{24,8},{28,12},{1,17},{... | collective-permute-start | bytes 884744 | tf_op jit(solution)/shard_map/ppermute | solution.py:208
  29.5 4.2 %collective-permute-start.3 = (bf16[4,4,48,128]{3,2,1,0:T(8,128)(2,1)S(1)}, bf16[4,4,48,128]{3,2,1,0:T(8,128)(2,1)S(1)}, u32[]{:S(2)}, u32[]{:S(2)}) collective-permute-start(bf16[4,4,48,128]{3,2,1,0:T(8,128)(2,1)S(1)} %get-tuple-element.39.refs_0_), channel_id=1, source_target_pairs={{0,2},{1,3},{2,0},{3,1},{4,6},{5,7},{6,4},{7,5},{8,10},{9,11},{10,... | collective-permute-start | bytes 589832 | tf_op jit(solution)/shard_map/ppermute | solution.py:208
  34.3 1.8 %collective-permute-done.14.refs_3_ = bf16[4,4,48,128]{3,2,1,0:T(8,128)(2,1)S(1)} collective-permute-done((bf16[4,4,48,128]{3,2,1,0:T(8,128)(2,1)S(1)}, bf16[4,4,48,128]{3,2,1,0:T(8,128)(2,1)S(1)}, u32[]{:S(2)}, u32[]{:S(2)}) %collective-permute-start.14) | collective-permute-done | bytes 196640 | tf_op jit(solution)/shard_map/ppermute | solution.py:208
  36.0 1.3 %collective-permute-start.2 = (bf16[4,4,48,128]{3,2,1,0:T(8,128)(2,1)S(1)}, bf16[4,4,48,128]{3,2,1,0:T(8,128)(2,1)S(1)}, u32[]{:S(2)}, u32[]{:S(2)}) collective-permute-start(bf16[4,4,48,128]{3,2,1,0:T(8,128)(2,1)S(1)} %get-tuple-element.39.refs_0_), channel_id=1, source_target_pairs={{0,1},{1,0},{2,3},{3,2},{4,5},{5,4},{6,7},{7,6},{8,9},{9,8},{10,11... | collective-permute-start | bytes 589832 | tf_op jit(solution)/shard_map/ppermute | solution.py:208
  37.3 0.8 %shard_map.67 = (bf16[6,4,48,128]{3,2,1,0:T(8,128)(2,1)S(1)}, bf16[6,4,48,128]{3,2,1,0:T(8,128)(2,1)S(1)}, bf16[6,4,48,128]{3,2,1,0:T(8,128)(2,1)S(1)}, bf16[6,4,48,128]{3,2,1,0:T(8,128)(2,1)S(1)}) custom-call(s32[4]{0:T(128)S(1)} %pad_add_fusion.where_ref, bf16[4,4,48,128]{3,2,1,0:T(8,128)(2,1)S(1)} %get-tuple-element.38.refs_0_, ...), custom_call_target="tpu_custom_call" | custom-call | bytes 3000000 | tf_op jit(solution)/shard_map/pallas_call | solution.py:233
  38.1 2.5 %collective-permute-done.3.refs_2_ = bf16[4,4,48,128]{3,2,1,0:T(8,128)(2,1)S(1)} collective-permute-done((bf16[4,4,48,128]{3,2,1,0:T(8,128)(2,1)S(1)}, bf16[4,4,48,128]{3,2,1,0:T(8,128)(2,1)S(1)}, u32[]{:S(2)}, u32[]{:S(2)}) %collective-permute-start.3) | collective-permute-done | bytes 196640 | tf_op jit(solution)/shard_map/ppermute | solution.py:208
  40.7 1.5 %collective-permute-start.16 = (bf16[6,4,48,128]{3,2,1,0:T(8,128)(2,1)S(1)}, bf16[6,4,48,128]{3,2,1,0:T(8,128)(2,1)S(1)}, u32[]{:S(2)}, u32[]{:S(2)}) collective-permute-start(bf16[6,4,48,128]{3,2,1,0:T(8,128)(2,1)S(1)} %get-tuple-element.55), channel_id=1, source_target_pairs={{0,8},{4,12},{8,0},{12,4},{16,24},{20,28},{24,16},{28,20},{1,9},{5... | collective-permute-start | bytes 884744 | tf_op jit(solution)/shard_map/ppermute | solution.py:208
  42.2 0.6 collective-permute-start.17
  42.8 1.4 %collective-permute-start.18 = (bf16[6,4,48,128]{3,2,1,0:T(8,128)(2,1)S(1)}, bf16[6,4,48,128]{3,2,1,0:T(8,128)(2,1)S(1)}, u32[]{:S(2)}, u32[]{:S(2)}) collective-permute-start(bf16[6,4,48,128]{3,2,1,0:T(8,128)(2,1)S(1)} %get-tuple-element.57), channel_id=1, source_target_pairs={{0,24},{4,28},{8,16},{12,20},{16,8},{20,12},{24,0},{28,4},{1,25},{... | collective-permute-start | bytes 884744 | tf_op jit(solution)/shard_map/ppermute | solution.py:208
  44.2 0.7 collective-permute-start.4
  45.6 4.2 %collective-permute-done.4.refs_3_ = bf16[4,4,48,128]{3,2,1,0:T(8,128)(2,1)S(1)} collective-permute-done((bf16[4,4,48,128]{3,2,1,0:T(8,128)(2,1)S(1)}, bf16[4,4,48,128]{3,2,1,0:T(8,128)(2,1)S(1)}, u32[]{:S(2)}, u32[]{:S(2)}) %collective-permute-start.4) | collective-permute-done | bytes 196640 | tf_op jit(solution)/shard_map/ppermute | solution.py:208
  49.9 0.8 %shard_map.64 = (bf16[6,4,48,128]{3,2,1,0:T(8,128)(2,1)S(1)}, bf16[6,4,48,128]{3,2,1,0:T(8,128)(2,1)S(1)}, bf16[6,4,48,128]{3,2,1,0:T(8,128)(2,1)S(1)}, bf16[6,4,48,128]{3,2,1,0:T(8,128)(2,1)S(1)}) custom-call(s32[4]{0:T(128)S(1)} %pad_add_fusion.where_ref, bf16[4,4,48,128]{3,2,1,0:T(8,128)(2,1)S(1)} %get-tuple-element.39.refs_0_, ...), custom_call_target="tpu_custom_call" | custom-call | bytes 3000000 | tf_op jit(solution)/shard_map/pallas_call | solution.py:233
  50.7 3.6 %collective-permute-done.17.refs_2_ = bf16[6,4,48,128]{3,2,1,0:T(8,128)(2,1)S(1)} collective-permute-done((bf16[6,4,48,128]{3,2,1,0:T(8,128)(2,1)S(1)}, bf16[6,4,48,128]{3,2,1,0:T(8,128)(2,1)S(1)}, u32[]{:S(2)}, u32[]{:S(2)}) %collective-permute-start.17) | collective-permute-done | bytes 294944 | tf_op jit(solution)/shard_map/ppermute | solution.py:208
  54.3 0.6 shard_map.70
  55.0 0.7 collective-permute-start.5
  55.7 0.9 %collective-permute-start.6 = (bf16[6,4,48,128]{3,2,1,0:T(8,128)(2,1)S(1)}, bf16[6,4,48,128]{3,2,1,0:T(8,128)(2,1)S(1)}, u32[]{:S(2)}, u32[]{:S(2)}) collective-permute-start(bf16[6,4,48,128]{3,2,1,0:T(8,128)(2,1)S(1)} %get-tuple-element.42), channel_id=1, source_target_pairs={{0,16},{4,20},{8,24},{12,28},{16,0},{20,4},{24,8},{28,12},{1,17},{... | collective-permute-start | bytes 884744 | tf_op jit(solution)/shard_map/ppermute | solution.py:208
  56.5 2.0 %collective-permute-start.7 = (bf16[6,4,48,128]{3,2,1,0:T(8,128)(2,1)S(1)}, bf16[6,4,48,128]{3,2,1,0:T(8,128)(2,1)S(1)}, u32[]{:S(2)}, u32[]{:S(2)}) collective-permute-start(bf16[6,4,48,128]{3,2,1,0:T(8,128)(2,1)S(1)} %get-tuple-element.43), channel_id=1, source_target_pairs={{0,24},{4,28},{8,16},{12,20},{16,8},{20,12},{24,0},{28,4},{1,25},{... | collective-permute-start | bytes 884744 | tf_op jit(solution)/shard_map/ppermute | solution.py:208
  58.5 3.9 %shard_map.69.refs_10_ = bf16[2,2,16,48,256]{4,3,2,1,0:T(8,128)(2,1)S(1)} custom-call(s32[4]{0:T(128)S(1)} %pad_add_fusion.where_ref, s32[8]{0:T(128)S(1)} %copy-done.3, f32[3,8]{1,0:T(4,128)S(1)} %bitcast.10, bf16[6,4,48,128]{3,2,1,0:T(8,128)(2,1)S(1)} %get-tuple-element.58.refs_0_, bf16[6,4,48,128]{3,2,1,0:T(8,128)(2,1)S(1)} %collective-permute-done.10.refs_1_, ...), custom_call_target="tpu_custom_call" | custom-call | flops 2000000000 | bytes 8000000 | tf_op jit(solution)/shard_map/pallas_call | solution.py:171
  62.5 3.9 %shard_map.71.refs_11_ = bf16[2,2,16,48,256]{4,3,2,1,0:T(8,128)(2,1)S(1)} custom-call(s32[4]{0:T(128)S(1)} %pad_add_fusion.where_ref, s32[8]{0:T(128)S(1)} %copy-done.3, f32[3,8]{1,0:T(4,128)S(1)} %bitcast.11, bf16[6,4,48,128]{3,2,1,0:T(8,128)(2,1)S(1)} %get-tuple-element.63.refs_0_, bf16[6,4,48,128]{3,2,1,0:T(8,128)(2,1)S(1)} %collective-permute-done.16.refs_1_, ...), custom_call_target="tpu_custom_call" | custom-call | flops 2000000000 | bytes 8000000 | tf_op jit(solution)/shard_map/pallas_call | solution.py:171
  66.4 4.8 %collective-permute-done.7.refs_3_ = bf16[6,4,48,128]{3,2,1,0:T(8,128)(2,1)S(1)} collective-permute-done((bf16[6,4,48,128]{3,2,1,0:T(8,128)(2,1)S(1)}, bf16[6,4,48,128]{3,2,1,0:T(8,128)(2,1)S(1)}, u32[]{:S(2)}, u32[]{:S(2)}) %collective-permute-start.7) | collective-permute-done | bytes 294944 | tf_op jit(solution)/shard_map/ppermute | solution.py:208
  71.7 1.1 %collective-permute-done.21.refs_5_ = bf16[6,4,48,128]{3,2,1,0:T(8,128)(2,1)S(1)} collective-permute-done((bf16[6,4,48,128]{3,2,1,0:T(8,128)(2,1)S(1)}, bf16[6,4,48,128]{3,2,1,0:T(8,128)(2,1)S(1)}, u32[]{:S(2)}, u32[]{:S(2)}) %collective-permute-start.21) | collective-permute-done | bytes 294944 | tf_op jit(solution)/shard_map/ppermute | solution.py:208
  73.6 7.0 %shard_map.72 = bf16[2,2,137,32,128]{4,3,2,1,0:T(8,128)(2,1)} custom-call(s32[4]{0:T(128)S(1)} %pad_add_fusion.where_ref, s32[8]{0:T(128)S(1)} %copy-done.3, f32[3,8]{1,0:T(4,128)S(1)} %bitcast.12, bf16[6,4,48,128]{3,2,1,0:T(8,128)(2,1)S(1)} %get-tuple-element.40.refs_0_, bf16[6,4,48,128]{3,2,1,0:T(8,128)(2,1)S(1)} %collective-permute-done.5.refs_1_, ...), custom_call_target="tpu_custom_call" | custom-call | flops 4000000000 | bytes 12000000 | tf_op jit(solution)/shard_map/pallas_call | solution.py:189
  (38 shorter events, 2.8 us)
Async XLA Ops:
  0.0 19.0 %copy-start.3 = (s32[8]{0:T(128)S(1)}, s32[8]{0:T(128)}, u32[]{:S(2)}) copy-start(s32[8]{0:T(128)} %slot_ref.7) | copy-start | bytes 100
  0.0 19.0 %copy-start.1 = (bf16[8,137,137]{2,0,1:T(8,128)(2,1)S(1)}, bf16[8,137,137]{2,0,1:T(8,128)(2,1)}, u32[]{:S(2)}) copy-start(bf16[8,137,137]{2,0,1:T(8,128)(2,1)} %param.10) | copy-start | bytes 900916
  0.0 19.0 %copy-start = (bf16[8,5,128,128]{3,2,1,0:T(8,128)(2,1)S(1)}, bf16[8,5,128,128]{3,2,1,0:T(8,128)(2,1)}, u32[]{:S(2)}) copy-start(bf16[8,5,128,128]{3,2,1,0:T(8,128)(2,1)} %filter_ref.1) | copy-start | bytes 3932164
  0.0 19.0 %copy-start.2 = (s32[8,5]{1,0:T(8,128)S(1)}, s32[8,5]{1,0:T(8,128)}, u32[]{:S(2)}) copy-start(s32[8,5]{1,0:T(8,128)} %offset_ref.1) | copy-start | bytes 484
  1.6 13.3 %collective-permute-start = (bf16[4,4,48,128]{3,2,1,0:T(8,128)(2,1)S(1)}, bf16[4,4,48,128]{3,2,1,0:T(8,128)(2,1)S(1)}, u32[]{:S(2)}, u32[]{:S(2)}) collective-permute-start(bf16[4,4,48,128]{3,2,1,0:T(8,128)(2,1)S(1)} %get-tuple-element.46.refs_0_), channel_id=1, source_target_pairs={{0,2},{1,3},{2,0},{3,1},{4,6},{5,7},{6,4},{7,5},{8,10},{9,11},{10,... | collective-permute-start | bytes 589832 | tf_op jit(solution)/shard_map/ppermute | solution.py:208
  5.7 14.3 %collective-permute-start.8 = (bf16[4,4,48,128]{3,2,1,0:T(8,128)(2,1)S(1)}, bf16[4,4,48,128]{3,2,1,0:T(8,128)(2,1)S(1)}, u32[]{:S(2)}, u32[]{:S(2)}) collective-permute-start(bf16[4,4,48,128]{3,2,1,0:T(8,128)(2,1)S(1)} %get-tuple-element.46.refs_0_), channel_id=1, source_target_pairs={{0,1},{1,0},{2,3},{3,2},{4,5},{5,4},{6,7},{7,6},{8,9},{9,8},{10,11... | collective-permute-start | bytes 589832 | tf_op jit(solution)/shard_map/ppermute | solution.py:208
  14.9 11.3 %collective-permute-start.9 = (bf16[4,4,48,128]{3,2,1,0:T(8,128)(2,1)S(1)}, bf16[4,4,48,128]{3,2,1,0:T(8,128)(2,1)S(1)}, u32[]{:S(2)}, u32[]{:S(2)}) collective-permute-start(bf16[4,4,48,128]{3,2,1,0:T(8,128)(2,1)S(1)} %collective-permute-done.refs_2_), channel_id=1, source_target_pairs={{0,1},{1,0},{2,3},{3,2},{4,5},{5,4},{6,7},{7,6},{8,9},{9,8},{10,11... | collective-permute-start | bytes 589832 | tf_op jit(solution)/shard_map/ppermute | solution.py:208
  15.5 14.0 %collective-permute-start.1 = (bf16[4,4,48,128]{3,2,1,0:T(8,128)(2,1)S(1)}, bf16[4,4,48,128]{3,2,1,0:T(8,128)(2,1)S(1)}, u32[]{:S(2)}, u32[]{:S(2)}) collective-permute-start(bf16[4,4,48,128]{3,2,1,0:T(8,128)(2,1)S(1)} %get-tuple-element.38.refs_0_), channel_id=1, source_target_pairs={{0,2},{1,3},{2,0},{3,1},{4,6},{5,7},{6,4},{7,5},{8,10},{9,11},{10,... | collective-permute-start | bytes 589832 | tf_op jit(solution)/shard_map/ppermute | solution.py:208
  18.9 14.9 %collective-permute-start.13 = (bf16[4,4,48,128]{3,2,1,0:T(8,128)(2,1)S(1)}, bf16[4,4,48,128]{3,2,1,0:T(8,128)(2,1)S(1)}, u32[]{:S(2)}, u32[]{:S(2)}) collective-permute-start(bf16[4,4,48,128]{3,2,1,0:T(8,128)(2,1)S(1)} %get-tuple-element.38.refs_0_), channel_id=1, source_target_pairs={{0,1},{1,0},{2,3},{3,2},{4,5},{5,4},{6,7},{7,6},{8,9},{9,8},{10,11... | collective-permute-start | bytes 589832 | tf_op jit(solution)/shard_map/ppermute | solution.py:208
  27.0 15.1 %collective-permute-start.10 = (bf16[6,4,48,128]{3,2,1,0:T(8,128)(2,1)S(1)}, bf16[6,4,48,128]{3,2,1,0:T(8,128)(2,1)S(1)}, u32[]{:S(2)}, u32[]{:S(2)}) collective-permute-start(bf16[6,4,48,128]{3,2,1,0:T(8,128)(2,1)S(1)} %get-tuple-element.51), channel_id=1, source_target_pairs={{0,8},{4,12},{8,0},{12,4},{16,24},{20,28},{24,16},{28,20},{1,9},{5... | collective-permute-start | bytes 884744 | tf_op jit(solution)/shard_map/ppermute | solution.py:208
  28.0 14.8 %collective-permute-start.11 = (bf16[6,4,48,128]{3,2,1,0:T(8,128)(2,1)S(1)}, bf16[6,4,48,128]{3,2,1,0:T(8,128)(2,1)S(1)}, u32[]{:S(2)}, u32[]{:S(2)}) collective-permute-start(bf16[6,4,48,128]{3,2,1,0:T(8,128)(2,1)S(1)} %get-tuple-element.52), channel_id=1, source_target_pairs={{0,16},{4,20},{8,24},{12,28},{16,0},{20,4},{24,8},{28,12},{1,17},{... | collective-permute-start | bytes 884744 | tf_op jit(solution)/shard_map/ppermute | solution.py:208
  29.5 6.5 %collective-permute-start.14 = (bf16[4,4,48,128]{3,2,1,0:T(8,128)(2,1)S(1)}, bf16[4,4,48,128]{3,2,1,0:T(8,128)(2,1)S(1)}, u32[]{:S(2)}, u32[]{:S(2)}) collective-permute-start(bf16[4,4,48,128]{3,2,1,0:T(8,128)(2,1)S(1)} %collective-permute-done.1.refs_2_), channel_id=1, source_target_pairs={{0,1},{1,0},{2,3},{3,2},{4,5},{5,4},{6,7},{7,6},{8,9},{9,8},{10,11... | collective-permute-start | bytes 589832 | tf_op jit(solution)/shard_map/ppermute | solution.py:208
  29.5 11.1 %collective-permute-start.3 = (bf16[4,4,48,128]{3,2,1,0:T(8,128)(2,1)S(1)}, bf16[4,4,48,128]{3,2,1,0:T(8,128)(2,1)S(1)}, u32[]{:S(2)}, u32[]{:S(2)}) collective-permute-start(bf16[4,4,48,128]{3,2,1,0:T(8,128)(2,1)S(1)} %get-tuple-element.39.refs_0_), channel_id=1, source_target_pairs={{0,2},{1,3},{2,0},{3,1},{4,6},{5,7},{6,4},{7,5},{8,10},{9,11},{10,... | collective-permute-start | bytes 589832 | tf_op jit(solution)/shard_map/ppermute | solution.py:208
  33.8 10.4 %collective-permute-start.12 = (bf16[6,4,48,128]{3,2,1,0:T(8,128)(2,1)S(1)}, bf16[6,4,48,128]{3,2,1,0:T(8,128)(2,1)S(1)}, u32[]{:S(2)}, u32[]{:S(2)}) collective-permute-start(bf16[6,4,48,128]{3,2,1,0:T(8,128)(2,1)S(1)} %get-tuple-element.53), channel_id=1, source_target_pairs={{0,24},{4,28},{8,16},{12,20},{16,8},{20,12},{24,0},{28,4},{1,25},{... | collective-permute-start | bytes 884744 | tf_op jit(solution)/shard_map/ppermute | solution.py:208
  36.0 9.5 %collective-permute-start.2 = (bf16[4,4,48,128]{3,2,1,0:T(8,128)(2,1)S(1)}, bf16[4,4,48,128]{3,2,1,0:T(8,128)(2,1)S(1)}, u32[]{:S(2)}, u32[]{:S(2)}) collective-permute-start(bf16[4,4,48,128]{3,2,1,0:T(8,128)(2,1)S(1)} %get-tuple-element.39.refs_0_), channel_id=1, source_target_pairs={{0,1},{1,0},{2,3},{3,2},{4,5},{5,4},{6,7},{7,6},{8,9},{9,8},{10,11... | collective-permute-start | bytes 589832 | tf_op jit(solution)/shard_map/ppermute | solution.py:208
  40.7 10.0 %collective-permute-start.16 = (bf16[6,4,48,128]{3,2,1,0:T(8,128)(2,1)S(1)}, bf16[6,4,48,128]{3,2,1,0:T(8,128)(2,1)S(1)}, u32[]{:S(2)}, u32[]{:S(2)}) collective-permute-start(bf16[6,4,48,128]{3,2,1,0:T(8,128)(2,1)S(1)} %get-tuple-element.55), channel_id=1, source_target_pairs={{0,8},{4,12},{8,0},{12,4},{16,24},{20,28},{24,16},{28,20},{1,9},{5... | collective-permute-start | bytes 884744 | tf_op jit(solution)/shard_map/ppermute | solution.py:208
  42.2 12.1 %collective-permute-start.17 = (bf16[6,4,48,128]{3,2,1,0:T(8,128)(2,1)S(1)}, bf16[6,4,48,128]{3,2,1,0:T(8,128)(2,1)S(1)}, u32[]{:S(2)}, u32[]{:S(2)}) collective-permute-start(bf16[6,4,48,128]{3,2,1,0:T(8,128)(2,1)S(1)} %get-tuple-element.56), channel_id=1, source_target_pairs={{0,16},{4,20},{8,24},{12,28},{16,0},{20,4},{24,8},{28,12},{1,17},{... | collective-permute-start | bytes 884744 | tf_op jit(solution)/shard_map/ppermute | solution.py:208
  42.8 11.5 %collective-permute-start.18 = (bf16[6,4,48,128]{3,2,1,0:T(8,128)(2,1)S(1)}, bf16[6,4,48,128]{3,2,1,0:T(8,128)(2,1)S(1)}, u32[]{:S(2)}, u32[]{:S(2)}) collective-permute-start(bf16[6,4,48,128]{3,2,1,0:T(8,128)(2,1)S(1)} %get-tuple-element.57), channel_id=1, source_target_pairs={{0,24},{4,28},{8,16},{12,20},{16,8},{20,12},{24,0},{28,4},{1,25},{... | collective-permute-start | bytes 884744 | tf_op jit(solution)/shard_map/ppermute | solution.py:208
  44.2 5.7 %collective-permute-start.4 = (bf16[4,4,48,128]{3,2,1,0:T(8,128)(2,1)S(1)}, bf16[4,4,48,128]{3,2,1,0:T(8,128)(2,1)S(1)}, u32[]{:S(2)}, u32[]{:S(2)}) collective-permute-start(bf16[4,4,48,128]{3,2,1,0:T(8,128)(2,1)S(1)} %collective-permute-done.3.refs_2_), channel_id=1, source_target_pairs={{0,1},{1,0},{2,3},{3,2},{4,5},{5,4},{6,7},{7,6},{8,9},{9,8},{10,11... | collective-permute-start | bytes 589832 | tf_op jit(solution)/shard_map/ppermute | solution.py:208
  45.5 13.0 %copy-start.4 = (f32[8,3]{0,1:T(4,128)S(1)}, f32[8,3]{0,1:T(4,128)}, u32[]{:S(2)}) copy-start(f32[8,3]{0,1:T(4,128)} %param.7) | copy-start | bytes 292
  45.5 13.0 %collective-permute-start.15 = (bf16[4,4,4,48,128]{4,3,2,1,0:T(8,128)(2,1)S(1)}, bf16[4,4,4,48,128]{4,3,2,1,0:T(8,128)(2,1)S(1)}, u32[]{:S(2)}, u32[]{:S(2)}) collective-permute-start(bf16[4,4,4,48,128]{4,3,2,1,0:T(8,128)(2,1)S(1)} %shard_map.68), channel_id=1, source_target_pairs={{0,4},{4,0},{8,12},{12,8},{16,20},{20,16},{24,28},{28,24},{1,5},{5... | collective-permute-start | bytes 2359304 | tf_op jit(solution)/shard_map/ppermute | solution.py:208
  54.9 7.6 %collective-permute-start.19 = (bf16[4,4,4,48,128]{4,3,2,1,0:T(8,128)(2,1)S(1)}, bf16[4,4,4,48,128]{4,3,2,1,0:T(8,128)(2,1)S(1)}, u32[]{:S(2)}, u32[]{:S(2)}) collective-permute-start(bf16[4,4,4,48,128]{4,3,2,1,0:T(8,128)(2,1)S(1)} %shard_map.70), channel_id=1, source_target_pairs={{0,4},{4,0},{8,12},{12,8},{16,20},{20,16},{24,28},{28,24},{1,5},{5... | collective-permute-start | bytes 2359304 | tf_op jit(solution)/shard_map/ppermute | solution.py:208
  55.0 11.4 %collective-permute-start.5 = (bf16[6,4,48,128]{3,2,1,0:T(8,128)(2,1)S(1)}, bf16[6,4,48,128]{3,2,1,0:T(8,128)(2,1)S(1)}, u32[]{:S(2)}, u32[]{:S(2)}) collective-permute-start(bf16[6,4,48,128]{3,2,1,0:T(8,128)(2,1)S(1)} %get-tuple-element.41), channel_id=1, source_target_pairs={{0,8},{4,12},{8,0},{12,4},{16,24},{20,28},{24,16},{28,20},{1,9},{5... | collective-permute-start | bytes 884744 | tf_op jit(solution)/shard_map/ppermute | solution.py:208
  55.7 10.8 %collective-permute-start.6 = (bf16[6,4,48,128]{3,2,1,0:T(8,128)(2,1)S(1)}, bf16[6,4,48,128]{3,2,1,0:T(8,128)(2,1)S(1)}, u32[]{:S(2)}, u32[]{:S(2)}) collective-permute-start(bf16[6,4,48,128]{3,2,1,0:T(8,128)(2,1)S(1)} %get-tuple-element.42), channel_id=1, source_target_pairs={{0,16},{4,20},{8,24},{12,28},{16,0},{20,4},{24,8},{28,12},{1,17},{... | collective-permute-start | bytes 884744 | tf_op jit(solution)/shard_map/ppermute | solution.py:208
  56.5 14.7 %collective-permute-start.7 = (bf16[6,4,48,128]{3,2,1,0:T(8,128)(2,1)S(1)}, bf16[6,4,48,128]{3,2,1,0:T(8,128)(2,1)S(1)}, u32[]{:S(2)}, u32[]{:S(2)}) collective-permute-start(bf16[6,4,48,128]{3,2,1,0:T(8,128)(2,1)S(1)} %get-tuple-element.43), channel_id=1, source_target_pairs={{0,24},{4,28},{8,16},{12,20},{16,8},{20,12},{24,0},{28,4},{1,25},{... | collective-permute-start | bytes 884744 | tf_op jit(solution)/shard_map/ppermute | solution.py:208
  58.5 13.2 %collective-permute-start.20 = (bf16[6,4,48,128]{3,2,1,0:T(8,128)(2,1)S(1)}, bf16[6,4,48,128]{3,2,1,0:T(8,128)(2,1)S(1)}, u32[]{:S(2)}, u32[]{:S(2)}) collective-permute-start(bf16[6,4,48,128]{3,2,1,0:T(8,128)(2,1)S(1)} %get-tuple-element.40.refs_0_), channel_id=1, source_target_pairs={{0,4},{4,0},{8,12},{12,8},{16,20},{20,16},{24,28},{28,24},{1,5},{5... | collective-permute-start | bytes 884744 | tf_op jit(solution)/shard_map/ppermute | solution.py:208
  71.2 1.6 %collective-permute-start.21 = (bf16[6,4,48,128]{3,2,1,0:T(8,128)(2,1)S(1)}, bf16[6,4,48,128]{3,2,1,0:T(8,128)(2,1)S(1)}, u32[]{:S(2)}, u32[]{:S(2)}) collective-permute-start(bf16[6,4,48,128]{3,2,1,0:T(8,128)(2,1)S(1)} %collective-permute-done.5.refs_1_), channel_id=1, source_target_pairs={{0,4},{4,0},{8,12},{12,8},{16,20},{20,16},{24,28},{28,24},{1,5},{5... | collective-permute-start | bytes 884744 | tf_op jit(solution)/shard_map/ppermute | solution.py:208
  71.2 2.0 %collective-permute-start.22 = (bf16[6,4,48,128]{3,2,1,0:T(8,128)(2,1)S(1)}, bf16[6,4,48,128]{3,2,1,0:T(8,128)(2,1)S(1)}, u32[]{:S(2)}, u32[]{:S(2)}) collective-permute-start(bf16[6,4,48,128]{3,2,1,0:T(8,128)(2,1)S(1)} %collective-permute-done.6.refs_2_), channel_id=1, source_target_pairs={{0,4},{4,0},{8,12},{12,8},{16,20},{20,16},{24,28},{28,24},{1,5},{5... | collective-permute-start | bytes 884744 | tf_op jit(solution)/shard_map/ppermute | solution.py:208
  71.7 1.9 %collective-permute-start.23 = (bf16[6,4,48,128]{3,2,1,0:T(8,128)(2,1)S(1)}, bf16[6,4,48,128]{3,2,1,0:T(8,128)(2,1)S(1)}, u32[]{:S(2)}, u32[]{:S(2)}) collective-permute-start(bf16[6,4,48,128]{3,2,1,0:T(8,128)(2,1)S(1)} %collective-permute-done.7.refs_3_), channel_id=1, source_target_pairs={{0,4},{4,0},{8,12},{12,8},{16,20},{20,16},{24,28},{28,24},{1,5},{5... | collective-permute-start | bytes 884744 | tf_op jit(solution)/shard_map/ppermute | solution.py:208
